TPU v7x, 128 devices: a whole 4x4x4 slice. The times are simulated.
128 devices in a mesh: vdp: 32 (over y, z, core), seq: 4 (over x).
Axes of the slice: x: 4, y: 4, z: 4, core: 2. Of those that a mesh axis runs over, the one named last changes fastest.
Arguments:
- pre_act: bfloat16 [8192, 5120], P(('vdp', 'seq')), may hold values from -6 to 6
- proj_weight: bfloat16 [5120, 8192], P('vdp', 'seq'), may hold values from -0.078125 to 0.078125
- proj_bias: bfloat16 [8192], P('seq'), may hold values from -3 to 3
- frame_tokens: int32 [32, 32], replicated, may hold values from 6 to 8, as said below
- frame_sample: int32 [32, 32], replicated, may hold values from 0 to 31, as said below
- clip_offset: int32 [32, 32], replicated, may hold values from 0 to 506, as said below
- embed_grad: bfloat16 [16384, 8192], P(('vdp', 'seq')), may hold values from -6 to 6
Outputs:
- image_embeds: bfloat16 [16384, 8192], P(('vdp', 'seq'))
- pre_grad: bfloat16 [8192, 5120], P(('vdp', 'seq'))
Inputs may be any that keep to these rules, and one draw needn't show every extreme that they name: `frame_tokens`: in every draw at least one vision group has all its frames at 8 merged tokens; the frames of other groups hold 6 to 8. `frame_sample`: each vision group sends exactly 1 of its frames to each sequence. The frames of group g with frame_sample equal to t, in frame order, occupy positions clip_offset[g, t] onward of sequence t; within a sequence these runs don't intersect and end by position 512. In every draw a run of 8 tokens begins at the first position of its sequence.
All inputs are finite; a program needn't handle non-finite values.
Results may differ from a plain program's by a relative error of at most 0.015.
Values may be sent and summed in bfloat16 or wider, within the bound.
No kernel may reach another device: no remote copies, remote signals or barrier semaphores. Data moves between devices by JAX's collectives and lax.ppermute only.
A program may use at most 128 MiB of HBM per device.

v0:
```python
import jax
import jax.numpy as jnp
from jax import lax
from jax.sharding import PartitionSpec as P

MAXTOK = 8


def gelu_exact(values):
    return 0.5 * values * (1.0 + jax.scipy.special.erf(values * 0.7071067811865476))


def gelu_slope(values):
    normal_cdf = 0.5 * (1.0 + jax.scipy.special.erf(values * 0.7071067811865476))
    return normal_cdf + values * jnp.exp(-0.5 * values * values) * 0.3989422804014327


def row_layout(frame_tokens, frame_sample, clip_offset, total_rows):
    frames = frame_tokens.shape[1]
    frame_ends = jnp.cumsum(frame_tokens, axis=1)
    frame_starts = frame_ends - frame_tokens
    frame_ids = jnp.arange(frames, dtype=jnp.int32)
    same_clip = frame_sample[:, :, None] == frame_sample[:, None, :]
    earlier = frame_ids[None, :] < frame_ids[:, None]
    preceding = jnp.sum(jnp.where(same_clip & earlier[None], frame_tokens[:, None, :], 0), axis=2)
    frame_position = jnp.take_along_axis(clip_offset, frame_sample, axis=1) + preceding
    row_ids = jnp.arange(total_rows, dtype=jnp.int32)
    frame_of_row = (
        jnp.sum((row_ids[None, :, None] >= frame_starts[:, None, :]).astype(jnp.int32), axis=2) - 1
    )
    is_live = row_ids[None, :] < frame_ends[:, -1:]
    frame_safe = jnp.clip(frame_of_row, 0, frames - 1)
    row_start = jnp.take_along_axis(frame_starts, frame_safe, axis=1)
    samples = jnp.take_along_axis(frame_sample, frame_safe, axis=1)
    positions = (
        jnp.take_along_axis(frame_position, frame_safe, axis=1) + row_ids[None, :] - row_start
    )
    clip_starts = jnp.take_along_axis(clip_offset, samples, axis=1)
    return (samples, positions, clip_starts, is_live)


def select_rows(index, count, table):
    selector = (index[:, None] == jnp.arange(count, dtype=jnp.int32)[None, :]).astype(jnp.bfloat16)
    return jnp.dot(selector, table, preferred_element_type=jnp.float32).astype(jnp.bfloat16)


def place_rows(index, count, values):
    selector = (jnp.arange(count, dtype=jnp.int32)[:, None] == index[None, :]).astype(jnp.bfloat16)
    return jnp.dot(selector, values, preferred_element_type=jnp.float32).astype(jnp.bfloat16)


def local(pre_act, proj_weight, proj_bias, frame_tokens, frame_sample, clip_offset, embed_grad):
    group_count = lax.axis_size("vdp")
    part_count = lax.axis_size("seq")
    own_group = lax.axis_index("vdp")
    own_rows = pre_act.shape[0]
    total_rows = own_rows * part_count
    span_len = embed_grad.shape[0]
    seq_len = span_len * part_count
    capacity = MAXTOK * (frame_tokens.shape[1] // group_count)
    samples, positions, clip_starts, is_live = row_layout(
        frame_tokens, frame_sample, clip_offset, total_rows
    )
    row_sample = lax.dynamic_index_in_dim(samples, own_group, 0, keepdims=False)
    row_position = lax.dynamic_index_in_dim(positions, own_group, 0, keepdims=False)
    row_clip = lax.dynamic_index_in_dim(clip_starts, own_group, 0, keepdims=False)
    row_live = lax.dynamic_index_in_dim(is_live, own_group, 0, keepdims=False)
    group_ids = jnp.arange(group_count, dtype=jnp.int32)
    matches = frame_sample[:, :, None] == group_ids[None, None, :]
    clip_lengths = jnp.sum(jnp.where(matches, frame_tokens[:, :, None], 0), axis=1)
    offsets_here = lax.dynamic_index_in_dim(clip_offset, own_group, 1, keepdims=False)
    lengths_here = lax.dynamic_index_in_dim(clip_lengths, own_group, 1, keepdims=False)
    slot_ids = jnp.arange(capacity, dtype=jnp.int32)
    bias_row = proj_bias.astype(jnp.float32)
    activated = gelu_exact(
        lax.all_gather(pre_act, "seq", axis=0, tiled=True).astype(jnp.float32)
    ).astype(jnp.bfloat16)
    weight_full = lax.all_gather(proj_weight, "vdp", axis=0, tiled=True)
    product = jnp.dot(activated, weight_full, preferred_element_type=jnp.float32)
    projected = (product + bias_row).astype(jnp.bfloat16)
    slot_total = group_count * capacity
    slot_key = jnp.where(row_live, row_sample * capacity + row_position - row_clip, slot_total)
    outgoing = place_rows(slot_key, slot_total, projected)
    incoming = lax.all_to_all(outgoing, "vdp", split_axis=0, concat_axis=0, tiled=True)
    spots = jnp.arange(seq_len, dtype=jnp.int32)
    inside = (spots[:, None] >= offsets_here[None, :]) & (
        spots[:, None] < (offsets_here + lengths_here)[None, :]
    )
    source = jnp.sum(jnp.where(inside, group_ids[None, :], 0), axis=1)
    covered = jnp.any(inside, axis=1)
    take_rows = jnp.where(
        covered,
        source * capacity + jnp.clip(spots - offsets_here[source], 0, capacity - 1),
        slot_total,
    )
    seq_line = select_rows(take_rows, slot_total, incoming)
    image_embeds = lax.all_to_all(seq_line, "seq", split_axis=0, concat_axis=1, tiled=True)
    columns = lax.all_to_all(embed_grad, "seq", split_axis=1, concat_axis=0, tiled=True)
    valid_slot = slot_ids[None, :] < lengths_here[:, None]
    wanted = jnp.where(valid_slot, offsets_here[:, None] + slot_ids[None, :], seq_len)
    send_box = select_rows(wanted.reshape(slot_total), seq_len, columns)
    returned = lax.all_to_all(send_box, "vdp", split_axis=0, concat_axis=0, tiled=True)
    row_grad = select_rows(slot_key, slot_total, returned)
    summed = lax.psum_scatter(
        lax.dot_general(
            row_grad, weight_full, (((1,), (1,)), ((), ())), preferred_element_type=jnp.float32
        ).astype(jnp.bfloat16),
        "seq",
        scatter_dimension=0,
        tiled=True,
    ).astype(jnp.float32)
    pre_grad = (summed * gelu_slope(pre_act.astype(jnp.float32))).astype(jnp.bfloat16)
    return (image_embeds, pre_grad)


def solution(mesh):
    in_specs = (
        P(("vdp", "seq"), None),
        P("vdp", "seq"),
        P("seq"),
        P(),
        P(),
        P(),
        P(("vdp", "seq"), None),
    )
    out_specs = (P(("vdp", "seq"), None), P(("vdp", "seq"), None))
    return jax.shard_map(local, mesh=mesh, in_specs=in_specs, out_specs=out_specs, check_vma=False)
```

profile of v0, /device:TPU:6, one launch (start us, length us, event | category | flops | bytes accessed | tf_op | source)
XLA Modules:
  0.0 350.5 jit_solution(14771528827474985820)
XLA Ops:
  7.2 0.7 all-gather.5.cloned.1.call-update
  7.9 4.1 %copy.18 = bf16[128,8192]{0,1:T(8,128)(2,1)} copy(bf16[128,8192]{1,0:T(8,128)(2,1)} %param.15) | data formatting | bytes 4194304 | tf_op args[6]
  12.0 4.8 %all-to-all-start.2 = ((bf16[128,4,2048]{0,2,1:T(8,128)(2,1)}), bf16[128,4,2048]{0,2,1:T(8,128)(2,1)S(1)}, u32[]{:S(2)}, u32[]{:S(2)}) async-start(bf16[128,4,2048]{0,2,1:T(8,128)(2,1)} %bitcast.83), calls=%async_computation.2 | async-start | bytes 4194304 | tf_op jit(solution)/shard_map/all_to_all | solution.py:98
  16.8 0.7 all-gather.3.cloned.1.call-update
  18.0 52.9 %gather_fusion.3 = s32[8192]{0:T(1024)S(1)} fusion(s32[32,32]{1,0:T(8,128)S(1)} %sub.27, s32[8192]{0:T(1024)S(1)} %bitcast.78), kind=kCustom, calls=%fused_computation.2.clone | custom fusion | bytes 131072 | tf_op jit(solution)/shard_map/jit(take_along_axis)/gather | solution.py:33
  71.0 52.9 %gather_fusion.1 = s32[8192]{0:T(1024)S(1)} fusion(s32[32,32]{1,0:T(8,128)S(1)} %copy-done.1, s32[8192]{0:T(1024)S(1)} %bitcast.79), kind=kCustom, calls=%fused_computation.clone | custom fusion | bytes 131072 | tf_op jit(solution)/shard_map/jit(take_along_axis)/gather | solution.py:34
  124.6 0.9 select_reduce_fusion.1
  125.9 2.6 copy.19
  128.5 3.3 fusion.12
  131.9 8.3 %all-to-all-start.3 = ((bf16[32,8,2048]{2,1,0:T(8,128)(2,1)}), bf16[32,8,2048]{2,1,0:T(8,128)(2,1)S(1)}, u32[]{:S(2)}, u32[]{:S(2)}) async-start(bf16[32,8,2048]{2,1,0:T(8,128)(2,1)} %fusion.12), calls=%async_computation.3 | async-start | bytes 2097152 | tf_op jit(solution)/shard_map/all_to_all | solution.py:102
  140.5 7.1 %gather_fusion = s32[1024]{0:T(1024)S(1)} fusion(s32[32,32]{1,0:T(8,128)S(1)} %copy-done, s32[1024]{0:T(1024)S(1)} %reshape.211), kind=kCustom, calls=%fused_computation.4 | custom fusion | bytes 16384 | tf_op jit(solution)/shard_map/jit(take_along_axis)/gather | solution.py:26
  147.7 52.9 %gather_fusion.2 = s32[8192]{0:T(1024)S(1)} fusion(s32[32,32]{1,0:T(8,128)S(1)} %select_add_fusion, s32[8192]{0:T(1024)S(1)} %bitcast.80), kind=kCustom, calls=%fused_computation.1.clone | custom fusion | bytes 131072 | tf_op jit(solution)/shard_map/jit(take_along_axis)/gather | solution.py:36
  200.7 52.9 %gather_fusion.4 = s32[8192]{0:T(1024)S(1)} fusion(s32[32,32]{1,0:T(8,128)S(1)} %copy-done, s32[8192]{0:T(1024)S(1)} %bitcast.81), kind=kCustom, calls=%fused_computation.3.clone | custom fusion | bytes 131072 | tf_op jit(solution)/shard_map/jit(take_along_axis)/gather | solution.py:38
  254.3 11.5 %convolution_convert_fusion = bf16[256,5120]{1,0:T(8,128)(2,1)} fusion(bf16[5120,2048]{1,0:T(8,128)(2,1)} %all-gather.5.cloned.1.call-done, bf16[32,8,2048]{2,1,0:T(8,128)(2,1)S(1)} %all-to-all-done.3, s32[256]{0:T(256)S(1)} %bitcast.90), kind=kOutput, calls=%fused_computation.7 | convolution fusion | flops 5639045120 | bytes 24642560 | tf_op jit(solution)/shard_map/dot_general | solution.py:105
  265.9 14.6 %fusion.11 = bf16[32,8,2048]{2,1,0:T(8,128)(2,1)} fusion(s32[256]{0:T(256)S(1)} %bitcast.91, bf16[5120,2048]{1,0:T(8,128)(2,1)} %all-gather.5.cloned.1.call-done, bf16[256,5120]{1,0:T(8,128)(2,1)} %all-gather.3.cloned.1.call-done, f32[2048]{0:T(1024)S(1)} %convert_element_type.46), kind=kOutput, calls=%fused_computation.21 | convolution fusion | flops 5646647296 | bytes 24650752 | tf_op jit(solution)/shard_map/dot_general | solution.py:49
  280.5 7.4 %all-to-all-start = ((bf16[32,8,2048]{2,1,0:T(8,128)(2,1)}), bf16[32,8,2048]{2,1,0:T(8,128)(2,1)S(1)}, u32[]{:S(2)}, u32[]{:S(2)}) async-start(bf16[32,8,2048]{2,1,0:T(8,128)(2,1)} %fusion.11), calls=%async_computation | async-start | bytes 2097152 | tf_op jit(solution)/shard_map/all_to_all | solution.py:84
  287.9 0.7 fusion.52
  288.6 0.8 fusion.51
  289.6 4.2 %compare_select_fusion.4 = (s32[512,1]{0,1:T(1,128)S(1)}, s32[512,1]{0,1:T(1,128)S(1)}) fusion(s32[]{:T(128)} %bitcast.26, s32[]{:T(128)} %bitcast.27, s32[]{:T(128)} %bitcast.28, s32[]{:T(128)} %bitcast.29, s32[]{:T(128)} %bitcast.30, s32[]{:T(128)} %bitcast.32, s32[]{:T(128)} %bitcast.31, s32[512,1]{0,1:T(1,128)S(1)} %bitcast.88), kind=kLoop, calls=%fused_computation.99 | loop fusion | flops 7680 | bytes 6172 | tf_op jit(solution)/shard_map/gather | solution.py:93
  294.0 15.8 %fusion.37 = s32[512]{0:T(512)S(1)} fusion(pred[512]{0:T(512)(128)(4,1)S(1)} %fusion.30, pred[512]{0:T(512)(128)(4,1)S(1)} %get-tuple-element.29, pred[512]{0:T(512)(128)(4,1)S(1)} %get-tuple-element.28, pred[512]{0:T(512)(128)(4,1)S(1)} %get-tuple-element.27, pred[512]{0:T(512)(128)(4,1)S(1)} %get-tuple-element.26, ...), kind=kLoop, calls=%fused_computation.117 | loop fusion | flops 15360 | bytes 19556 | tf_op jit(solution)/shard_map/jit(_where)/select_n | solution.py:91
  309.8 0.7 convolution_convert_fusion.1
  310.6 29.4 %all_to_all.62 = bf16[4,128,2048]{2,1,0:T(8,128)(2,1)S(1)} all-to-all(bf16[4,128,2048]{2,1,0:T(8,128)(2,1)S(1)} %bitcast.85), channel_id=1, replica_groups=mesh['vdp'=32,'seq'=4] {'seq'}, dimensions={0} | all-to-all | bytes 4194304 | tf_op jit(solution)/shard_map/all_to_all | solution.py:97
  340.0 1.5 copy.20
  341.5 2.5 fusion.20
  (48 shorter events, 3.3 us)
Async XLA Ops:
  7.2 247.1 %all-gather.5.cloned.1.call-start = ((), (), s32[]{:S(2)}) async-start(), calls=%async_computation.6 | async-start | bytes 21626880 | tf_op jit(solution)/shard_map/all_gather | solution.py:78
  7.9 9.6 %copy-start.3 = (s32[32,32]{1,0:T(8,128)S(1)}, s32[32,32]{1,0:T(8,128)}, u32[]{:S(2)}) copy-start(s32[32,32]{1,0:T(8,128)} %param.12) | copy-start | bytes 12292
  12.0 114.0 %all-to-all-start.2 = ((bf16[128,4,2048]{0,2,1:T(8,128)(2,1)}), bf16[128,4,2048]{0,2,1:T(8,128)(2,1)S(1)}, u32[]{:S(2)}, u32[]{:S(2)}) async-start(bf16[128,4,2048]{0,2,1:T(8,128)(2,1)} %bitcast.83), calls=%async_computation.2 | async-start | bytes 4194304 | tf_op jit(solution)/shard_map/all_to_all | solution.py:98
  16.7 249.1 %all-gather.3.cloned.1.call-start = ((), (), s32[]{:S(2)}) async-start(), calls=%async_computation.5 | async-start | bytes 3276800 | tf_op jit(solution)/shard_map/all_gather | solution.py:76
  18.0 52.9 %copy-start.1 = (s32[32,32]{1,0:T(8,128)S(1)}, s32[32,32]{1,0:T(8,128)}, u32[]{:S(2)}) copy-start(s32[32,32]{1,0:T(8,128)} %param.13) | copy-start | bytes 12292
  70.9 54.6 %copy-start = (s32[32,32]{1,0:T(8,128)S(1)}, s32[32,32]{1,0:T(8,128)}, u32[]{:S(2)}) copy-start(s32[32,32]{1,0:T(8,128)} %param.14) | copy-start | bytes 12292
  131.9 122.4 %all-to-all-start.3 = ((bf16[32,8,2048]{2,1,0:T(8,128)(2,1)}), bf16[32,8,2048]{2,1,0:T(8,128)(2,1)S(1)}, u32[]{:S(2)}, u32[]{:S(2)}) async-start(bf16[32,8,2048]{2,1,0:T(8,128)(2,1)} %fusion.12), calls=%async_computation.3 | async-start | bytes 2097152 | tf_op jit(solution)/shard_map/all_to_all | solution.py:102
  140.2 201.3 %reduce-scatter.2.cloned.1.call-start = ((), (), s32[]{:S(2)}) async-start(), calls=%async_computation.7 | async-start | bytes 3276800 | tf_op jit(solution)/shard_map/reduce_scatter | solution.py:104
  254.3 11.5 %copy-start.4 = (bf16[2048]{0:T(1024)(128)(2,1)S(1)}, bf16[2048]{0:T(1024)(128)(2,1)}, u32[]{:S(2)}) copy-start(bf16[2048]{0:T(1024)(128)(2,1)} %param.11) | copy-start | bytes 12292
  280.5 29.3 %all-to-all-start = ((bf16[32,8,2048]{2,1,0:T(8,128)(2,1)}), bf16[32,8,2048]{2,1,0:T(8,128)(2,1)S(1)}, u32[]{:S(2)}, u32[]{:S(2)}) async-start(bf16[32,8,2048]{2,1,0:T(8,128)(2,1)} %fusion.11), calls=%async_computation | async-start | bytes 2097152 | tf_op jit(solution)/shard_map/all_to_all | solution.py:84
  310.6 30.9 %copy-start.2 = (bf16[64,5120]{1,0:T(8,128)(2,1)S(1)}, bf16[64,5120]{1,0:T(8,128)(2,1)}, u32[]{:S(2)}) copy-start(bf16[64,5120]{1,0:T(8,128)(2,1)} %param.9) | copy-start | bytes 1966084
Sparse Core Ops, SparseCore 0:
  10.3 84.7 all-gather.4
  96.7 32.6 all-gather.2
  266.0 33.4 reduce-scatter.1
where the time goes:
time: 353 us; the launch traced here: 351 us
  local copies, waits for them, and re-layouts  230 us (65%)
  matrix products  30.2 us (9%)
  blocking collectives  29.4 us (8%)
  other arithmetic  25.1 us (7%)
  starting transfers between devices  20.7 us (6%)
  between operations  14.1 us (4%)
    gather x2, local copies, waits for them, and re-layouts, row_layout(): clip_starts = jnp.take_along_axis(clip_offset, samples, axis=1)  52.9 us
    gather x2, local copies, waits for them, and re-layouts, row_layout(): samples = jnp.take_along_axis(frame_sample, frame_safe, axis=1)  52.9 us
    gather x2, local copies, waits for them, and re-layouts, row_layout(): jnp.take_along_axis(frame_position, frame_safe, axis=1) + row_ids[None, :]  52.9 us
    gather x2, local copies, waits for them, and re-layouts, row_layout(): row_start = jnp.take_along_axis(frame_starts, frame_safe, axis=1)  52.9 us
    all_to_all x1, blocking collectives, local(): lax.all_to_all(seq_line, 'seq', split_axis=0, concat_axis=1, tiled=True)  29.4 us
    select_n x1, other arithmetic, local(): jnp.where(covered, source * capacity + jnp.clip(spots - offsets_here[sour...  15.8 us
    dot_general x1, matrix products, place_rows(): jnp.dot(selector, values, preferred_element_type=jnp.float32)  14.6 us
    dot_general x1, matrix products, local(): lax.dot_general(row_grad, weight_full, (((1,), (1,)), ((), ())), preferre...  11.5 us
  transfers between devices with their start and end apart: 6, of which 0 were waited for; matrix products, arithmetic and copies ran while one was open for 81% of the time, Pallas kernels for 0%

commit v1 on v0

v1 whole, which is shorter than its diff:
```python
import jax
import jax.numpy as jnp
from jax import lax
from jax.sharding import PartitionSpec as P

MAXTOK = 8
CHUNKS = 2


def normal_cdf(values):
    return 0.5 * (1.0 + jax.scipy.special.erf(values * 0.7071067811865476))


def one_hot(condition):
    return condition.astype(jnp.bfloat16)


def pick(selector, table):
    return jnp.dot(selector, table, preferred_element_type=jnp.float32).astype(jnp.bfloat16)


def pick_t(selector, table):
    return lax.dot_general(
        selector, table, (((0,), (0,)), ((), ())), preferred_element_type=jnp.float32
    ).astype(jnp.bfloat16)


def slot_of_rows(frame_tokens, frame_sample, own_group, total_rows, slot_total):
    frames = frame_tokens.shape[1]
    tokens = lax.dynamic_slice_in_dim(frame_tokens, own_group, 1, 0)
    sample = lax.dynamic_slice_in_dim(frame_sample, own_group, 1, 0)
    frame_ids = jnp.arange(frames, dtype=jnp.int32)
    before = frame_ids[None, :] < frame_ids[:, None]
    starts = jnp.sum(jnp.where(before, tokens, 0), axis=1)[None, :]
    slots = lax.broadcasted_iota(jnp.int32, (slot_total, frames), 0)
    hit = sample == slots // MAXTOK
    step = (slots % MAXTOK)[:, :1]
    start = jnp.sum(jnp.where(hit, starts, 0), axis=1, keepdims=True)
    length = jnp.sum(jnp.where(hit, tokens, 0), axis=1, keepdims=True)
    row = jnp.where(step < length, start + step, -1)
    return one_hot(row == lax.broadcasted_iota(jnp.int32, (slot_total, total_rows), 1))


def spot_of_slots(frame_tokens, frame_sample, clip_offset, own_seq, seq_len, slot_total):
    groups = frame_tokens.shape[0]
    length = jnp.sum(jnp.where(frame_sample == own_seq, frame_tokens, 0), axis=1)[None, :]
    seq_ids = jnp.arange(clip_offset.shape[1], dtype=jnp.int32)
    offset = jnp.sum(jnp.where(seq_ids[None, :] == own_seq, clip_offset, 0), axis=1)[None, :]
    slots = lax.broadcasted_iota(jnp.int32, (slot_total, groups), 0)
    owner = slots // MAXTOK == lax.broadcasted_iota(jnp.int32, (slot_total, groups), 1)
    step = (slots % MAXTOK)[:, 0]
    slot_length = jnp.sum(jnp.where(owner, length, 0), axis=1)
    slot_offset = jnp.sum(jnp.where(owner, offset, 0), axis=1)
    spot = jnp.where(step < slot_length, slot_offset + step, -1)
    return one_hot(lax.broadcasted_iota(jnp.int32, (seq_len, slot_total), 0) == spot[None, :])


def local(pre_act, proj_weight, proj_bias, frame_tokens, frame_sample, clip_offset, embed_grad):
    groups = lax.axis_size("vdp")
    parts = lax.axis_size("seq")
    own = lax.axis_index("vdp")
    own_rows, hidden = pre_act.shape
    total_rows = own_rows * parts
    span = embed_grad.shape[0]
    seq_len = span * parts
    slab = proj_weight.shape[1]
    slot_total = groups * MAXTOK
    width = slab // CHUNKS

    weights = [
        lax.all_gather(proj_weight[:, q * width : (q + 1) * width], "vdp", axis=0, tiled=True)
        for q in range(CHUNKS)
    ]
    grads = embed_grad.reshape(span, parts, slab).transpose(1, 0, 2)
    columns = lax.all_to_all(grads, "seq", split_axis=0, concat_axis=0, tiled=True)

    rows = pre_act.astype(jnp.float32)
    cdf = normal_cdf(rows)
    activated = (rows * cdf).astype(jnp.bfloat16)
    everyone = lax.all_to_all(
        jnp.broadcast_to(activated[None], (parts, own_rows, hidden)),
        "seq",
        split_axis=0,
        concat_axis=0,
        tiled=True,
    ).reshape(total_rows, hidden)

    by_slot = slot_of_rows(frame_tokens, frame_sample, own, total_rows, slot_total)
    by_spot = spot_of_slots(frame_tokens, frame_sample, clip_offset, own, seq_len, slot_total)

    send_box = pick_t(by_spot, columns.reshape(seq_len, slab)).reshape(groups, MAXTOK, slab)
    returned = lax.all_to_all(send_box, "vdp", split_axis=0, concat_axis=0, tiled=True)
    row_grad = pick_t(by_slot, returned.reshape(slot_total, slab))
    act_slots = pick(by_slot, everyone)

    partial = jnp.zeros((total_rows, hidden), jnp.float32)
    pieces = []
    for q in range(CHUNKS):
        cols = slice(q * width, (q + 1) * width)
        product = jnp.dot(act_slots, weights[q], preferred_element_type=jnp.float32)
        projected = (product + proj_bias[cols].astype(jnp.float32)).astype(jnp.bfloat16)
        incoming = lax.all_to_all(
            projected.reshape(groups, MAXTOK, width), "vdp", split_axis=0, concat_axis=0, tiled=True
        )
        line = pick(by_spot, incoming.reshape(slot_total, width)).reshape(parts, span, width)
        pieces.append(lax.all_to_all(line, "seq", split_axis=0, concat_axis=0, tiled=True))
        partial = partial + lax.dot_general(
            row_grad[:, cols],
            weights[q],
            (((1,), (1,)), ((), ())),
            preferred_element_type=jnp.float32,
        )
    image_embeds = jnp.stack(pieces, axis=2).transpose(1, 0, 2, 3).reshape(span, parts * slab)
    summed = lax.psum_scatter(
        partial.astype(jnp.bfloat16), "seq", scatter_dimension=0, tiled=True
    ).astype(jnp.float32)
    slope = cdf + rows * jnp.exp(-0.5 * rows * rows) * 0.3989422804014327
    pre_grad = (summed * slope).astype(jnp.bfloat16)
    return (image_embeds, pre_grad)


def solution(mesh):
    in_specs = (
        P(("vdp", "seq"), None),
        P("vdp", "seq"),
        P("seq"),
        P(),
        P(),
        P(),
        P(("vdp", "seq"), None),
    )
    out_specs = (P(("vdp", "seq"), None), P(("vdp", "seq"), None))
    return jax.shard_map(local, mesh=mesh, in_specs=in_specs, out_specs=out_specs, check_vma=False)
```

time: 353 us -> 324 us (0.918)
  local copies, waits for them, and re-layouts: 230 us -> 17 us
  waiting for transfers between devices: 1.47 us -> 161 us
  other arithmetic: 25.1 us -> 3.17 us
  blocking collectives: 29.4 us -> 50.1 us
  matrix products: 30.2 us -> 47.3 us
  starting transfers between devices: 20.7 us -> 28.7 us
    gather x13 -> x0, local copies, waits for them, and re-layouts: 220 us -> none  [the longest x2 52.9 us: row_layout(): clip_starts = jnp.take_along_axis(clip_offset, samples, axis=1)]
    all_to_all x3 -> x5, waiting for transfers between devices: 0.01 us -> 80.2 us  [the longest x1 30.2 us: local(): lax.all_to_all(jnp.broadcast_to(activated[None], (parts, own_rows, hidden...]
    all_gather x2, waiting for transfers between devices: 0.04 us -> 48.2 us  [local(): lax.all_gather(proj_weight[:, q * width:(q + 1) * width], 'vdp', axis=0,...]
    reduce_scatter x1, waiting for transfers between devices: 0.01 us -> 31.7 us  [local(): lax.psum_scatter(partial.astype(jnp.bfloat16), 'seq', scatter_dimension=0...]
    all_to_all x1 -> x2, blocking collectives: 29.4 us -> 50.1 us  [the longest x1 32.3 us: local(): lax.all_to_all(send_box, 'vdp', split_axis=0, concat_axis=0, tiled=True)]
    dot_general x4 -> x9, matrix products: 30.2 us -> 47.3 us  [the longest x2 25.6 us: local(): lax.dot_general(row_grad[:, cols], weights[q], (((1,), (1,)), ((), ())),...]
    select_n x4 -> x2, other arithmetic: 16.5 us -> 0.01 us  [the longest x1 0.01 us: slot_of_rows(): row = jnp.where(step < length, start + step, -1)]
    all_to_all x3 -> x5, starting transfers between devices: 20.5 us -> 28.6 us  [the longest x2 12 us: local(): lax.all_to_all(projected.reshape(groups, MAXTOK, width), 'vdp', split_axi...]
  transfers between devices with their start and end apart: 6 -> 8, of which waited for: 0 -> 8; matrix products, arithmetic and copies ran while one was open for 81% -> 10% of each run, Pallas kernels for 0% -> 0%
where the time goes in v1:
time: 324 us; the launch traced here: 321 us
  waiting for transfers between devices  161 us (50%)
  blocking collectives  50.1 us (15%)
  matrix products  47.3 us (15%)
  starting transfers between devices  28.7 us (9%)
  local copies, waits for them, and re-layouts  17 us (5%)
  between operations  13.9 us (4%)
    all_gather x2, waiting for transfers between devices, local(): lax.all_gather(proj_weight[:, q * width:(q + 1) * width], 'vdp', axis=0,...  48.2 us
    all_to_all x1, blocking collectives, local(): lax.all_to_all(send_box, 'vdp', split_axis=0, concat_axis=0, tiled=True)  32.3 us
    reduce_scatter x1, waiting for transfers between devices, local(): lax.psum_scatter(partial.astype(jnp.bfloat16), 'seq', scatter_dimension=0...  31.7 us
    all_to_all x1, waiting for transfers between devices, local(): lax.all_to_all(jnp.broadcast_to(activated[None], (parts, own_rows, hidden...  30.2 us
    dot_general x2, matrix products, local(): lax.dot_general(row_grad[:, cols], weights[q], (((1,), (1,)), ((), ())),...  25.6 us
    all_to_all x1, waiting for transfers between devices, local(): lax.all_to_all(grads, 'seq', split_axis=0, concat_axis=0, tiled=True)  23.8 us
    all_to_all x1, blocking collectives, local(): lax.all_to_all(line, 'seq', split_axis=0, concat_axis=0, tiled=True)  17.8 us
    dot_general x2, matrix products, local(): product = jnp.dot(act_slots, weights[q], preferred_element_type=jnp.float32)  16.1 us
  transfers between devices with their start and end apart: 8, of which 8 were waited for; matrix products, arithmetic and copies ran while one was open for 10% of the time, Pallas kernels for 0%

profile of v1, /device:TPU:6, one launch (start us, length us, event | category | flops | bytes accessed | tf_op | source)
XLA Modules:
  0.0 321.0 jit_solution(2081118518114580966)
XLA Ops:
  9.9 4.1 %copy.15 = bf16[128,8192]{0,1:T(8,128)(2,1)} copy(bf16[128,8192]{1,0:T(8,128)(2,1)} %param.13) | data formatting | bytes 4194304 | tf_op args[6]
  14.0 4.9 %all-to-all-start.5 = ((bf16[4,128,2048]{1,2,0:T(8,128)(2,1)}), bf16[4,128,2048]{1,2,0:T(8,128)(2,1)S(1)}, u32[]{:S(2)}, u32[]{:S(2)}) async-start(bf16[4,128,2048]{1,2,0:T(8,128)(2,1)} %bitcast.43), calls=%async_computation.5 | async-start | bytes 4194304 | tf_op jit(solution)/shard_map/all_to_all | solution.py:75
  19.4 23.8 %all-to-all-done.5 = bf16[4,128,2048]{1,2,0:T(8,128)(2,1)S(1)} async-done(((bf16[4,128,2048]{1,2,0:T(8,128)(2,1)}), bf16[4,128,2048]{1,2,0:T(8,128)(2,1)S(1)}, u32[]{:S(2)}, u32[]{:S(2)}) %all-to-all-start.5) | async-done | bytes 2097184 | tf_op jit(solution)/shard_map/all_to_all | solution.py:75
  43.2 2.6 copy.16
  45.8 2.3 fusion.1
  48.1 32.3 %all_to_all.35 = bf16[32,8,2048]{2,1,0:T(8,128)(2,1)S(1)} all-to-all(bf16[32,8,2048]{2,1,0:T(8,128)(2,1)S(1)} %fusion.1), channel_id=1, replica_groups=mesh['vdp'=32,'seq'=4] {'vdp'}, dimensions={0} | all-to-all | bytes 2097152 | tf_op jit(solution)/shard_map/all_to_all | solution.py:92
  81.6 12.6 %fusion.17 = f32[256,5120]{1,0:T(8,128)} fusion(bf16[5120,1024]{1,0:T(8,128)(2,1)} %all-gather.3.cloned.1.call-done, bf16[256,2048]{1,0:T(8,128)(2,1)S(1)} %convolution_convert_fusion.2), kind=kOutput, calls=%fused_computation.31 | convolution fusion | flops 2684354560 | bytes 16252928 | tf_op jit(solution)/shard_map/dot_general | solution.py:107
  94.2 47.6 %all-gather.5.cloned.1.call-done = bf16[5120,1024]{1,0:T(8,128)(2,1)} async-done(((bf16[160,1024]{1,0:T(8,128)(2,1)}), bf16[5120,1024]{1,0:T(8,128)(2,1)}) %all-gather.5.cloned.1.call-update) | async-done | bytes 10485776 | tf_op jit(solution)/shard_map/all_gather | solution.py:71
  141.8 13.0 %fusion = bf16[256,5120]{1,0:T(8,128)(2,1)} fusion(f32[256,5120]{1,0:T(8,128)} %fusion.17, bf16[5120,1024]{1,0:T(8,128)(2,1)} %all-gather.5.cloned.1.call-done, bf16[256,2048]{1,0:T(8,128)(2,1)S(1)} %convolution_convert_fusion.2), kind=kOutput, calls=%fused_computation.1 | convolution fusion | flops 2686976000 | bytes 18874368 | tf_op jit(solution)/shard_map/dot_general | solution.py:107
  154.8 31.7 %reduce-scatter.2.cloned.1.call-done = bf16[64,5120]{1,0:T(8,128)(2,1)} async-done(((bf16[256,5120]{1,0:T(8,128)(2,1)}), bf16[64,5120]{1,0:T(8,128)(2,1)}) %reduce-scatter.2.cloned.1.call-update) | async-done | bytes 655376 | tf_op jit(solution)/shard_map/reduce_scatter | solution.py:114
  186.5 2.6 fusion.10
  191.0 6.2 %all-to-all-start = ((bf16[4,64,5120]{2,1,0:T(8,128)(2,1)}), bf16[4,64,5120]{2,1,0:T(8,128)(2,1)S(1)}, u32[]{:S(2)}, u32[]{:S(2)}) async-start(bf16[4,64,5120]{2,1,0:T(8,128)(2,1)} %broadcast_in_dim.92), calls=%async_computation | async-start | bytes 5242880 | tf_op jit(solution)/shard_map/all_to_all | solution.py:80
  197.1 30.2 %all-to-all-done = bf16[4,64,5120]{2,1,0:T(8,128)(2,1)S(1)} async-done(((bf16[4,64,5120]{2,1,0:T(8,128)(2,1)}), bf16[4,64,5120]{2,1,0:T(8,128)(2,1)S(1)}, u32[]{:S(2)}, u32[]{:S(2)}) %all-to-all-start) | async-done | bytes 2621472 | tf_op jit(solution)/shard_map/all_to_all | solution.py:80
  229.7 7.6 %fusion.14 = bf16[32,8,1024]{2,1,0:T(8,128)(2,1)} fusion(bf16[256,5120]{1,0:T(8,128)(2,1)S(1)} %convolution_convert_fusion, bf16[5120,1024]{1,0:T(8,128)(2,1)} %all-gather.3.cloned.1.call-done, f32[1024]{0:T(1024)S(1)} %get-tuple-element.12), kind=kOutput, calls=%fused_computation.28 | convolution fusion | flops 2684878848 | bytes 13635584 | tf_op jit(solution)/shard_map/dot_general | solution.py:100
  237.4 7.3 %all-to-all-start.1 = ((bf16[32,8,1024]{2,1,0:T(8,128)(2,1)}), bf16[32,8,1024]{2,1,0:T(8,128)(2,1)S(1)}, u32[]{:S(2)}, u32[]{:S(2)}) async-start(bf16[32,8,1024]{2,1,0:T(8,128)(2,1)} %fusion.14), calls=%async_computation.1 | async-start | bytes 1048576 | tf_op jit(solution)/shard_map/all_to_all | solution.py:102
  244.7 8.5 %fusion.13 = bf16[32,8,1024]{2,1,0:T(8,128)(2,1)} fusion(bf16[256,5120]{1,0:T(8,128)(2,1)} %copy-done, bf16[5120,1024]{1,0:T(8,128)(2,1)} %all-gather.5.cloned.1.call-done, f32[1024]{0:T(1024)S(1)} %get-tuple-element.13), kind=kOutput, calls=%fused_computation.27 | convolution fusion | flops 2684878848 | bytes 13635584 | tf_op jit(solution)/shard_map/dot_general | solution.py:100
  253.1 2.7 all-to-all-done.1
  255.9 4.7 %all-to-all-start.3 = ((bf16[32,8,1024]{2,1,0:T(8,128)(2,1)}), bf16[32,8,1024]{2,1,0:T(8,128)(2,1)S(1)}, u32[]{:S(2)}, u32[]{:S(2)}) async-start(bf16[32,8,1024]{2,1,0:T(8,128)(2,1)} %fusion.13), calls=%async_computation.3 | async-start | bytes 1048576 | tf_op jit(solution)/shard_map/all_to_all | solution.py:102
  262.0 9.8 %all-to-all-done.3 = bf16[32,8,1024]{2,1,0:T(8,128)(2,1)S(1)} async-done(((bf16[32,8,1024]{2,1,0:T(8,128)(2,1)}), bf16[32,8,1024]{2,1,0:T(8,128)(2,1)S(1)}, u32[]{:S(2)}, u32[]{:S(2)}) %all-to-all-start.3) | async-done | bytes 524320 | tf_op jit(solution)/shard_map/all_to_all | solution.py:102
  271.7 5.6 %all-to-all-start.2 = ((bf16[4,128,1024]{2,1,0:T(8,128)(2,1)}), bf16[4,128,1024]{2,1,0:T(8,128)(2,1)S(1)}, u32[]{:S(2)}, u32[]{:S(2)}) async-start(bf16[4,128,1024]{2,1,0:T(8,128)(2,1)} %bitcast.9), calls=%async_computation.2 | async-start | bytes 2097152 | tf_op jit(solution)/shard_map/all_to_all | solution.py:106
  277.7 13.7 %all-to-all-done.2 = bf16[4,128,1024]{2,1,0:T(8,128)(2,1)S(1)} async-done(((bf16[4,128,1024]{2,1,0:T(8,128)(2,1)}), bf16[4,128,1024]{2,1,0:T(8,128)(2,1)S(1)}, u32[]{:S(2)}, u32[]{:S(2)}) %all-to-all-start.2) | async-done | bytes 1048608 | tf_op jit(solution)/shard_map/all_to_all | solution.py:106
  291.5 17.8 %all_to_all.36 = bf16[4,128,1024]{2,1,0:T(8,128)(2,1)S(1)} all-to-all(bf16[4,128,1024]{2,1,0:T(8,128)(2,1)S(1)} %bitcast.45), channel_id=1, replica_groups=mesh['vdp'=32,'seq'=4] {'seq'}, dimensions={0} | all-to-all | bytes 2097152 | tf_op jit(solution)/shard_map/all_to_all | solution.py:106
  309.5 2.2 copy.14
  311.6 2.8 reshape.72
  (38 shorter events, 10.6 us)
Async XLA Ops:
  7.2 74.5 %all-gather.3.cloned.1.call-start = ((), (), s32[]{:S(2)}) async-start(), calls=%async_computation.8 | async-start | bytes 10813440 | tf_op jit(solution)/shard_map/all_gather | solution.py:71
  9.2 132.6 %all-gather.5.cloned.1.call-start = ((), (), s32[]{:S(2)}) async-start(), calls=%async_computation.9 | async-start | bytes 10813440 | tf_op jit(solution)/shard_map/all_gather | solution.py:71
  14.0 5.0 %copy-start.2 = (s32[32,32]{1,0:T(8,128)S(1)}, s32[32,32]{1,0:T(8,128)}, u32[]{:S(2)}) copy-start(s32[32,32]{1,0:T(8,128)} %param.10) | copy-start | bytes 12292
  14.0 5.0 %copy-start.3 = (s32[32,32]{1,0:T(8,128)S(1)}, s32[32,32]{1,0:T(8,128)}, u32[]{:S(2)}) copy-start(s32[32,32]{1,0:T(8,128)} %param.11) | copy-start | bytes 12292
  14.0 5.1 %copy-start.4 = (s32[32,32]{1,0:T(8,128)S(1)}, s32[32,32]{1,0:T(8,128)}, u32[]{:S(2)}) copy-start(s32[32,32]{1,0:T(8,128)} %param.12) | copy-start | bytes 12292
  14.0 29.2 %all-to-all-start.5 = ((bf16[4,128,2048]{1,2,0:T(8,128)(2,1)}), bf16[4,128,2048]{1,2,0:T(8,128)(2,1)S(1)}, u32[]{:S(2)}, u32[]{:S(2)}) async-start(bf16[4,128,2048]{1,2,0:T(8,128)(2,1)} %bitcast.43), calls=%async_computation.5 | async-start | bytes 4194304 | tf_op jit(solution)/shard_map/all_to_all | solution.py:75
  18.9 167.6 %reduce-scatter.2.cloned.1.call-start = ((), (), s32[]{:S(2)}) async-start(), calls=%async_computation.10 | async-start | bytes 3276800 | tf_op jit(solution)/shard_map/reduce_scatter | solution.py:114
  154.8 31.7 %copy-start.1 = (bf16[64,5120]{1,0:T(8,128)(2,1)S(1)}, bf16[64,5120]{1,0:T(8,128)(2,1)}, u32[]{:S(2)}) copy-start(bf16[64,5120]{1,0:T(8,128)(2,1)} %param.7) | copy-start | bytes 1966084
  191.0 6.2 %copy-start.5 = (bf16[2048]{0:T(1024)(128)(2,1)S(1)}, bf16[2048]{0:T(1024)(128)(2,1)}, u32[]{:S(2)}) copy-start(bf16[2048]{0:T(1024)(128)(2,1)} %param.9) | copy-start | bytes 12292
  191.0 36.3 %all-to-all-start = ((bf16[4,64,5120]{2,1,0:T(8,128)(2,1)}), bf16[4,64,5120]{2,1,0:T(8,128)(2,1)S(1)}, u32[]{:S(2)}, u32[]{:S(2)}) async-start(bf16[4,64,5120]{2,1,0:T(8,128)(2,1)} %broadcast_in_dim.92), calls=%async_computation | async-start | bytes 5242880 | tf_op jit(solution)/shard_map/all_to_all | solution.py:80
  228.2 1.5 copy-start
  237.4 18.5 %all-to-all-start.1 = ((bf16[32,8,1024]{2,1,0:T(8,128)(2,1)}), bf16[32,8,1024]{2,1,0:T(8,128)(2,1)S(1)}, u32[]{:S(2)}, u32[]{:S(2)}) async-start(bf16[32,8,1024]{2,1,0:T(8,128)(2,1)} %fusion.14), calls=%async_computation.1 | async-start | bytes 1048576 | tf_op jit(solution)/shard_map/all_to_all | solution.py:102
  255.9 15.9 %all-to-all-start.3 = ((bf16[32,8,1024]{2,1,0:T(8,128)(2,1)}), bf16[32,8,1024]{2,1,0:T(8,128)(2,1)S(1)}, u32[]{:S(2)}, u32[]{:S(2)}) async-start(bf16[32,8,1024]{2,1,0:T(8,128)(2,1)} %fusion.13), calls=%async_computation.3 | async-start | bytes 1048576 | tf_op jit(solution)/shard_map/all_to_all | solution.py:102
  271.7 19.7 %all-to-all-start.2 = ((bf16[4,128,1024]{2,1,0:T(8,128)(2,1)}), bf16[4,128,1024]{2,1,0:T(8,128)(2,1)S(1)}, u32[]{:S(2)}, u32[]{:S(2)}) async-start(bf16[4,128,1024]{2,1,0:T(8,128)(2,1)} %bitcast.9), calls=%async_computation.2 | async-start | bytes 2097152 | tf_op jit(solution)/shard_map/all_to_all | solution.py:106
Sparse Core Ops, SparseCore 0:
  10.8 70.7 all-gather.2
  83.9 57.8 all-gather.4
  154.9 31.5 reduce-scatter.1

commit v2 on v1

v2 whole, which is shorter than its diff:
```python
import jax
import jax.numpy as jnp
from jax import lax
from jax.sharding import Mesh, PartitionSpec as P

MAXTOK = 8
Y, Z, CORE, X = "y", "z", "core", "seq"
VDP = (Y, Z, CORE)
ALL = (Y, Z, CORE, X)


def normal_cdf(values):
    return 0.5 * (1.0 + jax.scipy.special.erf(values * 0.7071067811865476))


def pick(selector, table):
    return jnp.dot(selector, table, preferred_element_type=jnp.float32).astype(jnp.bfloat16)


def shift(value, axis, by):
    size = lax.axis_size(axis)
    return lax.ppermute(value, axis, [(i, (i + by) % size) for i in range(size)])


def tie(*values):
    return lax.optimization_barrier(values)


def rows_of_slots(frame_tokens, frame_sample, group, slots):
    tokens = lax.dynamic_slice_in_dim(frame_tokens, group, 1, 0)
    sample = lax.dynamic_slice_in_dim(frame_sample, group, 1, 0)
    frame_ids = jnp.arange(frame_tokens.shape[1], dtype=jnp.int32)
    before = frame_ids[None, :] < frame_ids[:, None]
    starts = jnp.sum(jnp.where(before, tokens, 0), axis=1)[None, :]
    hit = sample == slots // MAXTOK
    step = slots[:, 0] % MAXTOK
    start = jnp.sum(jnp.where(hit, starts, 0), axis=1)
    length = jnp.sum(jnp.where(hit, tokens, 0), axis=1)
    return jnp.where(step < length, start + step, -1)


def spots_of_slots(frame_tokens, frame_sample, clip_offset, own_seq, group_of_slot, step):
    length = jnp.sum(jnp.where(frame_sample == own_seq, frame_tokens, 0), axis=1)[None, :]
    seq_ids = jnp.arange(clip_offset.shape[1], dtype=jnp.int32)
    offset = jnp.sum(jnp.where(seq_ids[None, :] == own_seq, clip_offset, 0), axis=1)[None, :]
    group_ids = jnp.arange(frame_tokens.shape[0], dtype=jnp.int32)
    owner = group_of_slot[:, None] == group_ids[None, :]
    slot_length = jnp.sum(jnp.where(owner, length, 0), axis=1)
    slot_offset = jnp.sum(jnp.where(owner, offset, 0), axis=1)
    return jnp.where(step < slot_length, slot_offset + step, -1)


def hot(index, count):
    return (index[:, None] == jnp.arange(count, dtype=jnp.int32)[None, :]).astype(jnp.bfloat16)


def hot_t(index, count):
    return (jnp.arange(count, dtype=jnp.int32)[:, None] == index[None, :]).astype(jnp.bfloat16)


def local(pre_act, proj_weight, proj_bias, frame_tokens, frame_sample, clip_offset, embed_grad):
    ny, nz, nc, nx = (lax.axis_size(a) for a in ALL)
    iy, iz, ic, ix = (lax.axis_index(a) for a in ALL)
    chip = iy * nz + iz
    own = chip * nc + ic
    sibling = chip * nc + 1 - ic
    groups = ny * nz * nc
    own_rows, hidden = pre_act.shape
    total_rows = own_rows * nx
    span = embed_grad.shape[0]
    seq_len = span * nx
    krows, slab = proj_weight.shape
    half = slab // nc
    slot_total = groups * MAXTOK

    kept = lax.dynamic_slice_in_dim(proj_weight, ic * half, half, 1)
    given = lax.dynamic_slice_in_dim(proj_weight, (1 - ic) * half, half, 1)
    taken = shift(given, CORE, 1)

    rows = pre_act.astype(jnp.float32)
    cdf = normal_cdf(rows)
    activated = (rows * cdf).astype(jnp.bfloat16)
    activated, taken = tie(activated, taken)
    act_right = shift(activated, X, 1)
    act_left = shift(activated, X, -1)

    grads = embed_grad.reshape(span, nx, slab).transpose(1, 0, 2)
    columns = lax.all_to_all(grads, X, split_axis=0, concat_axis=0, tiled=True)
    columns = columns.reshape(seq_len, slab)

    first = jnp.where(ic == 0, kept, taken)
    second = jnp.where(ic == 0, taken, kept)

    weight = jnp.zeros((ny, nz, 2, krows, half), jnp.bfloat16)

    def put(weight, piece, y, z, which):
        zero = jnp.int32(0)
        return lax.dynamic_update_slice(
            weight, piece, (y % ny, z % nz, jnp.int32(which), zero, zero)
        )

    za = [first] + [shift(first, Z, d) for d in (1, -1, 2)]
    yb = [second] + [shift(second, Y, d) for d in (1, -1, 2)]
    line_z = jnp.zeros((nz, krows, half), jnp.bfloat16)
    line_y = jnp.zeros((ny, krows, half), jnp.bfloat16)
    for piece, d in zip(za, (0, 1, -1, 2)):
        line_z = lax.dynamic_update_slice(line_z, piece[None], ((iz - d) % nz, 0, 0))
    for piece, d in zip(yb, (0, 1, -1, 2)):
        line_y = lax.dynamic_update_slice(line_y, piece[None], ((iy - d) % ny, 0, 0))

    act_opp = jnp.concatenate(
        [
            shift(act_right[: own_rows // 2], X, 1),
            shift(act_left[own_rows // 2 :], X, -1),
        ]
    )
    everyone = jnp.zeros((nx, own_rows, hidden), jnp.bfloat16)
    for piece, d in ((activated, 0), (act_right, 1), (act_left, -1), (act_opp, 2)):
        everyone = lax.dynamic_update_slice(everyone, piece[None], ((ix - d) % nx, 0, 0))
    everyone = everyone.reshape(total_rows, hidden)

    zy = [shift(line_z, Y, d) for d in (1, -1)]
    yz = [shift(line_y, Z, d) for d in (1, -1)]

    step = jnp.arange(slot_total, dtype=jnp.int32) % MAXTOK
    pair = jnp.arange(slot_total, dtype=jnp.int32) // (nc * MAXTOK)
    member = jnp.arange(slot_total, dtype=jnp.int32) // MAXTOK % nc
    spot_of = [
        spots_of_slots(
            frame_tokens, frame_sample, clip_offset, own, pair * nc + (member if c == 0 else 1 - member), step
        )
        for c in range(nc)
    ]
    n_slots = nc * slot_total
    ids = lax.broadcasted_iota(jnp.int32, (n_slots, groups), 0)
    slots = ids // (nc * MAXTOK) * MAXTOK + ids % MAXTOK
    from_own = ids[:, 0] // MAXTOK % nc == 0
    row_own = rows_of_slots(frame_tokens, frame_sample, own, slots)
    row_sib = rows_of_slots(frame_tokens, frame_sample, sibling, slots)
    row_of = jnp.where(from_own, row_own, jnp.where(row_sib >= 0, row_sib + total_rows, -1))

    send_box = jnp.stack(
        [
            pick(hot(spot_of[c], seq_len), columns[:, c * half : (c + 1) * half]).reshape(
                ny * nz, nc * MAXTOK, half
            )
            for c in range(nc)
        ],
        axis=1,
    ).reshape(groups, nc * MAXTOK, half)
    returned = lax.all_to_all(send_box, VDP, split_axis=0, concat_axis=0, tiled=True)
    row_grad = pick(hot_t(row_of, nc * total_rows), returned.reshape(n_slots, half))

    other = shift(everyone, CORE, 1)
    act_slots = pick(hot(row_of, nc * total_rows), jnp.concatenate([everyone, other]))

    z_far = [shift(zy[0][: nz // 2], Y, 1), shift(zy[1][nz // 2 :], Y, -1)]
    y_far = [shift(yz[0][: ny // 2], Z, 1), shift(yz[1][ny // 2 :], Z, -1)]
    zero = jnp.int32(0)
    weight = put(weight, line_z[None, :, None], iy, zero, 0)
    weight = put(weight, zy[0][None, :, None], iy - 1, zero, 0)
    weight = put(weight, zy[1][None, :, None], iy + 1, zero, 0)
    weight = put(weight, z_far[0][None, :, None], iy + 2, zero, 0)
    weight = put(weight, z_far[1][None, :, None], iy + 2, zero + nz // 2, 0)
    weight = put(weight, line_y[:, None, None], zero, iz, 1)
    weight = put(weight, yz[0][:, None, None], zero, iz - 1, 1)
    weight = put(weight, yz[1][:, None, None], zero, iz + 1, 1)
    weight = put(weight, y_far[0][:, None, None], zero, iz + 2, 1)
    weight = put(weight, y_far[1][:, None, None], zero + ny // 2, iz + 2, 1)
    weight = weight.reshape(hidden, half)

    bias = lax.dynamic_slice_in_dim(proj_bias, ic * half, half, 0).astype(jnp.float32)
    product = jnp.dot(act_slots, weight, preferred_element_type=jnp.float32)
    projected = (product + bias).astype(jnp.bfloat16)
    incoming = lax.all_to_all(
        projected.reshape(groups, nc * MAXTOK, half), VDP, split_axis=0, concat_axis=0, tiled=True
    ).reshape(ny * nz, nc, nc * MAXTOK, half)

    def back(grad):
        return lax.dot_general(
            grad, weight, (((1,), (1,)), ((), ())), preferred_element_type=jnp.float32
        )

    away = back(row_grad[total_rows:]).astype(jnp.bfloat16)
    received = shift(away, CORE, 1)
    partial = (back(row_grad[:total_rows]) + received.astype(jnp.float32)).astype(jnp.bfloat16)
    parts = partial.reshape(nx, own_rows, hidden)

    def part(d):
        return lax.dynamic_index_in_dim(parts, (ix + d) % nx, 0, keepdims=False)

    mid = hidden // 2
    far = part(2)
    far_right = shift(far[:, :mid], X, 1)
    far_left = shift(far[:, mid:], X, -1)
    to_right, to_left = part(1), part(-1)
    to_right = jnp.concatenate(
        [(to_right[:, :mid].astype(jnp.float32) + far_right).astype(jnp.bfloat16), to_right[:, mid:]], 1
    )
    to_left = jnp.concatenate(
        [to_left[:, :mid], (to_left[:, mid:].astype(jnp.float32) + far_left).astype(jnp.bfloat16)], 1
    )
    got_right = shift(to_right, X, 1)
    got_left = shift(to_left, X, -1)
    summed = part(0).astype(jnp.float32) + got_right.astype(jnp.float32) + got_left.astype(jnp.float32)
    slope = cdf + rows * jnp.exp(-0.5 * rows * rows) * 0.3989422804014327
    pre_grad = (summed * slope).astype(jnp.bfloat16)

    line = jnp.stack(
        [
            pick(hot_t(spot_of[c], seq_len), incoming[:, c].reshape(slot_total, half)).reshape(
                nx, span, half
            )
            for c in range(nc)
        ],
        axis=2,
    ).reshape(nx, span, slab)
    placed = lax.all_to_all(line, X, split_axis=0, concat_axis=0, tiled=True)
    image_embeds = placed.transpose(1, 0, 2).reshape(span, nx * slab)
    return (image_embeds, pre_grad)


def solution(mesh):
    fine = Mesh(mesh.devices.reshape(4, 4, 2, 4), ALL)
    in_specs = (P(ALL, None), P(VDP, X), P(X), P(), P(), P(), P(ALL, None))
    out_specs = (P(ALL, None), P(ALL, None))
    return jax.shard_map(local, mesh=fine, in_specs=in_specs, out_specs=out_specs, check_vma=False)
```

time: 324 us -> 225 us (0.69)
  waiting for transfers between devices: 161 us -> 47.6 us
  blocking collectives: 50.1 us -> 0 us
  local copies, waits for them, and re-layouts: 17 us -> 55.4 us
  starting transfers between devices: 28.7 us -> 61.5 us
  between operations: 13.9 us -> 1.32 us
  other arithmetic: 3.17 us -> 14.6 us
  matrix products: 47.3 us -> 43.7 us
    all_to_all x5 -> x4, waiting for transfers between devices: 80.2 us -> 19.4 us  [the longest x1 17.8 us: local(): placed = lax.all_to_all(line, X, split_axis=0, concat_axis=0, tiled=True)]
    all_to_all x2 -> x0, blocking collectives: 50.1 us -> none  [the longest x1 32.3 us: local(): lax.all_to_all(send_box, 'vdp', split_axis=0, concat_axis=0, tiled=True)]
    all_gather x2 -> x0, waiting for transfers between devices: 48.2 us -> none  [local(): lax.all_gather(proj_weight[:, q * width:(q + 1) * width], 'vdp', axis=0,...]
    ppermute x0 -> x25, starting transfers between devices: none -> 36.6 us  [shift(): lax.ppermute(value, axis, [(i, (i + by) % size) for i in range(size)])]
    reduce_scatter x1 -> x0, waiting for transfers between devices: 31.7 us -> none  [local(): lax.psum_scatter(partial.astype(jnp.bfloat16), 'seq', scatter_dimension=0...]
    ppermute x0 -> x25, waiting for transfers between devices: none -> 28.2 us  [shift(): lax.ppermute(value, axis, [(i, (i + by) % size) for i in range(size)])]
    dynamic_update_slice x0 -> x19, local copies, waits for them, and re-layouts: none -> 23 us  [the longest x10 20.5 us: put(): lax.dynamic_update_slice(weight, piece, (y % ny, z % nz, jnp.int32(which)...]
    slice x1 -> x10, local copies, waits for them, and re-layouts: 1.95 us -> 10.5 us  [the longest x2 4.01 us: local(): z_far = [shift(zy[0][:nz // 2], Y, 1), shift(zy[1][nz // 2:], Y, -1)]]
  transfers between devices with their start and end apart: 8 -> 29, of which waited for: 8 -> 13; matrix products, arithmetic and copies ran while one was open for 10% -> 48% of each run, Pallas kernels for 0% -> 0%
where the time goes in v2:
time: 225 us; the launch traced here: 224 us
  starting transfers between devices  61.5 us (27%)
  local copies, waits for them, and re-layouts  55.4 us (25%)
  waiting for transfers between devices  47.6 us (21%)
  matrix products  43.7 us (19%)
  other arithmetic  14.6 us (6%)
    ppermute x25, starting transfers between devices, shift(): lax.ppermute(value, axis, [(i, (i + by) % size) for i in range(size)])  36.6 us
    ppermute x25, waiting for transfers between devices, shift(): lax.ppermute(value, axis, [(i, (i + by) % size) for i in range(size)])  28.2 us
    dot_general x2, matrix products, back(): lax.dot_general(grad, weight, (((1,), (1,)), ((), ())), preferred_element...  23.9 us
    dynamic_update_slice x10, local copies, waits for them, and re-layouts, put(): lax.dynamic_update_slice(weight, piece, (y % ny, z % nz, jnp.int32(which)...  20.5 us
    all_to_all x1, waiting for transfers between devices, local(): placed = lax.all_to_all(line, X, split_axis=0, concat_axis=0, tiled=True)  17.8 us
    dot_general x1, matrix products, local(): product = jnp.dot(act_slots, weight, preferred_element_type=jnp.float32)  14.8 us
    unnamed x26, local copies, waits for them, and re-layouts  8.97 us
    all_to_all x1, starting transfers between devices, local(): lax.all_to_all(send_box, VDP, split_axis=0, concat_axis=0, tiled=True)  7.13 us
  transfers between devices with their start and end apart: 29, of which 13 were waited for; matrix products, arithmetic and copies ran while one was open for 48% of the time, Pallas kernels for 0%

profile of v2, /device:TPU:6, one launch (start us, length us, event | category | flops | bytes accessed | tf_op | source)
XLA Modules:
  0.0 224.1 jit_solution(3291358037099418389)
XLA Ops:
  2.4 4.1 %copy.55 = bf16[128,8192]{0,1:T(8,128)(2,1)} copy(bf16[128,8192]{1,0:T(8,128)(2,1)} %param.13) | data formatting | bytes 4194304 | tf_op args[6]
  6.4 4.9 %all-to-all-start.2 = ((bf16[4,128,2048]{1,2,0:T(8,128)(2,1)}), bf16[4,128,2048]{1,2,0:T(8,128)(2,1)S(1)}, u32[]{:S(2)}, u32[]{:S(2)}) async-start(bf16[4,128,2048]{1,2,0:T(8,128)(2,1)} %bitcast.118), calls=%async_computation.2 | async-start | bytes 4194304 | tf_op jit(solution)/shard_map/all_to_all | solution.py:88
  28.3 3.2 %collective-permute-start.15 = (bf16[160,1024]{1,0:T(8,128)(2,1)S(1)}, bf16[160,1024]{1,0:T(8,128)(2,1)S(1)}, u32[]{:S(2)}, u32[]{:S(2)}) collective-permute-start(bf16[160,1024]{1,0:T(8,128)(2,1)S(1)} %get-tuple-element.23), channel_id=1, source_target_pairs={{0,64},{32,96},{64,0},{96,32},{1,65},{33,97},{65,1},{97,33},{2,66}... | collective-permute-start | bytes 983048 | tf_op jit(solution)/shard_map/ppermute | solution.py:22
  32.2 2.8 %collective-permute-done.7 = bf16[160,1024]{1,0:T(8,128)(2,1)S(1)} collective-permute-done((bf16[160,1024]{1,0:T(8,128)(2,1)S(1)}, bf16[160,1024]{1,0:T(8,128)(2,1)S(1)}, u32[]{:S(2)}, u32[]{:S(2)}) %collective-permute-start.7) | collective-permute-done | bytes 327712 | tf_op jit(solution)/shard_map/ppermute | solution.py:22
  40.6 3.7 %collective-permute-start.10 = (bf16[4,160,1024]{2,1,0:T(8,128)(2,1)}, bf16[4,160,1024]{2,1,0:T(8,128)(2,1)}, u32[]{:S(2)}, u32[]{:S(2)}) collective-permute-start(bf16[4,160,1024]{2,1,0:T(8,128)(2,1)} %bitcast_dynamic-update-slice_fusion.17), channel_id=1, source_target_pairs={{0,96},{32,0},{64,32},{96,64},{1,97},{33,1},{65,33},{97,65},{2,98}... | collective-permute-start | bytes 3932168 | tf_op jit(solution)/shard_map/ppermute | solution.py:22
  45.8 5.4 %broadcast_in_dim.219 = bf16[4,4,2,160,1024]{4,3,2,1,0:T(8,128)(2,1)} broadcast(bf16[]{:T(256)} %constant.311.clone.1), dimensions={} | broadcast | bytes 10485762 | tf_op jit(solution)/shard_map/broadcast_in_dim | solution.py:94
  60.0 2.6 %copy.56 = bf16[4,128,2048]{2,1,0:T(8,128)(2,1)} copy(bf16[4,128,2048]{1,2,0:T(8,128)(2,1)S(1)} %all-to-all-done.2) | data formatting | bytes 4194304 | tf_op jit(solution)/shard_map/all_to_all | solution.py:88
  68.8 7.1 %all-to-all-start.3 = ((bf16[32,16,1024]{2,1,0:T(8,128)(2,1)}), bf16[32,16,1024]{2,1,0:T(8,128)(2,1)S(1)}, u32[]{:S(2)}, u32[]{:S(2)}) async-start(bf16[32,16,1024]{2,1,0:T(8,128)(2,1)} %bitcast.59), calls=%async_computation.3 | async-start | bytes 2097152 | tf_op jit(solution)/shard_map/all_to_all | solution.py:151
  89.0 5.9 %collective-permute-done.17 = bf16[4,160,1024]{2,1,0:T(8,128)(2,1)} collective-permute-done((bf16[4,160,1024]{2,1,0:T(8,128)(2,1)S(1)}, bf16[4,160,1024]{2,1,0:T(8,128)(2,1)}, u32[]{:S(2)}, u32[]{:S(2)}) %collective-permute-start.17) | collective-permute-done | bytes 1310752 | tf_op jit(solution)/shard_map/ppermute | solution.py:22
  98.5 2.5 %bitcast_dynamic-update-slice_fusion.4 = bf16[4,4,2,160,1024]{4,3,2,1,0:T(8,128)(2,1)} fusion(bf16[4,4,2,160,1024]{4,3,2,1,0:T(8,128)(2,1)} %bitcast_dynamic-update-slice_fusion.5, s32[]{:T(128)S(6)} %select_n.548, bf16[4,160,1024]{2,1,0:T(8,128)(2,1)} %collective-permute-done.9), kind=kLoop, calls=%fused_computation.33 | loop fusion | bytes 2621444 | tf_op jit(solution)/shard_map/dynamic_update_slice | solution.py:98
  101.1 2.5 %bitcast_dynamic-update-slice_fusion.3 = bf16[4,4,2,160,1024]{4,3,2,1,0:T(8,128)(2,1)} fusion(bf16[4,4,2,160,1024]{4,3,2,1,0:T(8,128)(2,1)} %bitcast_dynamic-update-slice_fusion.4, s32[]{:T(128)S(6)} %select_n.550, bf16[4,160,1024]{2,1,0:T(8,128)(2,1)} %collective-permute-done.10), kind=kLoop, calls=%fused_computation.32 | loop fusion | bytes 2621444 | tf_op jit(solution)/shard_map/dynamic_update_slice | solution.py:98
  113.1 2.5 %bitcast_dynamic-update-slice_fusion = bf16[4,4,2,160,1024]{4,3,2,1,0:T(8,128)(2,1)} fusion(bf16[4,4,2,160,1024]{4,3,2,1,0:T(8,128)(2,1)} %bitcast_dynamic-update-slice_fusion.1, s32[]{:T(128)S(6)} %select_n.542, bf16[4,160,1024]{2,1,0:T(8,128)(2,1)} %collective-permute-done.17), kind=kLoop, calls=%fused_computation.29 | loop fusion | bytes 2621444 | tf_op jit(solution)/shard_map/dynamic_update_slice | solution.py:98
  118.5 12.3 %convolution_convert_fusion.1 = bf16[256,5120]{1,0:T(8,128)(2,1)} fusion(bf16[5120,1024]{1,0:T(8,128)(2,1)} %bitcast.41, bf16[512,1024]{1,0:T(8,128)(2,1)S(1)} %convolution_convert_fusion.2), kind=kOutput, calls=%fused_computation.3 | convolution fusion | flops 2685665280 | bytes 13631488 | tf_op jit(solution)/shard_map/dot_general | solution.py:180
  130.8 14.8 %add_convert_fusion = bf16[512,1024]{1,0:T(8,128)(2,1)} fusion(bf16[5120,1024]{1,0:T(8,128)(2,1)} %bitcast.41, bf16[256,5120]{1,0:T(8,128)(2,1)} %collective-permute-done.5, bf16[256,5120]{1,0:T(8,128)(2,1)} %bitcast.127, f32[1024]{0:T(1024)S(1)} %dynamic-slice_convert_fusion, s32[512]{0:T(512)S(1)} %bitcast.140), kind=kOutput, calls=%fused_computation.14 | convolution fusion | flops 8067481600 | bytes 16783360 | tf_op jit(solution)/shard_map/dot_general | solution.py:173
  145.6 5.9 %all-to-all-start = ((bf16[32,16,1024]{2,1,0:T(8,128)(2,1)}), bf16[32,16,1024]{2,1,0:T(8,128)(2,1)S(1)}, u32[]{:S(2)}, u32[]{:S(2)}) async-start(bf16[32,16,1024]{2,1,0:T(8,128)(2,1)} %bitcast.42), calls=%async_computation | async-start | bytes 2097152 | tf_op jit(solution)/shard_map/all_to_all | solution.py:175
  151.5 11.6 %fusion = bf16[256,5120]{1,0:T(8,128)(2,1)S(1)} fusion(bf16[5120,1024]{1,0:T(8,128)(2,1)} %bitcast.41, bf16[256,5120]{1,0:T(8,128)(2,1)} %collective-permute-done.20, bf16[512,1024]{1,0:T(8,128)(2,1)S(1)} %copy-done.11), kind=kOutput, calls=%fused_computation.2 | convolution fusion | flops 2688286720 | bytes 16252928 | tf_op jit(solution)/shard_map/dot_general | solution.py:180
  169.7 4.9 %collective-permute-done.21 = bf16[64,2560]{1,0:T(8,128)(2,1)} collective-permute-done((bf16[64,2560]{1,0:T(8,128)(2,1)S(1)}, bf16[64,2560]{1,0:T(8,128)(2,1)}, u32[]{:S(2)}, u32[]{:S(2)}) %collective-permute-start.21) | collective-permute-done | bytes 327712 | tf_op jit(solution)/shard_map/ppermute | solution.py:22
  176.5 2.9 %collective-permute-start.22 = (bf16[64,5120]{1,0:T(8,128)(2,1)}, bf16[64,5120]{1,0:T(8,128)(2,1)}, u32[]{:S(2)}, u32[]{:S(2)}) collective-permute-start(bf16[64,5120]{1,0:T(8,128)(2,1)} %pad_maximum_fusion.2), channel_id=1, source_target_pairs={{0,1},{1,2},{2,3},{3,0},{4,5},{5,6},{6,7},{7,4},{8,9},{9,10},{10,1... | collective-permute-start | bytes 1966088 | tf_op jit(solution)/shard_map/ppermute | solution.py:22
  184.4 6.9 %all-to-all-start.1 = ((bf16[4,128,2048]{1,2,0:T(8,128)(2,1)}), bf16[4,128,2048]{1,2,0:T(8,128)(2,1)S(1)}, u32[]{:S(2)}, u32[]{:S(2)}) async-start(bf16[4,128,2048]{1,2,0:T(8,128)(2,1)} %bitcast.120), calls=%async_computation.1 | async-start | bytes 4194304 | tf_op jit(solution)/shard_map/all_to_all | solution.py:218
  191.4 3.6 %collective-permute-done.22 = bf16[64,5120]{1,0:T(8,128)(2,1)} collective-permute-done((bf16[64,5120]{1,0:T(8,128)(2,1)}, bf16[64,5120]{1,0:T(8,128)(2,1)}, u32[]{:S(2)}, u32[]{:S(2)}) %collective-permute-start.22) | collective-permute-done | bytes 655392 | tf_op jit(solution)/shard_map/ppermute | solution.py:22
  195.0 5.3 %collective-permute-done.24 = bf16[64,5120]{1,0:T(8,128)(2,1)} collective-permute-done((bf16[64,5120]{1,0:T(8,128)(2,1)}, bf16[64,5120]{1,0:T(8,128)(2,1)}, u32[]{:S(2)}, u32[]{:S(2)}) %collective-permute-start.24) | collective-permute-done | bytes 655392 | tf_op jit(solution)/shard_map/ppermute | solution.py:22
  200.3 3.1 %fusion.17 = bf16[64,5120]{1,0:T(8,128)(2,1)} fusion(bf16[64,5120]{1,0:T(8,128)(2,1)S(1)} %copy-done.4, bf16[64,5120]{1,0:T(8,128)(2,1)} %collective-permute-done.24, bf16[64,5120]{1,0:T(8,128)(2,1)} %collective-permute-done.22, bf16[4,64,5120]{2,1,0:T(8,128)(2,1)} %bitcast.125, s32[]{:T(128)S(6)} %select_n.527), kind=kLoop, calls=%fused_computation.26 | loop fusion | flops 5242880 | bytes 3276804 | tf_op jit(solution)/shard_map/convert_element_type | solution.py:207
  203.4 17.8 %all-to-all-done.1 = bf16[4,128,2048]{1,2,0:T(8,128)(2,1)S(1)} async-done(((bf16[4,128,2048]{1,2,0:T(8,128)(2,1)}), bf16[4,128,2048]{1,2,0:T(8,128)(2,1)S(1)}, u32[]{:S(2)}, u32[]{:S(2)}) %all-to-all-start.1) | async-done | bytes 2097184 | tf_op jit(solution)/shard_map/all_to_all | solution.py:218
  221.2 2.9 %copy.59 = bf16[128,8192]{1,0:T(8,128)(2,1)} copy(bf16[128,8192]{0,1:T(8,128)(2,1)S(1)} %bitcast.119) | data formatting | bytes 4194304
  (137 shorter events, 83.5 us)
Async XLA Ops:
  6.4 53.5 %all-to-all-start.2 = ((bf16[4,128,2048]{1,2,0:T(8,128)(2,1)}), bf16[4,128,2048]{1,2,0:T(8,128)(2,1)S(1)}, u32[]{:S(2)}, u32[]{:S(2)}) async-start(bf16[4,128,2048]{1,2,0:T(8,128)(2,1)} %bitcast.118), calls=%async_computation.2 | async-start | bytes 4194304 | tf_op jit(solution)/shard_map/all_to_all | solution.py:88
  15.9 12.4 %collective-permute-start.6 = (bf16[160,1024]{1,0:T(8,128)(2,1)S(1)}, bf16[160,1024]{1,0:T(8,128)(2,1)S(1)}, u32[]{:S(2)}, u32[]{:S(2)}) collective-permute-start(bf16[160,1024]{1,0:T(8,128)(2,1)S(1)} %get-tuple-element.25), channel_id=1, source_target_pairs={{0,8},{8,16},{16,24},{24,0},{1,9},{9,17},{17,25},{25,1},{2,10},{10... | collective-permute-start | bytes 983048 | tf_op jit(solution)/shard_map/ppermute | solution.py:22
  17.8 17.2 %collective-permute-start.7 = (bf16[160,1024]{1,0:T(8,128)(2,1)S(1)}, bf16[160,1024]{1,0:T(8,128)(2,1)S(1)}, u32[]{:S(2)}, u32[]{:S(2)}) collective-permute-start(bf16[160,1024]{1,0:T(8,128)(2,1)S(1)} %get-tuple-element.25), channel_id=1, source_target_pairs={{0,24},{8,0},{16,8},{24,16},{1,25},{9,1},{17,9},{25,17},{2,26},{10... | collective-permute-start | bytes 983048 | tf_op jit(solution)/shard_map/ppermute | solution.py:22
  19.9 17.0 %collective-permute-start.8 = (bf16[160,1024]{1,0:T(8,128)(2,1)S(1)}, bf16[160,1024]{1,0:T(8,128)(2,1)S(1)}, u32[]{:S(2)}, u32[]{:S(2)}) collective-permute-start(bf16[160,1024]{1,0:T(8,128)(2,1)S(1)} %get-tuple-element.25), channel_id=1, source_target_pairs={{0,16},{8,24},{16,0},{24,8},{1,17},{9,25},{17,1},{25,9},{2,18},{10... | collective-permute-start | bytes 983048 | tf_op jit(solution)/shard_map/ppermute | solution.py:22
  23.2 15.4 %collective-permute-start.13 = (bf16[160,1024]{1,0:T(8,128)(2,1)S(1)}, bf16[160,1024]{1,0:T(8,128)(2,1)S(1)}, u32[]{:S(2)}, u32[]{:S(2)}) collective-permute-start(bf16[160,1024]{1,0:T(8,128)(2,1)S(1)} %get-tuple-element.23), channel_id=1, source_target_pairs={{0,32},{32,64},{64,96},{96,0},{1,33},{33,65},{65,97},{97,1},{2,34}... | collective-permute-start | bytes 983048 | tf_op jit(solution)/shard_map/ppermute | solution.py:22
  24.9 15.7 %collective-permute-start.14 = (bf16[160,1024]{1,0:T(8,128)(2,1)S(1)}, bf16[160,1024]{1,0:T(8,128)(2,1)S(1)}, u32[]{:S(2)}, u32[]{:S(2)}) collective-permute-start(bf16[160,1024]{1,0:T(8,128)(2,1)S(1)} %get-tuple-element.23), channel_id=1, source_target_pairs={{0,96},{32,0},{64,32},{96,64},{1,97},{33,1},{65,33},{97,65},{2,98}... | collective-permute-start | bytes 983048 | tf_op jit(solution)/shard_map/ppermute | solution.py:22
  28.3 16.0 %collective-permute-start.15 = (bf16[160,1024]{1,0:T(8,128)(2,1)S(1)}, bf16[160,1024]{1,0:T(8,128)(2,1)S(1)}, u32[]{:S(2)}, u32[]{:S(2)}) collective-permute-start(bf16[160,1024]{1,0:T(8,128)(2,1)S(1)} %get-tuple-element.23), channel_id=1, source_target_pairs={{0,64},{32,96},{64,0},{96,32},{1,65},{33,97},{65,1},{97,33},{2,66}... | collective-permute-start | bytes 983048 | tf_op jit(solution)/shard_map/ppermute | solution.py:22
  35.0 18.6 %collective-permute-start.1 = (bf16[64,5120]{1,0:T(8,128)(2,1)S(1)}, bf16[64,5120]{1,0:T(8,128)(2,1)S(1)}, u32[]{:S(2)}, u32[]{:S(2)}) collective-permute-start(bf16[64,5120]{1,0:T(8,128)(2,1)S(1)} %copy-done.2), channel_id=1, source_target_pairs={{0,1},{1,2},{2,3},{3,0},{4,5},{5,6},{6,7},{7,4},{8,9},{9,10},{10,1... | collective-permute-start | bytes 1966088 | tf_op jit(solution)/shard_map/ppermute | solution.py:22
  36.9 19.3 %collective-permute-start.2 = (bf16[64,5120]{1,0:T(8,128)(2,1)S(1)}, bf16[64,5120]{1,0:T(8,128)(2,1)S(1)}, u32[]{:S(2)}, u32[]{:S(2)}) collective-permute-start(bf16[64,5120]{1,0:T(8,128)(2,1)S(1)} %copy-done.2), channel_id=1, source_target_pairs={{0,3},{1,0},{2,1},{3,2},{4,7},{5,4},{6,5},{7,6},{8,11},{9,8},{10,9... | collective-permute-start | bytes 1966088 | tf_op jit(solution)/shard_map/ppermute | solution.py:22
  38.6 39.5 %collective-permute-start.9 = (bf16[4,160,1024]{2,1,0:T(8,128)(2,1)}, bf16[4,160,1024]{2,1,0:T(8,128)(2,1)}, u32[]{:S(2)}, u32[]{:S(2)}) collective-permute-start(bf16[4,160,1024]{2,1,0:T(8,128)(2,1)} %bitcast_dynamic-update-slice_fusion.17), channel_id=1, source_target_pairs={{0,32},{32,64},{64,96},{96,0},{1,33},{33,65},{65,97},{97,1},{2,34}... | collective-permute-start | bytes 3932168 | tf_op jit(solution)/shard_map/ppermute | solution.py:22
  40.6 41.2 %collective-permute-start.10 = (bf16[4,160,1024]{2,1,0:T(8,128)(2,1)}, bf16[4,160,1024]{2,1,0:T(8,128)(2,1)}, u32[]{:S(2)}, u32[]{:S(2)}) collective-permute-start(bf16[4,160,1024]{2,1,0:T(8,128)(2,1)} %bitcast_dynamic-update-slice_fusion.17), channel_id=1, source_target_pairs={{0,96},{32,0},{64,32},{96,64},{1,97},{33,1},{65,33},{97,65},{2,98}... | collective-permute-start | bytes 3932168 | tf_op jit(solution)/shard_map/ppermute | solution.py:22
  44.3 41.1 %collective-permute-start.16 = (bf16[4,160,1024]{2,1,0:T(8,128)(2,1)S(1)}, bf16[4,160,1024]{2,1,0:T(8,128)(2,1)}, u32[]{:S(2)}, u32[]{:S(2)}) collective-permute-start(bf16[4,160,1024]{2,1,0:T(8,128)(2,1)S(1)} %bitcast_dynamic-update-slice_fusion.13), channel_id=1, source_target_pairs={{0,8},{8,16},{16,24},{24,0},{1,9},{9,17},{17,25},{25,1},{2,10},{10... | collective-permute-start | bytes 3932168 | tf_op jit(solution)/shard_map/ppermute | solution.py:22
  53.7 41.3 %collective-permute-start.17 = (bf16[4,160,1024]{2,1,0:T(8,128)(2,1)S(1)}, bf16[4,160,1024]{2,1,0:T(8,128)(2,1)}, u32[]{:S(2)}, u32[]{:S(2)}) collective-permute-start(bf16[4,160,1024]{2,1,0:T(8,128)(2,1)S(1)} %bitcast_dynamic-update-slice_fusion.13), channel_id=1, source_target_pairs={{0,24},{8,0},{16,8},{24,16},{1,25},{9,1},{17,9},{25,17},{2,26},{10... | collective-permute-start | bytes 3932168 | tf_op jit(solution)/shard_map/ppermute | solution.py:22
  68.8 34.8 %all-to-all-start.3 = ((bf16[32,16,1024]{2,1,0:T(8,128)(2,1)}), bf16[32,16,1024]{2,1,0:T(8,128)(2,1)S(1)}, u32[]{:S(2)}, u32[]{:S(2)}) async-start(bf16[32,16,1024]{2,1,0:T(8,128)(2,1)} %bitcast.59), calls=%async_computation.3 | async-start | bytes 2097152 | tf_op jit(solution)/shard_map/all_to_all | solution.py:151
  77.8 52.9 %collective-permute-start.5 = (bf16[256,5120]{1,0:T(8,128)(2,1)}, bf16[256,5120]{1,0:T(8,128)(2,1)}, u32[]{:S(2)}, u32[]{:S(2)}) collective-permute-start(bf16[256,5120]{1,0:T(8,128)(2,1)} %bitcast.126), channel_id=1, source_target_pairs={{0,4},{4,0},{1,5},{5,1},{2,6},{6,2},{3,7},{7,3},{8,12},{12,8},{9,1... | collective-permute-start | bytes 7864328 | tf_op jit(solution)/shard_map/ppermute | solution.py:22
  80.1 25.4 %collective-permute-start.11 = (bf16[2,160,1024]{2,1,0:T(8,128)(2,1)}, bf16[2,160,1024]{2,1,0:T(8,128)(2,1)}, u32[]{:S(2)}, u32[]{:S(2)}) collective-permute-start(bf16[2,160,1024]{2,1,0:T(8,128)(2,1)} %slice.95), channel_id=1, source_target_pairs={{0,32},{32,64},{64,96},{96,0},{1,33},{33,65},{65,97},{97,1},{2,34}... | collective-permute-start | bytes 1966088 | tf_op jit(solution)/shard_map/ppermute | solution.py:22
  83.8 23.6 %collective-permute-start.12 = (bf16[2,160,1024]{2,1,0:T(8,128)(2,1)}, bf16[2,160,1024]{2,1,0:T(8,128)(2,1)}, u32[]{:S(2)}, u32[]{:S(2)}) collective-permute-start(bf16[2,160,1024]{2,1,0:T(8,128)(2,1)} %slice.96), channel_id=1, source_target_pairs={{0,96},{32,0},{64,32},{96,64},{1,97},{33,1},{65,33},{97,65},{2,98}... | collective-permute-start | bytes 1966088 | tf_op jit(solution)/shard_map/ppermute | solution.py:22
  87.3 28.2 %collective-permute-start.18 = (bf16[2,160,1024]{2,1,0:T(8,128)(2,1)}, bf16[2,160,1024]{2,1,0:T(8,128)(2,1)S(1)}, u32[]{:S(2)}, u32[]{:S(2)}) collective-permute-start(bf16[2,160,1024]{2,1,0:T(8,128)(2,1)} %slice.97), channel_id=1, source_target_pairs={{0,8},{8,16},{16,24},{24,0},{1,9},{9,17},{17,25},{25,1},{2,10},{10... | collective-permute-start | bytes 1966088 | tf_op jit(solution)/shard_map/ppermute | solution.py:22
  96.9 19.6 %collective-permute-start.19 = (bf16[2,160,1024]{2,1,0:T(8,128)(2,1)}, bf16[2,160,1024]{2,1,0:T(8,128)(2,1)}, u32[]{:S(2)}, u32[]{:S(2)}) collective-permute-start(bf16[2,160,1024]{2,1,0:T(8,128)(2,1)} %slice.98), channel_id=1, source_target_pairs={{0,24},{8,0},{16,8},{24,16},{1,25},{9,1},{17,9},{25,17},{2,26},{10... | collective-permute-start | bytes 1966088 | tf_op jit(solution)/shard_map/ppermute | solution.py:22
  130.8 20.8 %collective-permute-start.20 = (bf16[256,5120]{1,0:T(8,128)(2,1)}, bf16[256,5120]{1,0:T(8,128)(2,1)}, u32[]{:S(2)}, u32[]{:S(2)}) collective-permute-start(bf16[256,5120]{1,0:T(8,128)(2,1)} %convolution_convert_fusion.1), channel_id=1, source_target_pairs={{0,4},{4,0},{1,5},{5,1},{2,6},{6,2},{3,7},{7,3},{8,12},{12,8},{9,1... | collective-permute-start | bytes 7864328 | tf_op jit(solution)/shard_map/ppermute | solution.py:22
  145.6 22.5 %all-to-all-start = ((bf16[32,16,1024]{2,1,0:T(8,128)(2,1)}), bf16[32,16,1024]{2,1,0:T(8,128)(2,1)S(1)}, u32[]{:S(2)}, u32[]{:S(2)}) async-start(bf16[32,16,1024]{2,1,0:T(8,128)(2,1)} %bitcast.42), calls=%async_computation | async-start | bytes 2097152 | tf_op jit(solution)/shard_map/all_to_all | solution.py:175
  176.5 18.4 %collective-permute-start.22 = (bf16[64,5120]{1,0:T(8,128)(2,1)}, bf16[64,5120]{1,0:T(8,128)(2,1)}, u32[]{:S(2)}, u32[]{:S(2)}) collective-permute-start(bf16[64,5120]{1,0:T(8,128)(2,1)} %pad_maximum_fusion.2), channel_id=1, source_target_pairs={{0,1},{1,2},{2,3},{3,0},{4,5},{5,6},{6,7},{7,4},{8,9},{9,10},{10,1... | collective-permute-start | bytes 1966088 | tf_op jit(solution)/shard_map/ppermute | solution.py:22
  181.1 19.2 %collective-permute-start.24 = (bf16[64,5120]{1,0:T(8,128)(2,1)}, bf16[64,5120]{1,0:T(8,128)(2,1)}, u32[]{:S(2)}, u32[]{:S(2)}) collective-permute-start(bf16[64,5120]{1,0:T(8,128)(2,1)} %pad_maximum_fusion.3), channel_id=1, source_target_pairs={{0,3},{1,0},{2,1},{3,2},{4,7},{5,4},{6,5},{7,6},{8,11},{9,8},{10,9... | collective-permute-start | bytes 1966088 | tf_op jit(solution)/shard_map/ppermute | solution.py:22
  184.4 36.8 %all-to-all-start.1 = ((bf16[4,128,2048]{1,2,0:T(8,128)(2,1)}), bf16[4,128,2048]{1,2,0:T(8,128)(2,1)S(1)}, u32[]{:S(2)}, u32[]{:S(2)}) async-start(bf16[4,128,2048]{1,2,0:T(8,128)(2,1)} %bitcast.120), calls=%async_computation.1 | async-start | bytes 4194304 | tf_op jit(solution)/shard_map/all_to_all | solution.py:218
  (17 other events, 136.1 us)

commit v3 on v2

v3 whole, which is shorter than its diff:
```python
import jax
import jax.numpy as jnp
from jax import lax
from jax.experimental import pallas as pl
from jax.experimental.pallas import tpu as pltpu
from jax.sharding import Mesh, PartitionSpec as P

MAXTOK = 8
Y, Z, CORE, X = "y", "z", "core", "seq"
VDP = (Y, Z, CORE)
ALL = (Y, Z, CORE, X)


def normal_cdf(values):
    return 0.5 * (1.0 + jax.scipy.special.erf(values * 0.7071067811865476))


def shift(value, axis, by):
    size = lax.axis_size(axis)
    return lax.ppermute(value, axis, [(i, (i + by) % size) for i in range(size)])


def tie(*values):
    return lax.optimization_barrier(values)


def rows_of_slots(frame_tokens, frame_sample, group, slots):
    tokens = lax.dynamic_slice_in_dim(frame_tokens, group, 1, 0)
    sample = lax.dynamic_slice_in_dim(frame_sample, group, 1, 0)
    frame_ids = jnp.arange(frame_tokens.shape[1], dtype=jnp.int32)
    before = frame_ids[None, :] < frame_ids[:, None]
    starts = jnp.sum(jnp.where(before, tokens, 0), axis=1)[None, :]
    hit = sample == slots // MAXTOK
    step = slots[:, 0] % MAXTOK
    start = jnp.sum(jnp.where(hit, starts, 0), axis=1)
    length = jnp.sum(jnp.where(hit, tokens, 0), axis=1)
    return jnp.where(step < length, start + step, -1)


def spots_of_slots(frame_tokens, frame_sample, clip_offset, own_seq, group_of_slot, step):
    length = jnp.sum(jnp.where(frame_sample == own_seq, frame_tokens, 0), axis=1)[None, :]
    seq_ids = jnp.arange(clip_offset.shape[1], dtype=jnp.int32)
    offset = jnp.sum(jnp.where(seq_ids[None, :] == own_seq, clip_offset, 0), axis=1)[None, :]
    group_ids = jnp.arange(frame_tokens.shape[0], dtype=jnp.int32)
    owner = group_of_slot[:, None] == group_ids[None, :]
    slot_length = jnp.sum(jnp.where(owner, length, 0), axis=1)
    slot_offset = jnp.sum(jnp.where(owner, offset, 0), axis=1)
    return jnp.where(step < slot_length, slot_offset + step, -1)


VMEM_LIMIT = 48 * 1024 * 1024


def kernel_params():
    return pltpu.CompilerParams(vmem_limit_bytes=VMEM_LIMIT)


def cost(flops, moved):
    return pl.CostEstimate(flops=int(flops), bytes_accessed=int(moved), transcendentals=0)


def split_columns(table, parts):
    rows, total = table.shape
    width = total // parts

    def body(in_ref, out_ref):
        out_ref[0] = in_ref[...]

    return pl.pallas_call(
        body,
        grid=(parts,),
        in_specs=[pl.BlockSpec((rows, width), lambda j: (0, j))],
        out_specs=pl.BlockSpec((1, rows, width), lambda j: (j, 0, 0)),
        out_shape=jax.ShapeDtypeStruct((parts, rows, width), table.dtype),
        compiler_params=kernel_params(),
        cost_estimate=cost(0, 4 * rows * total),
        name="split_columns",
    )(table)


def join_columns(table):
    parts, rows, width = table.shape

    def body(in_ref, out_ref):
        out_ref[...] = in_ref[0]

    return pl.pallas_call(
        body,
        grid=(parts,),
        in_specs=[pl.BlockSpec((1, rows, width), lambda j: (j, 0, 0))],
        out_specs=pl.BlockSpec((rows, width), lambda j: (0, j)),
        out_shape=jax.ShapeDtypeStruct((rows, parts * width), table.dtype),
        compiler_params=kernel_params(),
        cost_estimate=cost(0, 4 * rows * parts * width),
        name="join_columns",
    )(table)


def hot_rows(index, count):
    ids = lax.broadcasted_iota(jnp.int32, (index.shape[0], count), 1)
    return jnp.where(index == ids, 1.0, 0.0).astype(jnp.bfloat16)


def hot_columns(index, count):
    ids = lax.broadcasted_iota(jnp.int32, (count, index.shape[1]), 0)
    return jnp.where(index == ids, 1.0, 0.0).astype(jnp.bfloat16)


def exact(selector, table):
    return jnp.dot(selector, table, preferred_element_type=jnp.float32).astype(jnp.bfloat16)


def gather_spots(spots, columns, chips, cores):
    n = spots.shape[1]
    parts, span, slab = columns.shape
    half = slab // cores
    per = n // chips

    def body(spot_ref, table_ref, out_ref):
        table = table_ref[...].reshape(parts * span, half)
        picked = exact(hot_rows(spot_ref[0], parts * span), table)
        out_ref[...] = picked.reshape(chips, 1, per, half)

    return pl.pallas_call(
        body,
        grid=(cores,),
        in_specs=[
            pl.BlockSpec((1, n, 1), lambda c: (c, 0, 0)),
            pl.BlockSpec((parts, span, half), lambda c: (0, 0, c)),
        ],
        out_specs=pl.BlockSpec((chips, 1, per, half), lambda c: (0, c, 0, 0)),
        out_shape=jax.ShapeDtypeStruct((chips, cores, per, half), columns.dtype),
        compiler_params=kernel_params(),
        cost_estimate=cost(2 * n * parts * span * slab, 4 * parts * span * slab),
        name="gather_spots",
    )(spots, columns)


def scatter_spots(spots, incoming, parts, span):
    chips, cores, per, half = incoming.shape
    n = chips * per

    def body(spot_ref, table_ref, out_ref):
        table = table_ref[...].reshape(n, half)
        placed = exact(hot_columns(spot_ref[0], parts * span), table)
        out_ref[...] = placed.reshape(parts, span, half)

    return pl.pallas_call(
        body,
        grid=(cores,),
        in_specs=[
            pl.BlockSpec((1, 1, n), lambda c: (c, 0, 0)),
            pl.BlockSpec((chips, 1, per, half), lambda c: (0, c, 0, 0)),
        ],
        out_specs=pl.BlockSpec((parts, span, half), lambda c: (0, 0, c)),
        out_shape=jax.ShapeDtypeStruct((parts, span, cores * half), incoming.dtype),
        compiler_params=kernel_params(),
        cost_estimate=cost(2 * n * parts * span * cores * half, 4 * parts * span * cores * half),
        name="scatter_spots",
    )(spots, incoming)


def pick_rows(index, own, other, width):
    n = index.shape[0]
    rows, total = own.shape

    def body(index_ref, own_ref, other_ref, out_ref):
        selector = hot_rows(index_ref[...], 2 * rows)
        picked = jnp.dot(selector[:, :rows], own_ref[...], preferred_element_type=jnp.float32)
        picked += jnp.dot(selector[:, rows:], other_ref[...], preferred_element_type=jnp.float32)
        out_ref[...] = picked.astype(jnp.bfloat16)

    return pl.pallas_call(
        body,
        grid=(total // width,),
        in_specs=[
            pl.BlockSpec((n, 1), lambda j: (0, 0)),
            pl.BlockSpec((rows, width), lambda j: (0, j)),
            pl.BlockSpec((rows, width), lambda j: (0, j)),
        ],
        out_specs=pl.BlockSpec((n, width), lambda j: (0, j)),
        out_shape=jax.ShapeDtypeStruct((n, total), own.dtype),
        compiler_params=kernel_params(),
        cost_estimate=cost(4 * n * rows * total, 8 * rows * total),
        name="pick_rows",
    )(index, own, other)


def unpick_rows(index, table, rows):
    n, width = table.shape

    def body(index_ref, table_ref, out_ref):
        out_ref[...] = exact(hot_columns(index_ref[...], rows), table_ref[...])

    return pl.pallas_call(
        body,
        out_shape=jax.ShapeDtypeStruct((rows, width), table.dtype),
        compiler_params=kernel_params(),
        cost_estimate=cost(2 * n * rows * width, 4 * rows * width),
        name="unpick_rows",
    )(index, table)


def project_back(places, grad, pieces, block, hidden):
    n, half = grad.shape
    tile = 1024
    count = len(pieces)
    blocks = [(p, b * block) for p in range(count) for b in range(pieces[p].shape[0] // block)]

    def body(*refs):
        place_ref, grad_ref = refs[:2]
        piece_refs = refs[2 : 2 + count]
        kept_ref, away_ref, weight_ref, held, arrive, leave = refs[2 + count :]
        copies = []
        for i, (p, start) in enumerate(blocks):
            first = pl.multiple_of(place_ref[i], block)
            copies.append(
                pltpu.make_async_copy(
                    piece_refs[p].at[pl.ds(start, block)],
                    held.at[pl.ds(first, block)],
                    arrive.at[i],
                )
            )
        for copy in copies:
            copy.start()
        for copy in copies:
            copy.wait()
        onward = pltpu.make_async_copy(held, weight_ref, leave)
        onward.start()

        @pl.loop(0, hidden // tile)
        def _(j):
            span = pl.ds(pl.multiple_of(j * tile, tile), tile)
            product = lax.dot_general(
                grad_ref[...],
                held[span, :],
                (((1,), (1,)), ((), ())),
                preferred_element_type=jnp.float32,
            )
            kept_ref[:, span] = product[: n // 2].astype(jnp.bfloat16)
            away_ref[:, span] = product[n // 2 :].astype(jnp.bfloat16)

        onward.wait()

    vmem = pl.BlockSpec(memory_space=pltpu.VMEM)
    anywhere = pl.BlockSpec(memory_space=pl.ANY)
    return pl.pallas_call(
        body,
        in_specs=[pl.BlockSpec(memory_space=pltpu.SMEM), vmem] + [anywhere] * count,
        out_specs=[vmem, vmem, anywhere],
        out_shape=[
            jax.ShapeDtypeStruct((n // 2, hidden), jnp.bfloat16),
            jax.ShapeDtypeStruct((n // 2, hidden), jnp.bfloat16),
            jax.ShapeDtypeStruct((hidden, half), jnp.bfloat16),
        ],
        scratch_shapes=[
            pltpu.VMEM((hidden, half), jnp.bfloat16),
            pltpu.SemaphoreType.DMA((len(blocks),)),
            pltpu.SemaphoreType.DMA,
        ],
        compiler_params=kernel_params(),
        cost_estimate=cost(2 * n * hidden * half, 6 * hidden * half),
        name="project_back",
    )(places, grad, *pieces)


def project(act, bias, weight):
    n, k = act.shape
    half = weight.shape[1]
    tile = 512
    last = k // tile - 1

    def body(act_ref, bias_ref, weight_ref, out_ref, total):
        j = pl.program_id(0)
        product = jnp.dot(act_ref[...], weight_ref[...], preferred_element_type=jnp.float32)

        @pl.when(j == 0)
        def _():
            total[...] = product

        @pl.when(j > 0)
        def _():
            total[...] += product

        @pl.when(j == last)
        def _():
            out_ref[...] = (total[...] + bias_ref[...]).astype(jnp.bfloat16)

    return pl.pallas_call(
        body,
        grid=(k // tile,),
        in_specs=[
            pl.BlockSpec((n, tile), lambda j: (0, j)),
            pl.BlockSpec((1, half), lambda j: (0, 0)),
            pl.BlockSpec((tile, half), lambda j: (j, 0)),
        ],
        out_specs=pl.BlockSpec((n, half), lambda j: (0, 0)),
        out_shape=jax.ShapeDtypeStruct((n, half), jnp.bfloat16),
        scratch_shapes=[pltpu.VMEM((n, half), jnp.float32)],
        compiler_params=kernel_params(),
        cost_estimate=cost(2 * n * k * half, 2 * k * half),
        name="project",
    )(act, bias, weight)


def local(pre_act, proj_weight, proj_bias, frame_tokens, frame_sample, clip_offset, embed_grad):
    ny, nz, nc, nx = (lax.axis_size(a) for a in ALL)
    iy, iz, ic, ix = (lax.axis_index(a) for a in ALL)
    chip = iy * nz + iz
    own = chip * nc + ic
    sibling = chip * nc + 1 - ic
    groups = ny * nz * nc
    own_rows, hidden = pre_act.shape
    total_rows = own_rows * nx
    span = embed_grad.shape[0]
    seq_len = span * nx
    krows, slab = proj_weight.shape
    half = slab // nc
    slot_total = groups * MAXTOK

    rows = pre_act.astype(jnp.float32)
    cdf = normal_cdf(rows)
    activated = (rows * cdf).astype(jnp.bfloat16)
    columns = lax.all_to_all(
        split_columns(embed_grad, nx), X, split_axis=0, concat_axis=0, tiled=True
    )

    step = jnp.arange(slot_total, dtype=jnp.int32) % MAXTOK
    pair = jnp.arange(slot_total, dtype=jnp.int32) // (nc * MAXTOK)
    member = jnp.arange(slot_total, dtype=jnp.int32) // MAXTOK % nc
    spots = jnp.stack(
        [
            spots_of_slots(
                frame_tokens, frame_sample, clip_offset, own, pair * nc + (member if c == 0 else 1 - member), step
            )
            for c in range(nc)
        ]
    )
    n_slots = nc * slot_total
    ids = lax.broadcasted_iota(jnp.int32, (n_slots, groups), 0)
    slots = ids // (nc * MAXTOK) * MAXTOK + ids % MAXTOK
    from_own = ids[:, 0] // MAXTOK % nc == 0
    row_own = rows_of_slots(frame_tokens, frame_sample, own, slots)
    row_sib = rows_of_slots(frame_tokens, frame_sample, sibling, slots)
    row_of = jnp.where(from_own, row_own, jnp.where(row_sib >= 0, row_sib + total_rows, -1))
    def cross(value, near, by):
        pairs = []
        for y in range(ny):
            for z in range(nz):
                for c in range(nc):
                    to = (y, (z + by) % nz) if (c == 0) == near else ((y + by) % ny, z)
                    pairs.append(((y * nz + z) * nc + c, (to[0] * nz + to[1]) * nc + c))
        return lax.ppermute(value, VDP, pairs)

    steps = (0, -1, 1, 2)
    line = jnp.concatenate([proj_weight] + [cross(proj_weight, True, d) for d in (1, -1, 2)])
    mine = lax.dynamic_slice_in_dim(line, ic * half, half, 1)
    theirs = shift(lax.dynamic_slice_in_dim(line, (1 - ic) * half, half, 1), CORE, 1)
    lines = list(tie(mine, theirs, columns, activated))
    columns, activated = lines[2:]
    right, left = shift(activated, X, 1), shift(activated, X, -1)
    plus = [cross(lines[0], False, 1), cross(lines[1], True, 1)]
    minus = [cross(lines[0], False, -1), cross(lines[1], True, -1)]
    plus[0], plus[1], minus[0], minus[1] = tie(*plus, *minus)
    middle = 2 * krows
    far = [
        (
            cross(plus[whose][:middle], whose == 1, 1),
            cross(minus[whose][middle:], whose == 1, -1),
        )
        for whose in range(nc)
    ]
    pieces, places = [], []
    for whose in range(nc):
        which = ic if whose == 0 else 1 - ic
        for piece, nears, away_by in (
            (lines[whose], steps, 0),
            (plus[whose], steps, -1),
            (minus[whose], steps, 1),
            (far[whose][0], steps[:2], 2),
            (far[whose][1], steps[2:], 2),
        ):
            pieces.append(piece)
            for near_by in nears:
                dy = jnp.where(which == 0, away_by, near_by)
                dz = jnp.where(which == 0, near_by, away_by)
                places.append((((iy + dy) % ny * nz + (iz + dz) % nz) * nc + which) * krows)
    places = jnp.stack(places).astype(jnp.int32)

    send_box = gather_spots(spots[:, :, None], columns, ny * nz, nc)
    everyone = jnp.concatenate(
        [
            activated,
            right,
            left,
            shift(tie(right, send_box)[0][: own_rows // 2], X, 1),
            shift(tie(left, send_box)[0][own_rows // 2 :], X, -1),
        ]
    )
    away_by = (row_of // own_rows - ix) % nx
    seat = jnp.where(away_by == nx - 1, 1, jnp.where(away_by == 0, 0, away_by + 1))
    act_row = jnp.where(
        row_of < 0, -1, row_of // total_rows * total_rows + seat * own_rows + row_of % own_rows
    )

    returned = lax.all_to_all(
        send_box.reshape(groups, nc * MAXTOK, half), VDP, split_axis=0, concat_axis=0, tiled=True
    )
    returned = tie(returned, *far[0], *far[1])[0]
    row_grad = unpick_rows(row_of[None, :], returned.reshape(n_slots, half), nc * total_rows)

    other = shift(everyone, CORE, 1)
    act_slots = pick_rows(act_row[:, None], everyone, other, hidden // 4)

    bias = lax.dynamic_slice_in_dim(proj_bias, ic * half, half, 0).astype(jnp.float32)[None, :]
    kept_sum, away, weight = project_back(places, row_grad, pieces, krows, hidden)
    received = shift(away, CORE, 1).reshape(nx, own_rows, hidden)
    kept_sum = kept_sum.reshape(nx, own_rows, hidden)
    projected = project(act_slots, bias, weight)
    incoming = lax.all_to_all(
        projected.reshape(groups, nc * MAXTOK, half), VDP, split_axis=0, concat_axis=0, tiled=True
    ).reshape(ny * nz, nc, nc * MAXTOK, half)

    def part(d):
        here = (ix + d) % nx
        mine = lax.dynamic_index_in_dim(kept_sum, here, 0, keepdims=False)
        theirs = lax.dynamic_index_in_dim(received, here, 0, keepdims=False)
        return mine.astype(jnp.float32) + theirs.astype(jnp.float32)

    mid = hidden // 2
    far = part(2).astype(jnp.bfloat16)
    far_right = shift(far[:, :mid], X, 1)
    far_left = shift(far[:, mid:], X, -1)
    to_right, to_left = part(1), part(-1)
    got_right_top = shift((to_right[:, :mid] + far_right.astype(jnp.float32)).astype(jnp.bfloat16), X, 1)
    got_right_end = shift(to_right[:, mid:].astype(jnp.bfloat16), X, 1)
    got_left_top = shift(to_left[:, :mid].astype(jnp.bfloat16), X, -1)
    got_left_end = shift((to_left[:, mid:] + far_left.astype(jnp.float32)).astype(jnp.bfloat16), X, -1)
    arrived = jnp.concatenate(
        [
            got_right_top.astype(jnp.float32) + got_left_top.astype(jnp.float32),
            got_right_end.astype(jnp.float32) + got_left_end.astype(jnp.float32),
        ],
        axis=1,
    )
    summed = part(0) + arrived
    slope = cdf + rows * jnp.exp(-0.5 * rows * rows) * 0.3989422804014327
    pre_grad = (summed * slope).astype(jnp.bfloat16)

    line = scatter_spots(spots[:, None, :], incoming, nx, span)
    placed = lax.all_to_all(line, X, split_axis=0, concat_axis=0, tiled=True)
    placed, pre_grad = tie(placed, pre_grad)
    return (join_columns(placed), pre_grad)


def solution(mesh):
    fine = Mesh(mesh.devices.reshape(4, 4, 2, 4), ALL)
    in_specs = (P(ALL, None), P(VDP, X), P(X), P(), P(), P(), P(ALL, None))
    out_specs = (P(ALL, None), P(ALL, None))
    return jax.shard_map(local, mesh=fine, in_specs=in_specs, out_specs=out_specs, check_vma=False)
```

time: 225 us -> 216 us (0.960); the launches traced: 224 us -> 212 us
  matrix products: 43.7 us -> 0 us
  Pallas kernels: 0 us -> 40.3 us
  local copies, waits for them, and re-layouts: 55.4 us -> 30.7 us
  waiting for transfers between devices: 47.6 us -> 69.2 us
  starting transfers between devices: 61.5 us -> 53.3 us
    dot_general x8 -> x0, matrix products: 43.7 us -> none  [the longest x2 23.9 us: back(): lax.dot_general(grad, weight, (((1,), (1,)), ((), ())), preferred_element...]
    pallas_call x0 -> x8, Pallas kernels: none -> 40.3 us  [the longest x1 13.8 us: project(): pl.pallas_call(body, grid=(k // tile,), in_specs=[pl.BlockSpec((n, tile),...]
    ppermute x25 -> x13, starting transfers between devices: 36.6 us -> 11.5 us  [shift(): lax.ppermute(value, axis, [(i, (i + by) % size) for i in range(size)])]
    dynamic_update_slice x19 -> x0, local copies, waits for them, and re-layouts: 23 us -> none  [the longest x10 20.5 us: put(): lax.dynamic_update_slice(weight, piece, (y % ny, z % nz, jnp.int32(which)...]
    ppermute x0 -> x11, waiting for transfers between devices: none -> 22.8 us  [cross(): return lax.ppermute(value, VDP, pairs)]
    ppermute x0 -> x11, starting transfers between devices: none -> 20.1 us  [cross(): return lax.ppermute(value, VDP, pairs)]
    all_to_all x1, waiting for transfers between devices: 17.8 us -> 0.01 us  [local(): placed = lax.all_to_all(line, X, split_axis=0, concat_axis=0, tiled=True)]
    all_to_all x2, waiting for transfers between devices: 0.01 us -> 10.4 us  [the longest x1 10.4 us: local(): lax.all_to_all(split_columns(embed_grad, nx), X, split_axis=0, concat_axi...]
  transfers between devices with their start and end apart: 29 -> 28, of which waited for: 13 -> 11; matrix products, arithmetic and copies ran while one was open for 48% -> 20% of each run, Pallas kernels for 0% -> 18%
where the time goes in v3:
time: 216 us; the launch traced here: 212 us
  waiting for transfers between devices  69.2 us (32%)
  starting transfers between devices  53.3 us (25%)
  Pallas kernels  40.3 us (19%)
  local copies, waits for them, and re-layouts  30.7 us (14%)
  other arithmetic  16.8 us (8%)
    ppermute x13, waiting for transfers between devices, shift(): lax.ppermute(value, axis, [(i, (i + by) % size) for i in range(size)])  31.6 us
    ppermute x11, waiting for transfers between devices, cross(): return lax.ppermute(value, VDP, pairs)  22.8 us
    ppermute x11, starting transfers between devices, cross(): return lax.ppermute(value, VDP, pairs)  20.1 us
    pallas_call x1, Pallas kernels, project(): pl.pallas_call(body, grid=(k // tile,), in_specs=[pl.BlockSpec((n, tile),...  13.8 us
    pallas_call x1, Pallas kernels, project_back(): pl.pallas_call(body, in_specs=[pl.BlockSpec(memory_space=pltpu.SMEM), vme...  13.5 us
    unnamed x37, local copies, waits for them, and re-layouts  13.3 us
    ppermute x13, starting transfers between devices, shift(): lax.ppermute(value, axis, [(i, (i + by) % size) for i in range(size)])  11.5 us
    all_to_all x1, waiting for transfers between devices, local(): lax.all_to_all(split_columns(embed_grad, nx), X, split_axis=0, concat_axi...  10.4 us
  transfers between devices with their start and end apart: 28, of which 11 were waited for; matrix products, arithmetic and copies ran while one was open for 20% of the time, Pallas kernels for 18%

profile of v3, /device:TPU:6, one launch (start us, length us, event | category | flops | bytes accessed | tf_op | source)
XLA Modules:
  0.0 211.6 jit_solution(5592467066313543688)
XLA Ops:
  2.6 2.2 %collective-permute-start.1 = (bf16[160,2048]{1,0:T(8,128)(2,1)}, bf16[160,2048]{1,0:T(8,128)(2,1)}, u32[]{:S(2)}, u32[]{:S(2)}) collective-permute-start(bf16[160,2048]{1,0:T(8,128)(2,1)} %param.8), channel_id=1, source_target_pairs={{0,24},{4,100},{8,0},{12,108},{16,8},{20,116},{24,16},{28,124},{32... | collective-permute-start | bytes 1966088 | tf_op jit(solution)/shard_map/ppermute | solution.py:353
  9.9 4.9 %all-to-all-start = ((bf16[4,128,2048]{2,1,0:T(8,128)(2,1)}), bf16[4,128,2048]{2,1,0:T(8,128)(2,1)S(1)}, u32[]{:S(2)}, u32[]{:S(2)}) async-start(bf16[4,128,2048]{2,1,0:T(8,128)(2,1)} %copy-done), calls=%async_computation | async-start | bytes 4194304 | tf_op jit(solution)/shard_map/all_to_all | solution.py:324
  24.9 2.2 %fusion.3 = bf16[64,5120]{1,0:T(8,128)(2,1)} fusion(bf16[64,5120]{1,0:T(8,128)(2,1)} %param.7), kind=kLoop, calls=%fused_computation.8 | loop fusion | flops 1966080 | bytes 1310720 | tf_op jit(solution)/shard_map/convert_element_type | solution.py:323
  27.1 10.4 %all-to-all-done.table_ref = bf16[4,128,2048]{2,1,0:T(8,128)(2,1)S(1)} async-done(((bf16[4,128,2048]{2,1,0:T(8,128)(2,1)}), bf16[4,128,2048]{2,1,0:T(8,128)(2,1)S(1)}, u32[]{:S(2)}, u32[]{:S(2)}) %all-to-all-start) | async-done | bytes 2097184 | tf_op jit(solution)/shard_map/all_to_all | solution.py:324
  37.5 3.2 %collective-permute-start.4 = (bf16[64,5120]{1,0:T(8,128)(2,1)}, bf16[64,5120]{1,0:T(8,128)(2,1)}, u32[]{:S(2)}, u32[]{:S(2)}) collective-permute-start(bf16[64,5120]{1,0:T(8,128)(2,1)} %fusion.3), channel_id=1, source_target_pairs={{0,1},{1,2},{2,3},{3,0},{4,5},{5,6},{6,7},{7,4},{8,9},{9,10},{10,1... | collective-permute-start | bytes 1966088 | tf_op jit(solution)/shard_map/ppermute | solution.py:20
  49.9 4.9 %all-to-all-start.1 = ((bf16[32,16,1024]{2,1,0:T(8,128)(2,1)}), bf16[32,16,1024]{2,1,0:T(8,128)(2,1)S(1)}, u32[]{:S(2)}, u32[]{:S(2)}) async-start(bf16[32,16,1024]{2,1,0:T(8,128)(2,1)} %bitcast.50), calls=%async_computation.1 | async-start | bytes 2097152 | tf_op jit(solution)/shard_map/all_to_all | solution.py:406
  60.4 2.0 constant_dynamic-update-slice_fusion.7
  64.4 4.7 %collective-permute-done.6 = bf16[32,5120]{1,0:T(8,128)(2,1)S(1)} collective-permute-done((bf16[32,5120]{1,0:T(8,128)(2,1)S(1)}, bf16[32,5120]{1,0:T(8,128)(2,1)S(1)}, u32[]{:S(2)}, u32[]{:S(2)}) %collective-permute-start.6) | collective-permute-done | bytes 327712 | tf_op jit(solution)/shard_map/ppermute | solution.py:20
  69.8 6.7 %collective-permute-done.11.refs_4_ = bf16[640,1024]{1,0:T(8,128)(2,1)} collective-permute-done((bf16[640,1024]{1,0:T(8,128)(2,1)S(1)}, bf16[640,1024]{1,0:T(8,128)(2,1)}, u32[]{:S(2)}, u32[]{:S(2)}) %collective-permute-start.11) | collective-permute-done | bytes 1310752 | tf_op jit(solution)/shard_map/ppermute | solution.py:353
  76.4 7.0 %collective-permute-done.12.refs_9_ = bf16[640,1024]{1,0:T(8,128)(2,1)} collective-permute-done((bf16[640,1024]{1,0:T(8,128)(2,1)}, bf16[640,1024]{1,0:T(8,128)(2,1)}, u32[]{:S(2)}, u32[]{:S(2)}) %collective-permute-start.12) | collective-permute-done | bytes 1310752 | tf_op jit(solution)/shard_map/ppermute | solution.py:353
  86.9 2.0 slice.61
  90.4 2.0 slice.62
  95.9 2.4 %collective-permute-start.16 = (bf16[320,1024]{1,0:T(8,128)(2,1)}, bf16[320,1024]{1,0:T(8,128)(2,1)}, u32[]{:S(2)}, u32[]{:S(2)}) collective-permute-start(bf16[320,1024]{1,0:T(8,128)(2,1)} %slice.63), channel_id=1, source_target_pairs={{0,24},{4,100},{8,0},{12,108},{16,8},{20,116},{24,16},{28,124},{32... | collective-permute-start | bytes 1966088 | tf_op jit(solution)/shard_map/ppermute | solution.py:353
  99.8 5.4 %collective-permute-done.15.refs_10_ = bf16[320,1024]{1,0:T(8,128)(2,1)} collective-permute-done((bf16[320,1024]{1,0:T(8,128)(2,1)}, bf16[320,1024]{1,0:T(8,128)(2,1)}, u32[]{:S(2)}, u32[]{:S(2)}) %collective-permute-start.15) | collective-permute-done | bytes 655392 | tf_op jit(solution)/shard_map/ppermute | solution.py:353
  107.6 13.5 %project_back.1 = (bf16[256,5120]{1,0:T(8,128)(2,1)}, bf16[256,5120]{1,0:T(8,128)(2,1)}, bf16[5120,1024]{1,0:T(8,128)(2,1)}) custom-call(s32[32]{0:T(128)S(1)} %stack.137.refs_0_, bf16[512,1024]{1,0:T(8,128)(2,1)S(1)} %unpick_rows.1.refs_1_, bf16[640,1024]{1,0:T(8,128)(2,1)S(1)} %get-tuple-element.22.refs_2_, bf16[640,1024]{1,0:T(8,128)(2,1)} %copy-done.10, ...), custom_call_target="tpu_custom_call" | custom-call | flops 5368709120 | bytes 31457280 | tf_op jit(solution)/shard_map/project_back/pallas_call | solution.py:247
  121.4 7.0 %pick_rows.1.act_ref = bf16[512,5120]{1,0:T(8,128)(2,1)} custom-call(s32[512,1]{1,0:T(8,128)S(1)} %copy-done.4, bf16[256,5120]{1,0:T(8,128)(2,1)} %constant_dynamic-update-slice_fusion.4.own_ref, bf16[256,5120]{1,0:T(8,128)(2,1)} %collective-permute-done.8.other_ref), custom_call_target="tpu_custom_call" | custom-call | flops 2684354560 | bytes 10485760 | tf_op jit(solution)/shard_map/pick_rows/pallas_call | solution.py:173
  128.4 13.8 %project.1 = bf16[512,1024]{1,0:T(8,128)(2,1)} custom-call(bf16[512,5120]{1,0:T(8,128)(2,1)} %pick_rows.1.act_ref, f32[1,1024]{1,0:T(1,128)S(1)} %bitcast.72, bf16[5120,1024]{1,0:T(8,128)(2,1)} %get-tuple-element.29.weight_ref), custom_call_target="tpu_custom_call" | custom-call | flops 5368709120 | bytes 10485760 | tf_op jit(solution)/shard_map/project/pallas_call | solution.py:289
  142.1 7.4 %all-to-all-start.2 = ((bf16[32,16,1024]{2,1,0:T(8,128)(2,1)}), bf16[32,16,1024]{2,1,0:T(8,128)(2,1)S(1)}, u32[]{:S(2)}, u32[]{:S(2)}) async-start(bf16[32,16,1024]{2,1,0:T(8,128)(2,1)} %bitcast.52), calls=%async_computation.2 | async-start | bytes 2097152 | tf_op jit(solution)/shard_map/all_to_all | solution.py:420
  149.5 3.7 %add_bitcast_fusion.1 = (f32[64,5120]{1,0:T(8,128)}, f32[64,5120]{1,0:T(8,128)S(1)}, bf16[64,5120]{1,0:T(8,128)(2,1)S(1)}) fusion(bf16[4,64,5120]{2,1,0:T(8,128)(2,1)} %bitcast.55, s32[]{:T(128)S(6)} %select_n.882, bf16[4,64,5120]{2,1,0:T(8,128)(2,1)} %bitcast.73, s32[]{:T(128)S(6)} %select_n.886, s32[]{:T(128)S(6)} %select_n.884), kind=kLoop, calls=%fused_computation.17 | loop fusion | flops 3276800 | bytes 7208972 | tf_op jit(solution)/shard_map/add | solution.py:428
  158.8 3.2 %collective-permute-start.21 = (bf16[64,2560]{1,0:T(8,128)(2,1)}, bf16[64,2560]{1,0:T(8,128)(2,1)}, u32[]{:S(2)}, u32[]{:S(2)}) collective-permute-start(bf16[64,2560]{1,0:T(8,128)(2,1)} %slice.87), channel_id=1, source_target_pairs={{0,1},{1,2},{2,3},{3,0},{4,5},{5,6},{6,7},{7,4},{8,9},{9,10},{10,1... | collective-permute-start | bytes 983048 | tf_op jit(solution)/shard_map/ppermute | solution.py:20
  162.0 4.3 %all-to-all-done.2 = bf16[32,16,1024]{2,1,0:T(8,128)(2,1)S(1)} async-done(((bf16[32,16,1024]{2,1,0:T(8,128)(2,1)}), bf16[32,16,1024]{2,1,0:T(8,128)(2,1)S(1)}, u32[]{:S(2)}, u32[]{:S(2)}) %all-to-all-start.2) | async-done | bytes 1048608 | tf_op jit(solution)/shard_map/all_to_all | solution.py:420
  168.8 4.5 %all-to-all-start.3 = ((bf16[4,128,2048]{2,1,0:T(8,128)(2,1)}), bf16[4,128,2048]{2,1,0:T(8,128)(2,1)S(1)}, u32[]{:S(2)}, u32[]{:S(2)}) async-start(bf16[4,128,2048]{2,1,0:T(8,128)(2,1)} %copy-done.1), calls=%async_computation.3 | async-start | bytes 4194304 | tf_op jit(solution)/shard_map/all_to_all | solution.py:451
  177.9 26.9 %collective-permute-done.19 = bf16[64,2560]{1,0:T(8,128)(2,1)S(1)} collective-permute-done((bf16[64,2560]{1,0:T(8,128)(2,1)S(1)}, bf16[64,2560]{1,0:T(8,128)(2,1)S(1)}, u32[]{:S(2)}, u32[]{:S(2)}) %collective-permute-start.19) | collective-permute-done | bytes 327712 | tf_op jit(solution)/shard_map/ppermute | solution.py:20
  206.9 2.9 %fusion.8 = bf16[64,5120]{1,0:T(8,128)(2,1)} fusion(bf16[64,5120]{1,0:T(8,128)(2,1)S(1)} %copy-done.8, f32[64,2560]{1,0:T(8,128)S(1)} %convert_add_fusion, f32[64,2560]{1,0:T(8,128)S(1)} %convert_add_fusion.1, bf16[4,64,5120]{2,1,0:T(8,128)(2,1)} %bitcast.55, s32[]{:T(128)S(6)} %select_n.880, bf16[4,64,5120]{2,1,0:T(8,128)(2,1)} %bitcast.74), kind=kLoop, calls=%fused_computation.13 | loop fusion | flops 5242880 | bytes 3932164 | tf_op jit(solution)/shard_map/convert_element_type | solution.py:448
  (124 shorter events, 63.0 us)
Async XLA Ops:
  0.6 18.5 %collective-permute-start = (bf16[160,2048]{1,0:T(8,128)(2,1)}, bf16[160,2048]{1,0:T(8,128)(2,1)}, u32[]{:S(2)}, u32[]{:S(2)}) collective-permute-start(bf16[160,2048]{1,0:T(8,128)(2,1)} %param.8), channel_id=1, source_target_pairs={{0,8},{4,36},{8,16},{12,44},{16,24},{20,52},{24,0},{28,60},{32,40}... | collective-permute-start | bytes 1966088 | tf_op jit(solution)/shard_map/ppermute | solution.py:353
  2.6 17.7 %collective-permute-start.1 = (bf16[160,2048]{1,0:T(8,128)(2,1)}, bf16[160,2048]{1,0:T(8,128)(2,1)}, u32[]{:S(2)}, u32[]{:S(2)}) collective-permute-start(bf16[160,2048]{1,0:T(8,128)(2,1)} %param.8), channel_id=1, source_target_pairs={{0,24},{4,100},{8,0},{12,108},{16,8},{20,116},{24,16},{28,124},{32... | collective-permute-start | bytes 1966088 | tf_op jit(solution)/shard_map/ppermute | solution.py:353
  4.8 17.3 %collective-permute-start.2 = (bf16[160,2048]{1,0:T(8,128)(2,1)}, bf16[160,2048]{1,0:T(8,128)(2,1)}, u32[]{:S(2)}, u32[]{:S(2)}) collective-permute-start(bf16[160,2048]{1,0:T(8,128)(2,1)} %param.8), channel_id=1, source_target_pairs={{0,16},{4,68},{8,24},{12,76},{16,0},{20,84},{24,8},{28,92},{32,48}... | collective-permute-start | bytes 1966088 | tf_op jit(solution)/shard_map/ppermute | solution.py:353
  9.9 27.6 %all-to-all-start = ((bf16[4,128,2048]{2,1,0:T(8,128)(2,1)}), bf16[4,128,2048]{2,1,0:T(8,128)(2,1)S(1)}, u32[]{:S(2)}, u32[]{:S(2)}) async-start(bf16[4,128,2048]{2,1,0:T(8,128)(2,1)} %copy-done), calls=%async_computation | async-start | bytes 4194304 | tf_op jit(solution)/shard_map/all_to_all | solution.py:324
  24.6 13.0 %collective-permute-start.3 = (bf16[640,1024]{1,0:T(8,128)(2,1)}, bf16[640,1024]{1,0:T(8,128)(2,1)}, u32[]{:S(2)}, u32[]{:S(2)}) collective-permute-start(bf16[640,1024]{1,0:T(8,128)(2,1)} %get-tuple-element.47), channel_id=1, source_target_pairs={{0,4},{4,0},{1,5},{5,1},{2,6},{6,2},{3,7},{7,3},{8,12},{12,8},{9,1... | collective-permute-start | bytes 3932168 | tf_op jit(solution)/shard_map/ppermute | solution.py:20
  37.5 18.1 %collective-permute-start.5 = (bf16[64,5120]{1,0:T(8,128)(2,1)}, bf16[64,5120]{1,0:T(8,128)(2,1)}, u32[]{:S(2)}, u32[]{:S(2)}) collective-permute-start(bf16[64,5120]{1,0:T(8,128)(2,1)} %fusion.3), channel_id=1, source_target_pairs={{0,3},{1,0},{2,1},{3,2},{4,7},{5,4},{6,5},{7,6},{8,11},{9,8},{10,9... | collective-permute-start | bytes 1966088 | tf_op jit(solution)/shard_map/ppermute | solution.py:20
  37.5 20.9 %collective-permute-start.4 = (bf16[64,5120]{1,0:T(8,128)(2,1)}, bf16[64,5120]{1,0:T(8,128)(2,1)}, u32[]{:S(2)}, u32[]{:S(2)}) collective-permute-start(bf16[64,5120]{1,0:T(8,128)(2,1)} %fusion.3), channel_id=1, source_target_pairs={{0,1},{1,2},{2,3},{3,0},{4,5},{5,6},{6,7},{7,4},{8,9},{9,10},{10,1... | collective-permute-start | bytes 1966088 | tf_op jit(solution)/shard_map/ppermute | solution.py:20
  41.8 28.0 %collective-permute-start.10 = (bf16[640,1024]{1,0:T(8,128)(2,1)}, bf16[640,1024]{1,0:T(8,128)(2,1)}, u32[]{:S(2)}, u32[]{:S(2)}) collective-permute-start(bf16[640,1024]{1,0:T(8,128)(2,1)} %collective-permute-done.3.refs_7_), channel_id=1, source_target_pairs={{0,8},{4,36},{8,16},{12,44},{16,24},{20,52},{24,0},{28,60},{32,40}... | collective-permute-start | bytes 3932168 | tf_op jit(solution)/shard_map/ppermute | solution.py:353
  43.7 39.7 %collective-permute-start.12 = (bf16[640,1024]{1,0:T(8,128)(2,1)}, bf16[640,1024]{1,0:T(8,128)(2,1)}, u32[]{:S(2)}, u32[]{:S(2)}) collective-permute-start(bf16[640,1024]{1,0:T(8,128)(2,1)} %collective-permute-done.3.refs_7_), channel_id=1, source_target_pairs={{0,24},{4,100},{8,0},{12,108},{16,8},{20,116},{24,16},{28,124},{32... | collective-permute-start | bytes 3932168 | tf_op jit(solution)/shard_map/ppermute | solution.py:353
  45.3 31.2 %collective-permute-start.11 = (bf16[640,1024]{1,0:T(8,128)(2,1)S(1)}, bf16[640,1024]{1,0:T(8,128)(2,1)}, u32[]{:S(2)}, u32[]{:S(2)}) collective-permute-start(bf16[640,1024]{1,0:T(8,128)(2,1)S(1)} %get-tuple-element.22.refs_2_), channel_id=1, source_target_pairs={{0,96},{4,28},{8,104},{12,4},{16,112},{20,12},{24,120},{28,20},{32... | collective-permute-start | bytes 3932168 | tf_op jit(solution)/shard_map/ppermute | solution.py:353
  49.9 49.2 %all-to-all-start.1 = ((bf16[32,16,1024]{2,1,0:T(8,128)(2,1)}), bf16[32,16,1024]{2,1,0:T(8,128)(2,1)S(1)}, u32[]{:S(2)}, u32[]{:S(2)}) async-start(bf16[32,16,1024]{2,1,0:T(8,128)(2,1)} %bitcast.50), calls=%async_computation.1 | async-start | bytes 2097152 | tf_op jit(solution)/shard_map/all_to_all | solution.py:406
  55.7 28.5 %collective-permute-start.9 = (bf16[640,1024]{1,0:T(8,128)(2,1)S(1)}, bf16[640,1024]{1,0:T(8,128)(2,1)S(1)}, u32[]{:S(2)}, u32[]{:S(2)}) collective-permute-start(bf16[640,1024]{1,0:T(8,128)(2,1)S(1)} %get-tuple-element.22.refs_2_), channel_id=1, source_target_pairs={{0,32},{4,12},{8,40},{12,20},{16,48},{20,28},{24,56},{28,4},{32,64... | collective-permute-start | bytes 3932168 | tf_op jit(solution)/shard_map/ppermute | solution.py:353
  69.0 29.3 %collective-permute-start.7 = (bf16[32,5120]{1,0:T(8,128)(2,1)S(1)}, bf16[32,5120]{1,0:T(8,128)(2,1)S(1)}, u32[]{:S(2)}, u32[]{:S(2)}) collective-permute-start(bf16[32,5120]{1,0:T(8,128)(2,1)S(1)} %slice.59), channel_id=1, source_target_pairs={{0,3},{1,0},{2,1},{3,2},{4,7},{5,4},{6,5},{7,6},{8,11},{9,8},{10,9... | collective-permute-start | bytes 983048 | tf_op jit(solution)/shard_map/ppermute | solution.py:20
  85.2 13.9 %collective-permute-start.13 = (bf16[320,1024]{1,0:T(8,128)(2,1)}, bf16[320,1024]{1,0:T(8,128)(2,1)S(1)}, u32[]{:S(2)}, u32[]{:S(2)}) collective-permute-start(bf16[320,1024]{1,0:T(8,128)(2,1)} %slice.60), channel_id=1, source_target_pairs={{0,32},{4,12},{8,40},{12,20},{16,48},{20,28},{24,56},{28,4},{32,64... | collective-permute-start | bytes 1966088 | tf_op jit(solution)/shard_map/ppermute | solution.py:353
  99.1 22.3 %collective-permute-start.8 = (bf16[256,5120]{1,0:T(8,128)(2,1)}, bf16[256,5120]{1,0:T(8,128)(2,1)}, u32[]{:S(2)}, u32[]{:S(2)}) collective-permute-start(bf16[256,5120]{1,0:T(8,128)(2,1)} %constant_dynamic-update-slice_fusion.4.own_ref), channel_id=1, source_target_pairs={{0,4},{4,0},{1,5},{5,1},{2,6},{6,2},{3,7},{7,3},{8,12},{12,8},{9,1... | collective-permute-start | bytes 7864328 | tf_op jit(solution)/shard_map/ppermute | solution.py:20
  121.2 28.3 %collective-permute-start.17 = (bf16[256,5120]{1,0:T(8,128)(2,1)}, bf16[256,5120]{1,0:T(8,128)(2,1)}, u32[]{:S(2)}, u32[]{:S(2)}) collective-permute-start(bf16[256,5120]{1,0:T(8,128)(2,1)} %get-tuple-element.31), channel_id=1, source_target_pairs={{0,4},{4,0},{1,5},{5,1},{2,6},{6,2},{3,7},{7,3},{8,12},{12,8},{9,1... | collective-permute-start | bytes 7864328 | tf_op jit(solution)/shard_map/ppermute | solution.py:20
  142.1 24.2 %all-to-all-start.2 = ((bf16[32,16,1024]{2,1,0:T(8,128)(2,1)}), bf16[32,16,1024]{2,1,0:T(8,128)(2,1)S(1)}, u32[]{:S(2)}, u32[]{:S(2)}) async-start(bf16[32,16,1024]{2,1,0:T(8,128)(2,1)} %bitcast.52), calls=%async_computation.2 | async-start | bytes 2097152 | tf_op jit(solution)/shard_map/all_to_all | solution.py:420
  154.1 19.2 %collective-permute-start.18 = (bf16[64,2560]{1,0:T(8,128)(2,1)}, bf16[64,2560]{1,0:T(8,128)(2,1)}, u32[]{:S(2)}, u32[]{:S(2)}) collective-permute-start(bf16[64,2560]{1,0:T(8,128)(2,1)} %get-tuple-element.49), channel_id=1, source_target_pairs={{0,1},{1,2},{2,3},{3,0},{4,5},{5,6},{6,7},{7,4},{8,9},{9,10},{10,1... | collective-permute-start | bytes 983048 | tf_op jit(solution)/shard_map/ppermute | solution.py:20
  155.8 22.1 %collective-permute-start.20 = (bf16[64,2560]{1,0:T(8,128)(2,1)}, bf16[64,2560]{1,0:T(8,128)(2,1)}, u32[]{:S(2)}, u32[]{:S(2)}) collective-permute-start(bf16[64,2560]{1,0:T(8,128)(2,1)} %slice.88), channel_id=1, source_target_pairs={{0,3},{1,0},{2,1},{3,2},{4,7},{5,4},{6,5},{7,6},{8,11},{9,8},{10,9... | collective-permute-start | bytes 983048 | tf_op jit(solution)/shard_map/ppermute | solution.py:20
  156.9 17.8 %collective-permute-start.22 = (bf16[64,2560]{1,0:T(8,128)(2,1)}, bf16[64,2560]{1,0:T(8,128)(2,1)}, u32[]{:S(2)}, u32[]{:S(2)}) collective-permute-start(bf16[64,2560]{1,0:T(8,128)(2,1)} %get-tuple-element.50), channel_id=1, source_target_pairs={{0,3},{1,0},{2,1},{3,2},{4,7},{5,4},{6,5},{7,6},{8,11},{9,8},{10,9... | collective-permute-start | bytes 983048 | tf_op jit(solution)/shard_map/ppermute | solution.py:20
  158.8 47.0 %collective-permute-start.21 = (bf16[64,2560]{1,0:T(8,128)(2,1)}, bf16[64,2560]{1,0:T(8,128)(2,1)}, u32[]{:S(2)}, u32[]{:S(2)}) collective-permute-start(bf16[64,2560]{1,0:T(8,128)(2,1)} %slice.87), channel_id=1, source_target_pairs={{0,1},{1,2},{2,3},{3,0},{4,5},{5,6},{6,7},{7,4},{8,9},{9,10},{10,1... | collective-permute-start | bytes 983048 | tf_op jit(solution)/shard_map/ppermute | solution.py:20
  168.8 41.0 %all-to-all-start.3 = ((bf16[4,128,2048]{2,1,0:T(8,128)(2,1)}), bf16[4,128,2048]{2,1,0:T(8,128)(2,1)S(1)}, u32[]{:S(2)}, u32[]{:S(2)}) async-start(bf16[4,128,2048]{2,1,0:T(8,128)(2,1)} %copy-done.1), calls=%async_computation.3 | async-start | bytes 4194304 | tf_op jit(solution)/shard_map/all_to_all | solution.py:451
  174.6 30.1 %collective-permute-start.19 = (bf16[64,2560]{1,0:T(8,128)(2,1)S(1)}, bf16[64,2560]{1,0:T(8,128)(2,1)S(1)}, u32[]{:S(2)}, u32[]{:S(2)}) collective-permute-start(bf16[64,2560]{1,0:T(8,128)(2,1)S(1)} %fusion.11), channel_id=1, source_target_pairs={{0,1},{1,2},{2,3},{3,0},{4,5},{5,6},{6,7},{7,4},{8,9},{9,10},{10,1... | collective-permute-start | bytes 983048 | tf_op jit(solution)/shard_map/ppermute | solution.py:20
  176.0 29.9 %collective-permute-start.23 = (bf16[64,2560]{1,0:T(8,128)(2,1)S(1)}, bf16[64,2560]{1,0:T(8,128)(2,1)S(1)}, u32[]{:S(2)}, u32[]{:S(2)}) collective-permute-start(bf16[64,2560]{1,0:T(8,128)(2,1)S(1)} %fusion.10), channel_id=1, source_target_pairs={{0,3},{1,0},{2,1},{3,2},{4,7},{5,4},{6,5},{7,6},{8,11},{9,8},{10,9... | collective-permute-start | bytes 983048 | tf_op jit(solution)/shard_map/ppermute | solution.py:20
  (19 other events, 138.7 us)

commit v4 on v3

--- a/solution.py
+++ b/solution.py
@@ -264,13 +264,15 @@
     )(places, grad, *pieces)
 
 
-def project(act, bias, weight):
+def project(act, bias, weight, part, parts, earlier):
     n, k = act.shape
     half = weight.shape[1]
-    tile = 512
+    width = half // parts
+    tile = 1024
     last = k // tile - 1
 
-    def body(act_ref, bias_ref, weight_ref, out_ref, total):
+    def body(act_ref, bias_ref, weight_ref, *rest):
+        out_ref, total = rest[-2:]
         j = pl.program_id(0)
         product = jnp.dot(act_ref[...], weight_ref[...], preferred_element_type=jnp.float32)
 
@@ -291,16 +293,18 @@
         grid=(k // tile,),
         in_specs=[
             pl.BlockSpec((n, tile), lambda j: (0, j)),
-            pl.BlockSpec((1, half), lambda j: (0, 0)),
-            pl.BlockSpec((tile, half), lambda j: (j, 0)),
-        ],
-        out_specs=pl.BlockSpec((n, half), lambda j: (0, 0)),
+            pl.BlockSpec((1, width), lambda j: (0, part)),
+            pl.BlockSpec((tile, width), lambda j: (j, part)),
+        ]
+        + [pl.BlockSpec(memory_space=pl.ANY)] * len(earlier),
+        out_specs=pl.BlockSpec((n, width), lambda j: (0, part)),
         out_shape=jax.ShapeDtypeStruct((n, half), jnp.bfloat16),
-        scratch_shapes=[pltpu.VMEM((n, half), jnp.float32)],
-        compiler_params=kernel_params(),
-        cost_estimate=cost(2 * n * k * half, 2 * k * half),
+        scratch_shapes=[pltpu.VMEM((n, width), jnp.float32)],
+        compiler_params=kernel_params(),
+        cost_estimate=cost(2 * n * k * width, 2 * k * width),
+        input_output_aliases={3: 0} if earlier else {},
         name="project",
-    )(act, bias, weight)
+    )(act, bias, weight, *earlier)
 
 
 def local(pre_act, proj_weight, proj_bias, frame_tokens, frame_sample, clip_offset, embed_grad):
@@ -356,12 +360,23 @@
     line = jnp.concatenate([proj_weight] + [cross(proj_weight, True, d) for d in (1, -1, 2)])
     mine = lax.dynamic_slice_in_dim(line, ic * half, half, 1)
     theirs = shift(lax.dynamic_slice_in_dim(line, (1 - ic) * half, half, 1), CORE, 1)
-    lines = list(tie(mine, theirs, columns, activated))
-    columns, activated = lines[2:]
-    right, left = shift(activated, X, 1), shift(activated, X, -1)
+    lines = list(tie(mine, theirs, activated))
+    activated = lines[2]
+    send_box = gather_spots(spots[:, :, None], columns, ny * nz, nc)
+    right = shift(activated, X, 1)
+    left = shift(tie(activated, send_box)[0], X, -1)
     plus = [cross(lines[0], False, 1), cross(lines[1], True, 1)]
     minus = [cross(lines[0], False, -1), cross(lines[1], True, -1)]
-    plus[0], plus[1], minus[0], minus[1] = tie(*plus, *minus)
+    everyone = jnp.concatenate(
+        [
+            activated,
+            right,
+            left,
+            shift(tie(right, send_box)[0][: own_rows // 2], X, 1),
+            shift(tie(left, send_box)[0][own_rows // 2 :], X, -1),
+        ]
+    )
+    plus[0], plus[1], minus[0], minus[1], everyone = tie(*plus, *minus, everyone)
     middle = 2 * krows
     far = [
         (
@@ -387,16 +402,6 @@
                 places.append((((iy + dy) % ny * nz + (iz + dz) % nz) * nc + which) * krows)
     places = jnp.stack(places).astype(jnp.int32)
 
-    send_box = gather_spots(spots[:, :, None], columns, ny * nz, nc)
-    everyone = jnp.concatenate(
-        [
-            activated,
-            right,
-            left,
-            shift(tie(right, send_box)[0][: own_rows // 2], X, 1),
-            shift(tie(left, send_box)[0][own_rows // 2 :], X, -1),
-        ]
-    )
     away_by = (row_of // own_rows - ix) % nx
     seat = jnp.where(away_by == nx - 1, 1, jnp.where(away_by == 0, 0, away_by + 1))
     act_row = jnp.where(
@@ -413,13 +418,11 @@
     act_slots = pick_rows(act_row[:, None], everyone, other, hidden // 4)
 
     bias = lax.dynamic_slice_in_dim(proj_bias, ic * half, half, 0).astype(jnp.float32)[None, :]
+    row_grad, act_slots = tie(row_grad, act_slots)
     kept_sum, away, weight = project_back(places, row_grad, pieces, krows, hidden)
     received = shift(away, CORE, 1).reshape(nx, own_rows, hidden)
     kept_sum = kept_sum.reshape(nx, own_rows, hidden)
-    projected = project(act_slots, bias, weight)
-    incoming = lax.all_to_all(
-        projected.reshape(groups, nc * MAXTOK, half), VDP, split_axis=0, concat_axis=0, tiled=True
-    ).reshape(ny * nz, nc, nc * MAXTOK, half)
+    projected = project(act_slots, bias, weight, 0, 2, [])
 
     def part(d):
         here = (ix + d) % nx
@@ -429,6 +432,12 @@
 
     mid = hidden // 2
     far = part(2).astype(jnp.bfloat16)
+    far, act_slots = tie(far, act_slots)
+    projected = project(act_slots, bias, weight, 1, 2, [projected])
+    incoming = lax.all_to_all(
+        projected.reshape(groups, nc * MAXTOK, half), VDP, split_axis=0, concat_axis=0, tiled=True
+    ).reshape(ny * nz, nc, nc * MAXTOK, half)
+
     far_right = shift(far[:, :mid], X, 1)
     far_left = shift(far[:, mid:], X, -1)
     to_right, to_left = part(1), part(-1)

time: 216 us -> 229 us (1.060)
  waiting for transfers between devices: 69.2 us -> 80.1 us
    all_to_all x1, waiting for transfers between devices: 0.01 us -> 19.3 us  [local(): placed = lax.all_to_all(line, X, split_axis=0, concat_axis=0, tiled=True)]
    ppermute x11, waiting for transfers between devices: 22.8 us -> 16.6 us  [cross(): return lax.ppermute(value, VDP, pairs)]
    unnamed x37 -> x69, local copies, waits for them, and re-layouts: 13.3 us -> 18.1 us
    all_to_all x1, waiting for transfers between devices: 4.31 us -> 0.01 us  [local(): lax.all_to_all(projected.reshape(groups, nc * MAXTOK, half), VDP, split_a...]
    ppermute x13, starting transfers between devices: 11.5 us -> 14.9 us  [shift(): lax.ppermute(value, axis, [(i, (i + by) % size) for i in range(size)])]
    ppermute x13, waiting for transfers between devices: 31.6 us -> 34.1 us  [shift(): lax.ppermute(value, axis, [(i, (i + by) % size) for i in range(size)])]
    select_n x0 -> x1, other arithmetic: none -> 2.49 us  [local(): jnp.where(row_of < 0, -1, row_of // total_rows * total_rows + seat * own_...]
    all_to_all x1, starting transfers between devices: 7.37 us -> 4.9 us  [local(): lax.all_to_all(projected.reshape(groups, nc * MAXTOK, half), VDP, split_a...]
  transfers between devices with their start and end apart: 28 -> 28, of which waited for: 11 -> 12; matrix products, arithmetic and copies ran while one was open for 20% -> 15% of each run, Pallas kernels for 18% -> 9%
where the time goes in v4:
time: 229 us; the launch traced here: 226 us
  waiting for transfers between devices  80.1 us (35%)
  starting transfers between devices  53.9 us (24%)
  Pallas kernels  42.4 us (19%)
  local copies, waits for them, and re-layouts  30.7 us (13%)
  other arithmetic  17.5 us (8%)
    ppermute x13, waiting for transfers between devices, shift(): lax.ppermute(value, axis, [(i, (i + by) % size) for i in range(size)])  34.1 us
    ppermute x11, starting transfers between devices, cross(): return lax.ppermute(value, VDP, pairs)  20 us
    all_to_all x1, waiting for transfers between devices, local(): placed = lax.all_to_all(line, X, split_axis=0, concat_axis=0, tiled=True)  19.3 us
    unnamed x69, local copies, waits for them, and re-layouts  18.1 us
    ppermute x11, waiting for transfers between devices, cross(): return lax.ppermute(value, VDP, pairs)  16.6 us
    pallas_call x2, Pallas kernels, project(): pl.pallas_call(body, grid=(k // tile,), in_specs=[pl.BlockSpec((n, tile),...  15.9 us
    ppermute x13, starting transfers between devices, shift(): lax.ppermute(value, axis, [(i, (i + by) % size) for i in range(size)])  14.9 us
    pallas_call x1, Pallas kernels, project_back(): pl.pallas_call(body, in_specs=[pl.BlockSpec(memory_space=pltpu.SMEM), vme...  13.5 us
  transfers between devices with their start and end apart: 28, of which 12 were waited for; matrix products, arithmetic and copies ran while one was open for 15% of the time, Pallas kernels for 9%

profile of v4, /device:TPU:6, one launch (start us, length us, event | category | flops | bytes accessed | tf_op | source)
XLA Modules:
  0.0 225.8 jit_solution(14064485914578592066)
XLA Ops:
  9.9 4.9 %all-to-all-start = ((bf16[4,128,2048]{2,1,0:T(8,128)(2,1)}), bf16[4,128,2048]{2,1,0:T(8,128)(2,1)S(1)}, u32[]{:S(2)}, u32[]{:S(2)}) async-start(bf16[4,128,2048]{2,1,0:T(8,128)(2,1)} %copy-done), calls=%async_computation | async-start | bytes 4194304 | tf_op jit(solution)/shard_map/all_to_all | solution.py:328
  16.4 3.9 %collective-permute-done.1 = bf16[160,2048]{1,0:T(8,128)(2,1)} collective-permute-done((bf16[160,2048]{1,0:T(8,128)(2,1)}, bf16[160,2048]{1,0:T(8,128)(2,1)}, u32[]{:S(2)}, u32[]{:S(2)}) %collective-permute-start.1) | collective-permute-done | bytes 655392 | tf_op jit(solution)/shard_map/ppermute | solution.py:357
  27.4 10.2 %all-to-all-done.table_ref = bf16[4,128,2048]{2,1,0:T(8,128)(2,1)S(1)} async-done(((bf16[4,128,2048]{2,1,0:T(8,128)(2,1)}), bf16[4,128,2048]{2,1,0:T(8,128)(2,1)S(1)}, u32[]{:S(2)}, u32[]{:S(2)}) %all-to-all-start) | async-done | bytes 2097184 | tf_op jit(solution)/shard_map/all_to_all | solution.py:328
  41.2 2.6 %collective-permute-start.6 = (bf16[640,1024]{1,0:T(8,128)(2,1)S(1)}, bf16[640,1024]{1,0:T(8,128)(2,1)S(1)}, u32[]{:S(2)}, u32[]{:S(2)}) collective-permute-start(bf16[640,1024]{1,0:T(8,128)(2,1)S(1)} %get-tuple-element.23.refs_2_), channel_id=1, source_target_pairs={{0,96},{4,28},{8,104},{12,4},{16,112},{20,12},{24,120},{28,20},{32... | collective-permute-start | bytes 3932168 | tf_op jit(solution)/shard_map/ppermute | solution.py:357
  51.1 3.3 %collective-permute-start.7 = (bf16[640,1024]{1,0:T(8,128)(2,1)S(1)}, bf16[640,1024]{1,0:T(8,128)(2,1)S(1)}, u32[]{:S(2)}, u32[]{:S(2)}) collective-permute-start(bf16[640,1024]{1,0:T(8,128)(2,1)S(1)} %copy-done.30), channel_id=1, source_target_pairs={{0,24},{4,100},{8,0},{12,108},{16,8},{20,116},{24,16},{28,124},{32... | collective-permute-start | bytes 3932168 | tf_op jit(solution)/shard_map/ppermute | solution.py:357
  57.5 4.3 %collective-permute-done.9 = bf16[64,5120]{1,0:T(8,128)(2,1)S(1)} collective-permute-done((bf16[64,5120]{1,0:T(8,128)(2,1)}, bf16[64,5120]{1,0:T(8,128)(2,1)S(1)}, u32[]{:S(2)}, u32[]{:S(2)}) %collective-permute-start.9) | collective-permute-done | bytes 655392 | tf_op jit(solution)/shard_map/ppermute | solution.py:20
  63.9 5.0 %collective-permute-done.10 = bf16[32,5120]{1,0:T(8,128)(2,1)S(1)} collective-permute-done((bf16[32,5120]{1,0:T(8,128)(2,1)S(1)}, bf16[32,5120]{1,0:T(8,128)(2,1)S(1)}, u32[]{:S(2)}, u32[]{:S(2)}) %collective-permute-start.10) | collective-permute-done | bytes 327712 | tf_op jit(solution)/shard_map/ppermute | solution.py:20
  69.8 7.3 %collective-permute-done.11 = bf16[32,5120]{1,0:T(8,128)(2,1)S(1)} collective-permute-done((bf16[32,5120]{1,0:T(8,128)(2,1)S(1)}, bf16[32,5120]{1,0:T(8,128)(2,1)S(1)}, u32[]{:S(2)}, u32[]{:S(2)}) %collective-permute-start.11) | collective-permute-done | bytes 327712 | tf_op jit(solution)/shard_map/ppermute | solution.py:20
  82.9 4.6 %all-to-all-start.1 = ((bf16[32,16,1024]{2,1,0:T(8,128)(2,1)}), bf16[32,16,1024]{2,1,0:T(8,128)(2,1)S(1)}, u32[]{:S(2)}, u32[]{:S(2)}) async-start(bf16[32,16,1024]{2,1,0:T(8,128)(2,1)} %bitcast.45), calls=%async_computation.1 | async-start | bytes 2097152 | tf_op jit(solution)/shard_map/all_to_all | solution.py:411
  104.9 12.1 %collective-permute-done.12.refs_5_ = bf16[320,1024]{1,0:T(8,128)(2,1)S(1)} collective-permute-done((bf16[320,1024]{1,0:T(8,128)(2,1)}, bf16[320,1024]{1,0:T(8,128)(2,1)S(1)}, u32[]{:S(2)}, u32[]{:S(2)}) %collective-permute-start.12) | collective-permute-done | bytes 655392 | tf_op jit(solution)/shard_map/ppermute | solution.py:357
  118.6 7.0 %pick_rows.1.act_ref = bf16[512,5120]{1,0:T(8,128)(2,1)} custom-call(s32[512,1]{1,0:T(8,128)S(1)} %copy-done.4, bf16[256,5120]{1,0:T(8,128)(2,1)} %constant_dynamic-update-slice_fusion.4.own_ref, bf16[256,5120]{1,0:T(8,128)(2,1)} %collective-permute-done.16.other_ref), custom_call_target="tpu_custom_call" | custom-call | flops 2684354560 | bytes 10485760 | tf_op jit(solution)/shard_map/pick_rows/pallas_call | solution.py:173
  125.6 13.5 %project_back.1 = (bf16[256,5120]{1,0:T(8,128)(2,1)}, bf16[256,5120]{1,0:T(8,128)(2,1)}, bf16[5120,1024]{1,0:T(8,128)(2,1)}) custom-call(s32[32]{0:T(128)S(1)} %stack.137.refs_0_, bf16[512,1024]{1,0:T(8,128)(2,1)S(1)} %unpick_rows.1.refs_1_, bf16[640,1024]{1,0:T(8,128)(2,1)S(1)} %get-tuple-element.23.refs_2_, bf16[640,1024]{1,0:T(8,128)(2,1)} %copy-done.12, ...), custom_call_target="tpu_custom_call" | custom-call | flops 5368709120 | bytes 31457280 | tf_op jit(solution)/shard_map/project_back/pallas_call | solution.py:247
  139.3 5.1 %collective-permute-done.17 = bf16[256,5120]{1,0:T(8,128)(2,1)} collective-permute-done((bf16[256,5120]{1,0:T(8,128)(2,1)}, bf16[256,5120]{1,0:T(8,128)(2,1)}, u32[]{:S(2)}, u32[]{:S(2)}) %collective-permute-start.17) | collective-permute-done | bytes 2621472 | tf_op jit(solution)/shard_map/ppermute | solution.py:20
  144.4 3.6 %add_bitcast_fusion.1 = (f32[64,5120]{1,0:T(8,128)}, f32[64,5120]{1,0:T(8,128)S(1)}, bf16[64,5120]{1,0:T(8,128)(2,1)S(1)}) fusion(bf16[4,64,5120]{2,1,0:T(8,128)(2,1)} %bitcast.52, s32[]{:T(128)S(6)} %select_n.893, bf16[4,64,5120]{2,1,0:T(8,128)(2,1)} %bitcast.74, s32[]{:T(128)S(6)} %select_n.895, s32[]{:T(128)S(6)} %select_n.889), kind=kLoop, calls=%fused_computation.16 | loop fusion | flops 3276800 | bytes 7208972 | tf_op jit(solution)/shard_map/add | solution.py:431
  148.2 8.0 %project.2.rest_0_ = bf16[512,1024]{1,0:T(8,128)(2,1)} custom-call(bf16[512,5120]{1,0:T(8,128)(2,1)} %pick_rows.1.act_ref, f32[1,1024]{1,0:T(1,128)S(1)} %bitcast.72, bf16[5120,1024]{1,0:T(8,128)(2,1)} %get-tuple-element.40.weight_ref), custom_call_target="tpu_custom_call" | custom-call | flops 2684354560 | bytes 5242880 | tf_op jit(solution)/shard_map/project/pallas_call | solution.py:291
  156.2 8.0 %project.3 = bf16[512,1024]{1,0:T(8,128)(2,1)} custom-call(bf16[512,5120]{1,0:T(8,128)(2,1)} %pick_rows.1.act_ref, f32[1,1024]{1,0:T(1,128)S(1)} %bitcast.73, bf16[5120,1024]{1,0:T(8,128)(2,1)} %get-tuple-element.40.weight_ref, bf16[512,1024]{1,0:T(8,128)(2,1)} %project.2.rest_0_), custom_call_target="tpu_custom_call", output_to_operand_aliasing={{}: (3, {})} | custom-call | flops 2684354560 | bytes 5242880 | tf_op jit(solution)/shard_map/project/pallas_call | solution.py:291
  164.2 4.9 %all-to-all-start.2 = ((bf16[32,16,1024]{2,1,0:T(8,128)(2,1)}), bf16[32,16,1024]{2,1,0:T(8,128)(2,1)S(1)}, u32[]{:S(2)}, u32[]{:S(2)}) async-start(bf16[32,16,1024]{2,1,0:T(8,128)(2,1)} %bitcast.55), calls=%async_computation.2 | async-start | bytes 2097152 | tf_op jit(solution)/shard_map/all_to_all | solution.py:437
  170.3 3.3 %collective-permute-start.21 = (bf16[64,2560]{1,0:T(8,128)(2,1)S(1)}, bf16[64,2560]{1,0:T(8,128)(2,1)S(1)}, u32[]{:S(2)}, u32[]{:S(2)}) collective-permute-start(bf16[64,2560]{1,0:T(8,128)(2,1)S(1)} %slice.85), channel_id=1, source_target_pairs={{0,1},{1,2},{2,3},{3,0},{4,5},{5,6},{6,7},{7,4},{8,9},{9,10},{10,1... | collective-permute-start | bytes 983048 | tf_op jit(solution)/shard_map/ppermute | solution.py:20
  174.4 3.2 %collective-permute-start.18 = (bf16[64,2560]{1,0:T(8,128)(2,1)S(1)}, bf16[64,2560]{1,0:T(8,128)(2,1)S(1)}, u32[]{:S(2)}, u32[]{:S(2)}) collective-permute-start(bf16[64,2560]{1,0:T(8,128)(2,1)S(1)} %get-tuple-element.59), channel_id=1, source_target_pairs={{0,1},{1,2},{2,3},{3,0},{4,5},{5,6},{6,7},{7,4},{8,9},{9,10},{10,1... | collective-permute-start | bytes 983048 | tf_op jit(solution)/shard_map/ppermute | solution.py:20
  178.7 9.3 %collective-permute-done.18 = bf16[64,2560]{1,0:T(8,128)(2,1)S(1)} collective-permute-done((bf16[64,2560]{1,0:T(8,128)(2,1)S(1)}, bf16[64,2560]{1,0:T(8,128)(2,1)S(1)}, u32[]{:S(2)}, u32[]{:S(2)}) %collective-permute-start.18) | collective-permute-done | bytes 327712 | tf_op jit(solution)/shard_map/ppermute | solution.py:20
  188.8 3.7 %collective-permute-start.19 = (bf16[64,2560]{1,0:T(8,128)(2,1)}, bf16[64,2560]{1,0:T(8,128)(2,1)}, u32[]{:S(2)}, u32[]{:S(2)}) collective-permute-start(bf16[64,2560]{1,0:T(8,128)(2,1)} %fusion.11), channel_id=1, source_target_pairs={{0,1},{1,2},{2,3},{3,0},{4,5},{5,6},{6,7},{7,4},{8,9},{9,10},{10,1... | collective-permute-start | bytes 983048 | tf_op jit(solution)/shard_map/ppermute | solution.py:20
  195.8 4.5 %all-to-all-start.3 = ((bf16[4,128,2048]{2,1,0:T(8,128)(2,1)}), bf16[4,128,2048]{2,1,0:T(8,128)(2,1)S(1)}, u32[]{:S(2)}, u32[]{:S(2)}) async-start(bf16[4,128,2048]{2,1,0:T(8,128)(2,1)} %copy-done.1), calls=%async_computation.3 | async-start | bytes 4194304 | tf_op jit(solution)/shard_map/all_to_all | solution.py:460
  201.8 2.9 %fusion.8 = bf16[64,5120]{1,0:T(8,128)(2,1)} fusion(bf16[64,5120]{1,0:T(8,128)(2,1)S(1)} %copy-done.9, f32[64,2560]{1,0:T(8,128)S(1)} %copy-done.10, f32[64,2560]{1,0:T(8,128)S(1)} %convert_add_fusion.1, bf16[4,64,5120]{2,1,0:T(8,128)(2,1)} %bitcast.52, s32[]{:T(128)S(6)} %select_n.891, bf16[4,64,5120]{2,1,0:T(8,128)(2,1)} %bitcast.75), kind=kLoop, calls=%fused_computation.13 | loop fusion | flops 5242880 | bytes 3932164 | tf_op jit(solution)/shard_map/convert_element_type | solution.py:457
  204.7 19.3 %all-to-all-done.3.in_ref = bf16[4,128,2048]{2,1,0:T(8,128)(2,1)S(1)} async-done(((bf16[4,128,2048]{2,1,0:T(8,128)(2,1)}), bf16[4,128,2048]{2,1,0:T(8,128)(2,1)S(1)}, u32[]{:S(2)}, u32[]{:S(2)}) %all-to-all-start.3) | async-done | bytes 2097184 | tf_op jit(solution)/shard_map/all_to_all | solution.py:460
  (157 shorter events, 70.2 us)
Async XLA Ops:
  0.6 14.6 %collective-permute-start = (bf16[160,2048]{1,0:T(8,128)(2,1)}, bf16[160,2048]{1,0:T(8,128)(2,1)}, u32[]{:S(2)}, u32[]{:S(2)}) collective-permute-start(bf16[160,2048]{1,0:T(8,128)(2,1)} %param.8), channel_id=1, source_target_pairs={{0,8},{4,36},{8,16},{12,44},{16,24},{20,52},{24,0},{28,60},{32,40}... | collective-permute-start | bytes 1966088 | tf_op jit(solution)/shard_map/ppermute | solution.py:357
  2.6 17.7 %collective-permute-start.1 = (bf16[160,2048]{1,0:T(8,128)(2,1)}, bf16[160,2048]{1,0:T(8,128)(2,1)}, u32[]{:S(2)}, u32[]{:S(2)}) collective-permute-start(bf16[160,2048]{1,0:T(8,128)(2,1)} %param.8), channel_id=1, source_target_pairs={{0,24},{4,100},{8,0},{12,108},{16,8},{20,116},{24,16},{28,124},{32... | collective-permute-start | bytes 1966088 | tf_op jit(solution)/shard_map/ppermute | solution.py:357
  4.8 17.2 %collective-permute-start.2 = (bf16[160,2048]{1,0:T(8,128)(2,1)}, bf16[160,2048]{1,0:T(8,128)(2,1)S(1)}, u32[]{:S(2)}, u32[]{:S(2)}) collective-permute-start(bf16[160,2048]{1,0:T(8,128)(2,1)} %param.8), channel_id=1, source_target_pairs={{0,16},{4,68},{8,24},{12,76},{16,0},{20,84},{24,8},{28,92},{32,48}... | collective-permute-start | bytes 1966088 | tf_op jit(solution)/shard_map/ppermute | solution.py:357
  9.9 27.7 %all-to-all-start = ((bf16[4,128,2048]{2,1,0:T(8,128)(2,1)}), bf16[4,128,2048]{2,1,0:T(8,128)(2,1)S(1)}, u32[]{:S(2)}, u32[]{:S(2)}) async-start(bf16[4,128,2048]{2,1,0:T(8,128)(2,1)} %copy-done), calls=%async_computation | async-start | bytes 4194304 | tf_op jit(solution)/shard_map/all_to_all | solution.py:328
  25.4 25.7 %collective-permute-start.8 = (bf16[64,5120]{1,0:T(8,128)(2,1)}, bf16[64,5120]{1,0:T(8,128)(2,1)}, u32[]{:S(2)}, u32[]{:S(2)}) collective-permute-start(bf16[64,5120]{1,0:T(8,128)(2,1)} %fusion.3), channel_id=1, source_target_pairs={{0,1},{1,2},{2,3},{3,0},{4,5},{5,6},{6,7},{7,4},{8,9},{9,10},{10,1... | collective-permute-start | bytes 1966088 | tf_op jit(solution)/shard_map/ppermute | solution.py:20
  40.5 37.4 %collective-permute-start.4 = (bf16[640,1024]{1,0:T(8,128)(2,1)S(1)}, bf16[640,1024]{1,0:T(8,128)(2,1)S(1)}, u32[]{:S(2)}, u32[]{:S(2)}) collective-permute-start(bf16[640,1024]{1,0:T(8,128)(2,1)S(1)} %get-tuple-element.23.refs_2_), channel_id=1, source_target_pairs={{0,32},{4,12},{8,40},{12,20},{16,48},{20,28},{24,56},{28,4},{32,64... | collective-permute-start | bytes 3932168 | tf_op jit(solution)/shard_map/ppermute | solution.py:357
  41.2 36.7 %collective-permute-start.6 = (bf16[640,1024]{1,0:T(8,128)(2,1)S(1)}, bf16[640,1024]{1,0:T(8,128)(2,1)S(1)}, u32[]{:S(2)}, u32[]{:S(2)}) collective-permute-start(bf16[640,1024]{1,0:T(8,128)(2,1)S(1)} %get-tuple-element.23.refs_2_), channel_id=1, source_target_pairs={{0,96},{4,28},{8,104},{12,4},{16,112},{20,12},{24,120},{28,20},{32... | collective-permute-start | bytes 3932168 | tf_op jit(solution)/shard_map/ppermute | solution.py:357
  43.7 18.0 %collective-permute-start.9 = (bf16[64,5120]{1,0:T(8,128)(2,1)}, bf16[64,5120]{1,0:T(8,128)(2,1)S(1)}, u32[]{:S(2)}, u32[]{:S(2)}) collective-permute-start(bf16[64,5120]{1,0:T(8,128)(2,1)} %fusion.3), channel_id=1, source_target_pairs={{0,3},{1,0},{2,1},{3,2},{4,7},{5,4},{6,5},{7,6},{8,11},{9,8},{10,9... | collective-permute-start | bytes 1966088 | tf_op jit(solution)/shard_map/ppermute | solution.py:20
  48.2 29.7 %collective-permute-start.5 = (bf16[640,1024]{1,0:T(8,128)(2,1)S(1)}, bf16[640,1024]{1,0:T(8,128)(2,1)S(1)}, u32[]{:S(2)}, u32[]{:S(2)}) collective-permute-start(bf16[640,1024]{1,0:T(8,128)(2,1)S(1)} %copy-done.30), channel_id=1, source_target_pairs={{0,8},{4,36},{8,16},{12,44},{16,24},{20,52},{24,0},{28,60},{32,40}... | collective-permute-start | bytes 3932168 | tf_op jit(solution)/shard_map/ppermute | solution.py:357
  51.1 27.8 %collective-permute-start.7 = (bf16[640,1024]{1,0:T(8,128)(2,1)S(1)}, bf16[640,1024]{1,0:T(8,128)(2,1)S(1)}, u32[]{:S(2)}, u32[]{:S(2)}) collective-permute-start(bf16[640,1024]{1,0:T(8,128)(2,1)S(1)} %copy-done.30), channel_id=1, source_target_pairs={{0,24},{4,100},{8,0},{12,108},{16,8},{20,116},{24,16},{28,124},{32... | collective-permute-start | bytes 3932168 | tf_op jit(solution)/shard_map/ppermute | solution.py:357
  81.1 37.4 %collective-permute-start.16 = (bf16[256,5120]{1,0:T(8,128)(2,1)}, bf16[256,5120]{1,0:T(8,128)(2,1)}, u32[]{:S(2)}, u32[]{:S(2)}) collective-permute-start(bf16[256,5120]{1,0:T(8,128)(2,1)} %constant_dynamic-update-slice_fusion.4.own_ref), channel_id=1, source_target_pairs={{0,4},{4,0},{1,5},{5,1},{2,6},{6,2},{3,7},{7,3},{8,12},{12,8},{9,1... | collective-permute-start | bytes 7864328 | tf_op jit(solution)/shard_map/ppermute | solution.py:20
  82.9 21.9 %all-to-all-start.1 = ((bf16[32,16,1024]{2,1,0:T(8,128)(2,1)}), bf16[32,16,1024]{2,1,0:T(8,128)(2,1)S(1)}, u32[]{:S(2)}, u32[]{:S(2)}) async-start(bf16[32,16,1024]{2,1,0:T(8,128)(2,1)} %bitcast.45), calls=%async_computation.1 | async-start | bytes 2097152 | tf_op jit(solution)/shard_map/all_to_all | solution.py:411
  90.2 26.7 %collective-permute-start.12 = (bf16[320,1024]{1,0:T(8,128)(2,1)}, bf16[320,1024]{1,0:T(8,128)(2,1)S(1)}, u32[]{:S(2)}, u32[]{:S(2)}) collective-permute-start(bf16[320,1024]{1,0:T(8,128)(2,1)} %slice.60), channel_id=1, source_target_pairs={{0,32},{4,12},{8,40},{12,20},{16,48},{20,28},{24,56},{28,4},{32,64... | collective-permute-start | bytes 1966088 | tf_op jit(solution)/shard_map/ppermute | solution.py:357
  92.9 24.9 %collective-permute-start.13 = (bf16[320,1024]{1,0:T(8,128)(2,1)}, bf16[320,1024]{1,0:T(8,128)(2,1)}, u32[]{:S(2)}, u32[]{:S(2)}) collective-permute-start(bf16[320,1024]{1,0:T(8,128)(2,1)} %slice.61), channel_id=1, source_target_pairs={{0,96},{4,28},{8,104},{12,4},{16,112},{20,12},{24,120},{28,20},{32... | collective-permute-start | bytes 1966088 | tf_op jit(solution)/shard_map/ppermute | solution.py:357
  95.3 22.5 %collective-permute-start.14 = (bf16[320,1024]{1,0:T(8,128)(2,1)}, bf16[320,1024]{1,0:T(8,128)(2,1)}, u32[]{:S(2)}, u32[]{:S(2)}) collective-permute-start(bf16[320,1024]{1,0:T(8,128)(2,1)} %slice.62), channel_id=1, source_target_pairs={{0,8},{4,36},{8,16},{12,44},{16,24},{20,52},{24,0},{28,60},{32,40}... | collective-permute-start | bytes 1966088 | tf_op jit(solution)/shard_map/ppermute | solution.py:357
  97.9 19.9 %collective-permute-start.15 = (bf16[320,1024]{1,0:T(8,128)(2,1)}, bf16[320,1024]{1,0:T(8,128)(2,1)}, u32[]{:S(2)}, u32[]{:S(2)}) collective-permute-start(bf16[320,1024]{1,0:T(8,128)(2,1)} %slice.63), channel_id=1, source_target_pairs={{0,24},{4,100},{8,0},{12,108},{16,8},{20,116},{24,16},{28,124},{32... | collective-permute-start | bytes 1966088 | tf_op jit(solution)/shard_map/ppermute | solution.py:357
  148.1 29.5 %collective-permute-start.22 = (bf16[64,2560]{1,0:T(8,128)(2,1)S(1)}, bf16[64,2560]{1,0:T(8,128)(2,1)}, u32[]{:S(2)}, u32[]{:S(2)}) collective-permute-start(bf16[64,2560]{1,0:T(8,128)(2,1)S(1)} %get-tuple-element.60), channel_id=1, source_target_pairs={{0,3},{1,0},{2,1},{3,2},{4,7},{5,4},{6,5},{7,6},{8,11},{9,8},{10,9... | collective-permute-start | bytes 983048 | tf_op jit(solution)/shard_map/ppermute | solution.py:20
  164.2 29.2 %all-to-all-start.2 = ((bf16[32,16,1024]{2,1,0:T(8,128)(2,1)}), bf16[32,16,1024]{2,1,0:T(8,128)(2,1)S(1)}, u32[]{:S(2)}, u32[]{:S(2)}) async-start(bf16[32,16,1024]{2,1,0:T(8,128)(2,1)} %bitcast.55), calls=%async_computation.2 | async-start | bytes 2097152 | tf_op jit(solution)/shard_map/all_to_all | solution.py:437
  170.3 22.2 %collective-permute-start.21 = (bf16[64,2560]{1,0:T(8,128)(2,1)S(1)}, bf16[64,2560]{1,0:T(8,128)(2,1)S(1)}, u32[]{:S(2)}, u32[]{:S(2)}) collective-permute-start(bf16[64,2560]{1,0:T(8,128)(2,1)S(1)} %slice.85), channel_id=1, source_target_pairs={{0,1},{1,2},{2,3},{3,0},{4,5},{5,6},{6,7},{7,4},{8,9},{9,10},{10,1... | collective-permute-start | bytes 983048 | tf_op jit(solution)/shard_map/ppermute | solution.py:20
  174.4 26.0 %collective-permute-start.20 = (bf16[64,2560]{1,0:T(8,128)(2,1)}, bf16[64,2560]{1,0:T(8,128)(2,1)}, u32[]{:S(2)}, u32[]{:S(2)}) collective-permute-start(bf16[64,2560]{1,0:T(8,128)(2,1)} %slice.86), channel_id=1, source_target_pairs={{0,3},{1,0},{2,1},{3,2},{4,7},{5,4},{6,5},{7,6},{8,11},{9,8},{10,9... | collective-permute-start | bytes 983048 | tf_op jit(solution)/shard_map/ppermute | solution.py:20
  174.4 13.7 %collective-permute-start.18 = (bf16[64,2560]{1,0:T(8,128)(2,1)S(1)}, bf16[64,2560]{1,0:T(8,128)(2,1)S(1)}, u32[]{:S(2)}, u32[]{:S(2)}) collective-permute-start(bf16[64,2560]{1,0:T(8,128)(2,1)S(1)} %get-tuple-element.59), channel_id=1, source_target_pairs={{0,1},{1,2},{2,3},{3,0},{4,5},{5,6},{6,7},{7,4},{8,9},{9,10},{10,1... | collective-permute-start | bytes 983048 | tf_op jit(solution)/shard_map/ppermute | solution.py:20
  178.6 13.9 %collective-permute-start.23 = (bf16[64,2560]{1,0:T(8,128)(2,1)S(1)}, bf16[64,2560]{1,0:T(8,128)(2,1)S(1)}, u32[]{:S(2)}, u32[]{:S(2)}) collective-permute-start(bf16[64,2560]{1,0:T(8,128)(2,1)S(1)} %fusion.10), channel_id=1, source_target_pairs={{0,3},{1,0},{2,1},{3,2},{4,7},{5,4},{6,5},{7,6},{8,11},{9,8},{10,9... | collective-permute-start | bytes 983048 | tf_op jit(solution)/shard_map/ppermute | solution.py:20
  188.8 11.6 %collective-permute-start.19 = (bf16[64,2560]{1,0:T(8,128)(2,1)}, bf16[64,2560]{1,0:T(8,128)(2,1)}, u32[]{:S(2)}, u32[]{:S(2)}) collective-permute-start(bf16[64,2560]{1,0:T(8,128)(2,1)} %fusion.11), channel_id=1, source_target_pairs={{0,1},{1,2},{2,3},{3,0},{4,5},{5,6},{6,7},{7,4},{8,9},{9,10},{10,1... | collective-permute-start | bytes 983048 | tf_op jit(solution)/shard_map/ppermute | solution.py:20
  195.8 28.1 %all-to-all-start.3 = ((bf16[4,128,2048]{2,1,0:T(8,128)(2,1)}), bf16[4,128,2048]{2,1,0:T(8,128)(2,1)S(1)}, u32[]{:S(2)}, u32[]{:S(2)}) async-start(bf16[4,128,2048]{2,1,0:T(8,128)(2,1)} %copy-done.1), calls=%async_computation.3 | async-start | bytes 4194304 | tf_op jit(solution)/shard_map/all_to_all | solution.py:460
  (35 other events, 176.5 us)

commit v5 on v3

--- a/solution.py
+++ b/solution.py
@@ -356,12 +356,12 @@
     line = jnp.concatenate([proj_weight] + [cross(proj_weight, True, d) for d in (1, -1, 2)])
     mine = lax.dynamic_slice_in_dim(line, ic * half, half, 1)
     theirs = shift(lax.dynamic_slice_in_dim(line, (1 - ic) * half, half, 1), CORE, 1)
-    lines = list(tie(mine, theirs, columns, activated))
-    columns, activated = lines[2:]
     right, left = shift(activated, X, 1), shift(activated, X, -1)
+    lines = list(tie(mine, theirs, right, left))
+    right, left = lines[2:]
     plus = [cross(lines[0], False, 1), cross(lines[1], True, 1)]
     minus = [cross(lines[0], False, -1), cross(lines[1], True, -1)]
-    plus[0], plus[1], minus[0], minus[1] = tie(*plus, *minus)
+    plus[0], plus[1], minus[0], minus[1], columns = tie(*plus, *minus, columns)
     middle = 2 * krows
     far = [
         (
@@ -393,8 +393,8 @@
             activated,
             right,
             left,
-            shift(tie(right, send_box)[0][: own_rows // 2], X, 1),
-            shift(tie(left, send_box)[0][own_rows // 2 :], X, -1),
+            shift(right[: own_rows // 2], X, 1),
+            shift(left[own_rows // 2 :], X, -1),
         ]
     )
     away_by = (row_of // own_rows - ix) % nx
@@ -406,13 +406,13 @@
     returned = lax.all_to_all(
         send_box.reshape(groups, nc * MAXTOK, half), VDP, split_axis=0, concat_axis=0, tiled=True
     )
-    returned = tie(returned, *far[0], *far[1])[0]
-    row_grad = unpick_rows(row_of[None, :], returned.reshape(n_slots, half), nc * total_rows)
 
     other = shift(everyone, CORE, 1)
     act_slots = pick_rows(act_row[:, None], everyone, other, hidden // 4)
 
     bias = lax.dynamic_slice_in_dim(proj_bias, ic * half, half, 0).astype(jnp.float32)[None, :]
+    returned, act_slots = tie(returned, act_slots, *far[0], *far[1])[:2]
+    row_grad = unpick_rows(row_of[None, :], returned.reshape(n_slots, half), nc * total_rows)
     kept_sum, away, weight = project_back(places, row_grad, pieces, krows, hidden)
     received = shift(away, CORE, 1).reshape(nx, own_rows, hidden)
     kept_sum = kept_sum.reshape(nx, own_rows, hidden)

time: 216 us -> 262 us (1.21); the launches traced: 212 us -> 261 us
  waiting for transfers between devices: 69.2 us -> 124 us
  other arithmetic: 16.8 us -> 12.8 us
    ppermute x13, waiting for transfers between devices: 31.6 us -> 69.3 us  [shift(): lax.ppermute(value, axis, [(i, (i + by) % size) for i in range(size)])]
    ppermute x11, waiting for transfers between devices: 22.8 us -> 43.3 us  [cross(): return lax.ppermute(value, VDP, pairs)]
    all_to_all x1, waiting for transfers between devices: 10.4 us -> 0.01 us  [local(): lax.all_to_all(split_columns(embed_grad, nx), X, split_axis=0, concat_axi...]
    all_to_all x1, waiting for transfers between devices: 4.31 us -> 11.2 us  [local(): lax.all_to_all(projected.reshape(groups, nc * MAXTOK, half), VDP, split_a...]
    unnamed x37 -> x60, local copies, waits for them, and re-layouts: 13.3 us -> 12.9 us
  transfers between devices with their start and end apart: 28 -> 28, of which waited for: 11 -> 13; matrix products, arithmetic and copies ran while one was open for 20% -> 12% of each run, Pallas kernels for 18% -> 9%
where the time goes in v5:
time: 262 us; the launch traced here: 261 us
  waiting for transfers between devices  124 us (47%)
  starting transfers between devices  55.2 us (21%)
  Pallas kernels  39.3 us (15%)
  local copies, waits for them, and re-layouts  28.1 us (11%)
  other arithmetic  12.8 us (5%)
    ppermute x13, waiting for transfers between devices, shift(): lax.ppermute(value, axis, [(i, (i + by) % size) for i in range(size)])  69.3 us
    ppermute x11, waiting for transfers between devices, cross(): return lax.ppermute(value, VDP, pairs)  43.3 us
    ppermute x11, starting transfers between devices, cross(): return lax.ppermute(value, VDP, pairs)  19.6 us
    pallas_call x1, Pallas kernels, project(): pl.pallas_call(body, grid=(k // tile,), in_specs=[pl.BlockSpec((n, tile),...  13.8 us
    pallas_call x1, Pallas kernels, project_back(): pl.pallas_call(body, in_specs=[pl.BlockSpec(memory_space=pltpu.SMEM), vme...  13 us
    unnamed x60, local copies, waits for them, and re-layouts  12.9 us
    ppermute x13, starting transfers between devices, shift(): lax.ppermute(value, axis, [(i, (i + by) % size) for i in range(size)])  12.6 us
    all_to_all x1, waiting for transfers between devices, local(): lax.all_to_all(projected.reshape(groups, nc * MAXTOK, half), VDP, split_a...  11.2 us
  transfers between devices with their start and end apart: 28, of which 13 were waited for; matrix products, arithmetic and copies ran while one was open for 12% of the time, Pallas kernels for 9%

profile of v5, /device:TPU:6, one launch (start us, length us, event | category | flops | bytes accessed | tf_op | source)
XLA Modules:
  0.0 261.0 jit_solution(14473516010136134695)
XLA Ops:
  0.6 2.0 collective-permute-start
  2.6 2.2 collective-permute-start.1
  7.8 5.7 %collective-permute-done = bf16[160,2048]{1,0:T(8,128)(2,1)S(1)} collective-permute-done((bf16[160,2048]{1,0:T(8,128)(2,1)}, bf16[160,2048]{1,0:T(8,128)(2,1)S(1)}, u32[]{:S(2)}, u32[]{:S(2)}) %collective-permute-start) | collective-permute-done | bytes 655392 | tf_op jit(solution)/shard_map/ppermute | solution.py:353
  13.6 6.7 %collective-permute-done.1 = bf16[160,2048]{1,0:T(8,128)(2,1)S(1)} collective-permute-done((bf16[160,2048]{1,0:T(8,128)(2,1)}, bf16[160,2048]{1,0:T(8,128)(2,1)S(1)}, u32[]{:S(2)}, u32[]{:S(2)}) %collective-permute-start.1) | collective-permute-done | bytes 655392 | tf_op jit(solution)/shard_map/ppermute | solution.py:353
  28.5 5.4 %all-to-all-start = ((bf16[4,128,2048]{2,1,0:T(8,128)(2,1)}), bf16[4,128,2048]{2,1,0:T(8,128)(2,1)S(1)}, u32[]{:S(2)}, u32[]{:S(2)}) async-start(bf16[4,128,2048]{2,1,0:T(8,128)(2,1)} %copy-done), calls=%async_computation | async-start | bytes 4194304 | tf_op jit(solution)/shard_map/all_to_all | solution.py:324
  34.0 8.7 %collective-permute-done.4 = bf16[64,5120]{1,0:T(8,128)(2,1)} collective-permute-done((bf16[64,5120]{1,0:T(8,128)(2,1)}, bf16[64,5120]{1,0:T(8,128)(2,1)}, u32[]{:S(2)}, u32[]{:S(2)}) %collective-permute-start.4) | collective-permute-done | bytes 655392 | tf_op jit(solution)/shard_map/ppermute | solution.py:20
  45.4 2.0 constant_dynamic-update-slice_fusion.7
  50.4 2.0 constant_dynamic-update-slice_fusion.6
  52.4 19.3 %collective-permute-done.10 = bf16[32,5120]{1,0:T(8,128)(2,1)S(1)} collective-permute-done((bf16[32,5120]{1,0:T(8,128)(2,1)S(1)}, bf16[32,5120]{1,0:T(8,128)(2,1)S(1)}, u32[]{:S(2)}, u32[]{:S(2)}) %collective-permute-start.10) | collective-permute-done | bytes 327712 | tf_op jit(solution)/shard_map/ppermute | solution.py:20
  87.9 17.2 %collective-permute-done.6.refs_3_ = bf16[640,1024]{1,0:T(8,128)(2,1)} collective-permute-done((bf16[640,1024]{1,0:T(8,128)(2,1)S(1)}, bf16[640,1024]{1,0:T(8,128)(2,1)}, u32[]{:S(2)}, u32[]{:S(2)}) %collective-permute-start.6) | collective-permute-done | bytes 1310752 | tf_op jit(solution)/shard_map/ppermute | solution.py:353
  105.2 2.1 collective-permute-done.7.refs_8_
  110.1 7.4 %all-to-all-start.1 = ((bf16[32,16,1024]{2,1,0:T(8,128)(2,1)}), bf16[32,16,1024]{2,1,0:T(8,128)(2,1)S(1)}, u32[]{:S(2)}, u32[]{:S(2)}) async-start(bf16[32,16,1024]{2,1,0:T(8,128)(2,1)} %bitcast.5), calls=%async_computation.1 | async-start | bytes 2097152 | tf_op jit(solution)/shard_map/all_to_all | solution.py:406
  130.5 6.6 %pick_rows.1.act_ref = bf16[512,5120]{1,0:T(8,128)(2,1)} custom-call(s32[512,1]{1,0:T(8,128)S(1)} %get-tuple-element.54.index_ref, bf16[256,5120]{1,0:T(8,128)(2,1)S(1)} %copy-done.2, bf16[256,5120]{1,0:T(8,128)(2,1)} %collective-permute-done.12.other_ref), custom_call_target="tpu_custom_call" | custom-call | flops 2684354560 | bytes 10485760 | tf_op jit(solution)/shard_map/pick_rows/pallas_call | solution.py:173
  137.1 9.9 %collective-permute-done.13.refs_5_ = bf16[320,1024]{1,0:T(8,128)(2,1)S(1)} collective-permute-done((bf16[320,1024]{1,0:T(8,128)(2,1)S(1)}, bf16[320,1024]{1,0:T(8,128)(2,1)S(1)}, u32[]{:S(2)}, u32[]{:S(2)}) %collective-permute-start.13) | collective-permute-done | bytes 655392 | tf_op jit(solution)/shard_map/ppermute | solution.py:353
  151.0 13.0 %project_back.1 = (bf16[256,5120]{1,0:T(8,128)(2,1)}, bf16[256,5120]{1,0:T(8,128)(2,1)}, bf16[5120,1024]{1,0:T(8,128)(2,1)}) custom-call(s32[32]{0:T(128)S(1)} %stack.137.refs_0_, bf16[512,1024]{1,0:T(8,128)(2,1)S(1)} %unpick_rows.1.refs_1_, bf16[640,1024]{1,0:T(8,128)(2,1)S(1)} %get-tuple-element.18.refs_2_, ...), custom_call_target="tpu_custom_call" | custom-call | flops 5368709120 | bytes 31457280 | tf_op jit(solution)/shard_map/project_back/pallas_call | solution.py:247
  164.2 13.8 %project.1 = bf16[512,1024]{1,0:T(8,128)(2,1)} custom-call(bf16[512,5120]{1,0:T(8,128)(2,1)} %pick_rows.1.act_ref, f32[1,1024]{1,0:T(1,128)S(1)} %bitcast.72, bf16[5120,1024]{1,0:T(8,128)(2,1)} %get-tuple-element.29.weight_ref), custom_call_target="tpu_custom_call" | custom-call | flops 5368709120 | bytes 10485760 | tf_op jit(solution)/shard_map/project/pallas_call | solution.py:289
  178.0 5.6 %all-to-all-start.2 = ((bf16[32,16,1024]{2,1,0:T(8,128)(2,1)}), bf16[32,16,1024]{2,1,0:T(8,128)(2,1)S(1)}, u32[]{:S(2)}, u32[]{:S(2)}) async-start(bf16[32,16,1024]{2,1,0:T(8,128)(2,1)} %bitcast.52), calls=%async_computation.2 | async-start | bytes 2097152 | tf_op jit(solution)/shard_map/all_to_all | solution.py:420
  183.6 3.7 %add_bitcast_fusion.1 = (f32[64,5120]{1,0:T(8,128)}, f32[64,5120]{1,0:T(8,128)S(1)}, bf16[64,5120]{1,0:T(8,128)(2,1)S(1)}) fusion(bf16[4,64,5120]{2,1,0:T(8,128)(2,1)} %bitcast.55, s32[]{:T(128)S(6)} %select_n.882, bf16[4,64,5120]{2,1,0:T(8,128)(2,1)} %bitcast.73, s32[]{:T(128)S(6)} %select_n.886, s32[]{:T(128)S(6)} %select_n.884), kind=kLoop, calls=%fused_computation.17 | loop fusion | flops 3276800 | bytes 7208972 | tf_op jit(solution)/shard_map/add | solution.py:428
  189.2 11.2 %all-to-all-done.2 = bf16[32,16,1024]{2,1,0:T(8,128)(2,1)S(1)} async-done(((bf16[32,16,1024]{2,1,0:T(8,128)(2,1)}), bf16[32,16,1024]{2,1,0:T(8,128)(2,1)S(1)}, u32[]{:S(2)}, u32[]{:S(2)}) %all-to-all-start.2) | async-done | bytes 1048608 | tf_op jit(solution)/shard_map/all_to_all | solution.py:420
  202.8 4.6 %all-to-all-start.3 = ((bf16[4,128,2048]{2,1,0:T(8,128)(2,1)}), bf16[4,128,2048]{2,1,0:T(8,128)(2,1)S(1)}, u32[]{:S(2)}, u32[]{:S(2)}) async-start(bf16[4,128,2048]{2,1,0:T(8,128)(2,1)} %copy-done.1), calls=%async_computation.3 | async-start | bytes 4194304 | tf_op jit(solution)/shard_map/all_to_all | solution.py:451
  210.1 2.8 %collective-permute-start.21 = (bf16[64,2560]{1,0:T(8,128)(2,1)S(1)}, bf16[64,2560]{1,0:T(8,128)(2,1)S(1)}, u32[]{:S(2)}, u32[]{:S(2)}) collective-permute-start(bf16[64,2560]{1,0:T(8,128)(2,1)S(1)} %slice.87), channel_id=1, source_target_pairs={{0,1},{1,2},{2,3},{3,0},{4,5},{5,6},{6,7},{7,4},{8,9},{9,10},{10,1... | collective-permute-start | bytes 983048 | tf_op jit(solution)/shard_map/ppermute | solution.py:20
  215.1 30.3 %collective-permute-done.22 = bf16[64,2560]{1,0:T(8,128)(2,1)S(1)} collective-permute-done((bf16[64,2560]{1,0:T(8,128)(2,1)}, bf16[64,2560]{1,0:T(8,128)(2,1)S(1)}, u32[]{:S(2)}, u32[]{:S(2)}) %collective-permute-start.22) | collective-permute-done | bytes 327712 | tf_op jit(solution)/shard_map/ppermute | solution.py:20
  247.4 8.7 %collective-permute-done.23 = bf16[64,2560]{1,0:T(8,128)(2,1)S(1)} collective-permute-done((bf16[64,2560]{1,0:T(8,128)(2,1)S(1)}, bf16[64,2560]{1,0:T(8,128)(2,1)S(1)}, u32[]{:S(2)}, u32[]{:S(2)}) %collective-permute-start.23) | collective-permute-done | bytes 327712 | tf_op jit(solution)/shard_map/ppermute | solution.py:20
  256.3 2.9 %fusion.8 = bf16[64,5120]{1,0:T(8,128)(2,1)} fusion(bf16[64,5120]{1,0:T(8,128)(2,1)S(1)} %copy-done.13, f32[64,2560]{1,0:T(8,128)S(1)} %convert_add_fusion, f32[64,2560]{1,0:T(8,128)S(1)} %convert_add_fusion.1, bf16[4,64,5120]{2,1,0:T(8,128)(2,1)} %bitcast.55, s32[]{:T(128)S(6)} %select_n.880, bf16[4,64,5120]{2,1,0:T(8,128)(2,1)} %bitcast.74), kind=kLoop, calls=%fused_computation.13 | loop fusion | flops 5242880 | bytes 3932164 | tf_op jit(solution)/shard_map/convert_element_type | solution.py:448
  (147 shorter events, 65.5 us)
Async XLA Ops:
  23.4 21.0 %collective-permute-start.3 = (bf16[640,1024]{1,0:T(8,128)(2,1)}, bf16[640,1024]{1,0:T(8,128)(2,1)}, u32[]{:S(2)}, u32[]{:S(2)}) collective-permute-start(bf16[640,1024]{1,0:T(8,128)(2,1)} %get-tuple-element.49), channel_id=1, source_target_pairs={{0,4},{4,0},{1,5},{5,1},{2,6},{6,2},{3,7},{7,3},{8,12},{12,8},{9,1... | collective-permute-start | bytes 3932168 | tf_op jit(solution)/shard_map/ppermute | solution.py:20
  24.8 17.8 %collective-permute-start.4 = (bf16[64,5120]{1,0:T(8,128)(2,1)}, bf16[64,5120]{1,0:T(8,128)(2,1)}, u32[]{:S(2)}, u32[]{:S(2)}) collective-permute-start(bf16[64,5120]{1,0:T(8,128)(2,1)} %get-tuple-element.45), channel_id=1, source_target_pairs={{0,1},{1,2},{2,3},{3,0},{4,5},{5,6},{6,7},{7,4},{8,9},{9,10},{10,1... | collective-permute-start | bytes 1966088 | tf_op jit(solution)/shard_map/ppermute | solution.py:20
  25.3 19.1 %collective-permute-start.5 = (bf16[64,5120]{1,0:T(8,128)(2,1)}, bf16[64,5120]{1,0:T(8,128)(2,1)}, u32[]{:S(2)}, u32[]{:S(2)}) collective-permute-start(bf16[64,5120]{1,0:T(8,128)(2,1)} %get-tuple-element.45), channel_id=1, source_target_pairs={{0,3},{1,0},{2,1},{3,2},{4,7},{5,4},{6,5},{7,6},{8,11},{9,8},{10,9... | collective-permute-start | bytes 1966088 | tf_op jit(solution)/shard_map/ppermute | solution.py:20
  28.5 59.4 %all-to-all-start = ((bf16[4,128,2048]{2,1,0:T(8,128)(2,1)}), bf16[4,128,2048]{2,1,0:T(8,128)(2,1)S(1)}, u32[]{:S(2)}, u32[]{:S(2)}) async-start(bf16[4,128,2048]{2,1,0:T(8,128)(2,1)} %copy-done), calls=%async_computation | async-start | bytes 4194304 | tf_op jit(solution)/shard_map/all_to_all | solution.py:324
  47.3 24.4 %collective-permute-start.10 = (bf16[32,5120]{1,0:T(8,128)(2,1)S(1)}, bf16[32,5120]{1,0:T(8,128)(2,1)S(1)}, u32[]{:S(2)}, u32[]{:S(2)}) collective-permute-start(bf16[32,5120]{1,0:T(8,128)(2,1)S(1)} %slice.58), channel_id=1, source_target_pairs={{0,1},{1,2},{2,3},{3,0},{4,5},{5,6},{6,7},{7,4},{8,9},{9,10},{10,1... | collective-permute-start | bytes 983048 | tf_op jit(solution)/shard_map/ppermute | solution.py:20
  48.6 24.4 %collective-permute-start.11 = (bf16[32,5120]{1,0:T(8,128)(2,1)S(1)}, bf16[32,5120]{1,0:T(8,128)(2,1)S(1)}, u32[]{:S(2)}, u32[]{:S(2)}) collective-permute-start(bf16[32,5120]{1,0:T(8,128)(2,1)S(1)} %slice.59), channel_id=1, source_target_pairs={{0,3},{1,0},{2,1},{3,2},{4,7},{5,4},{6,5},{7,6},{8,11},{9,8},{10,9... | collective-permute-start | bytes 983048 | tf_op jit(solution)/shard_map/ppermute | solution.py:20
  73.8 56.6 %collective-permute-start.12 = (bf16[256,5120]{1,0:T(8,128)(2,1)}, bf16[256,5120]{1,0:T(8,128)(2,1)}, u32[]{:S(2)}, u32[]{:S(2)}) collective-permute-start(bf16[256,5120]{1,0:T(8,128)(2,1)} %constant_dynamic-update-slice_fusion.4.own_ref), channel_id=1, source_target_pairs={{0,4},{4,0},{1,5},{5,1},{2,6},{6,2},{3,7},{7,3},{8,12},{12,8},{9,1... | collective-permute-start | bytes 7864328 | tf_op jit(solution)/shard_map/ppermute | solution.py:20
  74.7 30.5 %collective-permute-start.6 = (bf16[640,1024]{1,0:T(8,128)(2,1)S(1)}, bf16[640,1024]{1,0:T(8,128)(2,1)}, u32[]{:S(2)}, u32[]{:S(2)}) collective-permute-start(bf16[640,1024]{1,0:T(8,128)(2,1)S(1)} %get-tuple-element.18.refs_2_), channel_id=1, source_target_pairs={{0,32},{4,12},{8,40},{12,20},{16,48},{20,28},{24,56},{28,4},{32,64... | collective-permute-start | bytes 3932168 | tf_op jit(solution)/shard_map/ppermute | solution.py:353
  76.3 30.9 %collective-permute-start.8 = (bf16[640,1024]{1,0:T(8,128)(2,1)S(1)}, bf16[640,1024]{1,0:T(8,128)(2,1)}, u32[]{:S(2)}, u32[]{:S(2)}) collective-permute-start(bf16[640,1024]{1,0:T(8,128)(2,1)S(1)} %get-tuple-element.18.refs_2_), channel_id=1, source_target_pairs={{0,96},{4,28},{8,104},{12,4},{16,112},{20,12},{24,120},{28,20},{32... | collective-permute-start | bytes 3932168 | tf_op jit(solution)/shard_map/ppermute | solution.py:353
  78.0 29.3 %collective-permute-start.7 = (bf16[640,1024]{1,0:T(8,128)(2,1)}, bf16[640,1024]{1,0:T(8,128)(2,1)}, u32[]{:S(2)}, u32[]{:S(2)}) collective-permute-start(bf16[640,1024]{1,0:T(8,128)(2,1)} %collective-permute-done.3.refs_7_), channel_id=1, source_target_pairs={{0,8},{4,36},{8,16},{12,44},{16,24},{20,52},{24,0},{28,60},{32,40}... | collective-permute-start | bytes 3932168 | tf_op jit(solution)/shard_map/ppermute | solution.py:353
  79.4 27.8 %collective-permute-start.9 = (bf16[640,1024]{1,0:T(8,128)(2,1)}, bf16[640,1024]{1,0:T(8,128)(2,1)}, u32[]{:S(2)}, u32[]{:S(2)}) collective-permute-start(bf16[640,1024]{1,0:T(8,128)(2,1)} %collective-permute-done.3.refs_7_), channel_id=1, source_target_pairs={{0,24},{4,100},{8,0},{12,108},{16,8},{20,116},{24,16},{28,124},{32... | collective-permute-start | bytes 3932168 | tf_op jit(solution)/shard_map/ppermute | solution.py:353
  110.1 39.4 %all-to-all-start.1 = ((bf16[32,16,1024]{2,1,0:T(8,128)(2,1)}), bf16[32,16,1024]{2,1,0:T(8,128)(2,1)S(1)}, u32[]{:S(2)}, u32[]{:S(2)}) async-start(bf16[32,16,1024]{2,1,0:T(8,128)(2,1)} %bitcast.5), calls=%async_computation.1 | async-start | bytes 2097152 | tf_op jit(solution)/shard_map/all_to_all | solution.py:406
  119.2 27.8 %collective-permute-start.13 = (bf16[320,1024]{1,0:T(8,128)(2,1)S(1)}, bf16[320,1024]{1,0:T(8,128)(2,1)S(1)}, u32[]{:S(2)}, u32[]{:S(2)}) collective-permute-start(bf16[320,1024]{1,0:T(8,128)(2,1)S(1)} %slice.60), channel_id=1, source_target_pairs={{0,32},{4,12},{8,40},{12,20},{16,48},{20,28},{24,56},{28,4},{32,64... | collective-permute-start | bytes 1966088 | tf_op jit(solution)/shard_map/ppermute | solution.py:353
  122.2 24.8 %collective-permute-start.14 = (bf16[320,1024]{1,0:T(8,128)(2,1)S(1)}, bf16[320,1024]{1,0:T(8,128)(2,1)S(1)}, u32[]{:S(2)}, u32[]{:S(2)}) collective-permute-start(bf16[320,1024]{1,0:T(8,128)(2,1)S(1)} %slice.61), channel_id=1, source_target_pairs={{0,96},{4,28},{8,104},{12,4},{16,112},{20,12},{24,120},{28,20},{32... | collective-permute-start | bytes 1966088 | tf_op jit(solution)/shard_map/ppermute | solution.py:353
  124.8 22.9 %collective-permute-start.15 = (bf16[320,1024]{1,0:T(8,128)(2,1)S(1)}, bf16[320,1024]{1,0:T(8,128)(2,1)S(1)}, u32[]{:S(2)}, u32[]{:S(2)}) collective-permute-start(bf16[320,1024]{1,0:T(8,128)(2,1)S(1)} %slice.62), channel_id=1, source_target_pairs={{0,8},{4,36},{8,16},{12,44},{16,24},{20,52},{24,0},{28,60},{32,40}... | collective-permute-start | bytes 1966088 | tf_op jit(solution)/shard_map/ppermute | solution.py:353
  127.8 20.8 %collective-permute-start.16 = (bf16[320,1024]{1,0:T(8,128)(2,1)S(1)}, bf16[320,1024]{1,0:T(8,128)(2,1)S(1)}, u32[]{:S(2)}, u32[]{:S(2)}) collective-permute-start(bf16[320,1024]{1,0:T(8,128)(2,1)S(1)} %slice.63), channel_id=1, source_target_pairs={{0,24},{4,100},{8,0},{12,108},{16,8},{20,116},{24,16},{28,124},{32... | collective-permute-start | bytes 1966088 | tf_op jit(solution)/shard_map/ppermute | solution.py:353
  164.0 19.6 %collective-permute-start.17 = (bf16[256,5120]{1,0:T(8,128)(2,1)}, bf16[256,5120]{1,0:T(8,128)(2,1)}, u32[]{:S(2)}, u32[]{:S(2)}) collective-permute-start(bf16[256,5120]{1,0:T(8,128)(2,1)} %get-tuple-element.31), channel_id=1, source_target_pairs={{0,4},{4,0},{1,5},{5,1},{2,6},{6,2},{3,7},{7,3},{8,12},{12,8},{9,1... | collective-permute-start | bytes 7864328 | tf_op jit(solution)/shard_map/ppermute | solution.py:20
  178.0 22.4 %all-to-all-start.2 = ((bf16[32,16,1024]{2,1,0:T(8,128)(2,1)}), bf16[32,16,1024]{2,1,0:T(8,128)(2,1)S(1)}, u32[]{:S(2)}, u32[]{:S(2)}) async-start(bf16[32,16,1024]{2,1,0:T(8,128)(2,1)} %bitcast.52), calls=%async_computation.2 | async-start | bytes 2097152 | tf_op jit(solution)/shard_map/all_to_all | solution.py:420
  188.1 24.7 %collective-permute-start.18 = (bf16[64,2560]{1,0:T(8,128)(2,1)}, bf16[64,2560]{1,0:T(8,128)(2,1)}, u32[]{:S(2)}, u32[]{:S(2)}) collective-permute-start(bf16[64,2560]{1,0:T(8,128)(2,1)} %get-tuple-element.51), channel_id=1, source_target_pairs={{0,1},{1,2},{2,3},{3,0},{4,5},{5,6},{6,7},{7,4},{8,9},{9,10},{10,1... | collective-permute-start | bytes 983048 | tf_op jit(solution)/shard_map/ppermute | solution.py:20
  202.8 56.3 %all-to-all-start.3 = ((bf16[4,128,2048]{2,1,0:T(8,128)(2,1)}), bf16[4,128,2048]{2,1,0:T(8,128)(2,1)S(1)}, u32[]{:S(2)}, u32[]{:S(2)}) async-start(bf16[4,128,2048]{2,1,0:T(8,128)(2,1)} %copy-done.1), calls=%async_computation.3 | async-start | bytes 4194304 | tf_op jit(solution)/shard_map/all_to_all | solution.py:451
  207.5 39.8 %collective-permute-start.20 = (bf16[64,2560]{1,0:T(8,128)(2,1)S(1)}, bf16[64,2560]{1,0:T(8,128)(2,1)S(1)}, u32[]{:S(2)}, u32[]{:S(2)}) collective-permute-start(bf16[64,2560]{1,0:T(8,128)(2,1)S(1)} %slice.88), channel_id=1, source_target_pairs={{0,3},{1,0},{2,1},{3,2},{4,7},{5,4},{6,5},{7,6},{8,11},{9,8},{10,9... | collective-permute-start | bytes 983048 | tf_op jit(solution)/shard_map/ppermute | solution.py:20
  208.4 37.0 %collective-permute-start.22 = (bf16[64,2560]{1,0:T(8,128)(2,1)}, bf16[64,2560]{1,0:T(8,128)(2,1)S(1)}, u32[]{:S(2)}, u32[]{:S(2)}) collective-permute-start(bf16[64,2560]{1,0:T(8,128)(2,1)} %get-tuple-element.52), channel_id=1, source_target_pairs={{0,3},{1,0},{2,1},{3,2},{4,7},{5,4},{6,5},{7,6},{8,11},{9,8},{10,9... | collective-permute-start | bytes 983048 | tf_op jit(solution)/shard_map/ppermute | solution.py:20
  210.1 37.3 %collective-permute-start.21 = (bf16[64,2560]{1,0:T(8,128)(2,1)S(1)}, bf16[64,2560]{1,0:T(8,128)(2,1)S(1)}, u32[]{:S(2)}, u32[]{:S(2)}) collective-permute-start(bf16[64,2560]{1,0:T(8,128)(2,1)S(1)} %slice.87), channel_id=1, source_target_pairs={{0,1},{1,2},{2,3},{3,0},{4,5},{5,6},{6,7},{7,4},{8,9},{9,10},{10,1... | collective-permute-start | bytes 983048 | tf_op jit(solution)/shard_map/ppermute | solution.py:20
  213.9 33.4 %collective-permute-start.19 = (bf16[64,2560]{1,0:T(8,128)(2,1)S(1)}, bf16[64,2560]{1,0:T(8,128)(2,1)S(1)}, u32[]{:S(2)}, u32[]{:S(2)}) collective-permute-start(bf16[64,2560]{1,0:T(8,128)(2,1)S(1)} %fusion.11), channel_id=1, source_target_pairs={{0,1},{1,2},{2,3},{3,0},{4,5},{5,6},{6,7},{7,4},{8,9},{9,10},{10,1... | collective-permute-start | bytes 983048 | tf_op jit(solution)/shard_map/ppermute | solution.py:20
  (31 other events, 242.8 us)

commit v6 on v5

--- a/solution.py
+++ b/solution.py
@@ -356,12 +356,22 @@
     line = jnp.concatenate([proj_weight] + [cross(proj_weight, True, d) for d in (1, -1, 2)])
     mine = lax.dynamic_slice_in_dim(line, ic * half, half, 1)
     theirs = shift(lax.dynamic_slice_in_dim(line, (1 - ic) * half, half, 1), CORE, 1)
+    lines = list(tie(mine, theirs, columns, activated))
+    columns, activated = lines[2:]
     right, left = shift(activated, X, 1), shift(activated, X, -1)
-    lines = list(tie(mine, theirs, right, left))
-    right, left = lines[2:]
     plus = [cross(lines[0], False, 1), cross(lines[1], True, 1)]
     minus = [cross(lines[0], False, -1), cross(lines[1], True, -1)]
-    plus[0], plus[1], minus[0], minus[1], columns = tie(*plus, *minus, columns)
+    send_box = gather_spots(spots[:, :, None], columns, ny * nz, nc)
+    everyone = jnp.concatenate(
+        [
+            activated,
+            right,
+            left,
+            shift(tie(right, send_box)[0][: own_rows // 2], X, 1),
+            shift(tie(left, send_box)[0][own_rows // 2 :], X, -1),
+        ]
+    )
+    plus[0], plus[1], minus[0], minus[1], everyone = tie(*plus, *minus, everyone)
     middle = 2 * krows
     far = [
         (
@@ -387,16 +397,6 @@
                 places.append((((iy + dy) % ny * nz + (iz + dz) % nz) * nc + which) * krows)
     places = jnp.stack(places).astype(jnp.int32)
 
-    send_box = gather_spots(spots[:, :, None], columns, ny * nz, nc)
-    everyone = jnp.concatenate(
-        [
-            activated,
-            right,
-            left,
-            shift(right[: own_rows // 2], X, 1),
-            shift(left[own_rows // 2 :], X, -1),
-        ]
-    )
     away_by = (row_of // own_rows - ix) % nx
     seat = jnp.where(away_by == nx - 1, 1, jnp.where(away_by == 0, 0, away_by + 1))
     act_row = jnp.where(

time: 262 us -> 236 us (0.901)
  waiting for transfers between devices: 124 us -> 90 us
  starting transfers between devices: 55.2 us -> 61.1 us
    ppermute x11, waiting for transfers between devices: 43.3 us -> 14.4 us  [cross(): return lax.ppermute(value, VDP, pairs)]
    ppermute x13, waiting for transfers between devices: 69.3 us -> 52.1 us  [shift(): lax.ppermute(value, axis, [(i, (i + by) % size) for i in range(size)])]
    all_to_all x1, waiting for transfers between devices: 0.01 us -> 13 us  [local(): lax.all_to_all(split_columns(embed_grad, nx), X, split_axis=0, concat_axi...]
    ppermute x11, starting transfers between devices: 19.6 us -> 24 us  [cross(): return lax.ppermute(value, VDP, pairs)]
    unnamed x60 -> x59, local copies, waits for them, and re-layouts: 12.9 us -> 16.7 us
  transfers between devices with their start and end apart: 28 -> 28, of which waited for: 13 -> 10; matrix products, arithmetic and copies ran while one was open for 12% -> 14% of each run, Pallas kernels for 9% -> 10%
where the time goes in v6:
time: 236 us; the launch traced here: 235 us
  waiting for transfers between devices  90 us (38%)
  starting transfers between devices  61.1 us (26%)
  Pallas kernels  40.2 us (17%)
  local copies, waits for them, and re-layouts  29.8 us (13%)
  other arithmetic  12.4 us (5%)
    ppermute x13, waiting for transfers between devices, shift(): lax.ppermute(value, axis, [(i, (i + by) % size) for i in range(size)])  52.1 us
    ppermute x11, starting transfers between devices, cross(): return lax.ppermute(value, VDP, pairs)  24 us
    unnamed x59, local copies, waits for them, and re-layouts  16.7 us
    ppermute x13, starting transfers between devices, shift(): lax.ppermute(value, axis, [(i, (i + by) % size) for i in range(size)])  14.5 us
    ppermute x11, waiting for transfers between devices, cross(): return lax.ppermute(value, VDP, pairs)  14.4 us
    pallas_call x1, Pallas kernels, project(): pl.pallas_call(body, grid=(k // tile,), in_specs=[pl.BlockSpec((n, tile),...  13.8 us
    pallas_call x1, Pallas kernels, project_back(): pl.pallas_call(body, in_specs=[pl.BlockSpec(memory_space=pltpu.SMEM), vme...  13.5 us
    all_to_all x1, waiting for transfers between devices, local(): lax.all_to_all(split_columns(embed_grad, nx), X, split_axis=0, concat_axi...  13 us
  transfers between devices with their start and end apart: 28, of which 10 were waited for; matrix products, arithmetic and copies ran while one was open for 14% of the time, Pallas kernels for 10%

profile of v6, /device:TPU:6, one launch (start us, length us, event | category | flops | bytes accessed | tf_op | source)
XLA Modules:
  0.0 234.6 jit_solution(6890424041560340572)
XLA Ops:
  2.6 2.2 collective-permute-start.1
  9.9 4.9 %all-to-all-start = ((bf16[4,128,2048]{2,1,0:T(8,128)(2,1)}), bf16[4,128,2048]{2,1,0:T(8,128)(2,1)S(1)}, u32[]{:S(2)}, u32[]{:S(2)}) async-start(bf16[4,128,2048]{2,1,0:T(8,128)(2,1)} %copy-done), calls=%async_computation | async-start | bytes 4194304 | tf_op jit(solution)/shard_map/all_to_all | solution.py:324
  16.4 3.9 %collective-permute-done.1 = bf16[160,2048]{1,0:T(8,128)(2,1)} collective-permute-done((bf16[160,2048]{1,0:T(8,128)(2,1)}, bf16[160,2048]{1,0:T(8,128)(2,1)}, u32[]{:S(2)}, u32[]{:S(2)}) %collective-permute-start.1) | collective-permute-done | bytes 655392 | tf_op jit(solution)/shard_map/ppermute | solution.py:353
  24.5 13.0 %all-to-all-done.table_ref = bf16[4,128,2048]{2,1,0:T(8,128)(2,1)S(1)} async-done(((bf16[4,128,2048]{2,1,0:T(8,128)(2,1)}), bf16[4,128,2048]{2,1,0:T(8,128)(2,1)S(1)}, u32[]{:S(2)}, u32[]{:S(2)}) %all-to-all-start) | async-done | bytes 2097184 | tf_op jit(solution)/shard_map/all_to_all | solution.py:324
  37.6 2.1 collective-permute-start.8
  44.1 2.3 collective-permute-start.6
  51.6 6.4 %collective-permute-start.7 = (bf16[640,1024]{1,0:T(8,128)(2,1)}, bf16[640,1024]{1,0:T(8,128)(2,1)S(1)}, u32[]{:S(2)}, u32[]{:S(2)}) collective-permute-start(bf16[640,1024]{1,0:T(8,128)(2,1)} %collective-permute-done.3.refs_7_), channel_id=1, source_target_pairs={{0,24},{4,100},{8,0},{12,108},{16,8},{20,116},{24,16},{28,124},{32... | collective-permute-start | bytes 3932168 | tf_op jit(solution)/shard_map/ppermute | solution.py:353
  61.0 3.3 %collective-permute-start.10 = (bf16[32,5120]{1,0:T(8,128)(2,1)S(1)}, bf16[32,5120]{1,0:T(8,128)(2,1)S(1)}, u32[]{:S(2)}, u32[]{:S(2)}) collective-permute-start(bf16[32,5120]{1,0:T(8,128)(2,1)S(1)} %slice.58), channel_id=1, source_target_pairs={{0,1},{1,2},{2,3},{3,0},{4,5},{5,6},{6,7},{7,4},{8,9},{9,10},{10,1... | collective-permute-start | bytes 983048 | tf_op jit(solution)/shard_map/ppermute | solution.py:20
  65.1 3.7 %collective-permute-done.10 = bf16[32,5120]{1,0:T(8,128)(2,1)S(1)} collective-permute-done((bf16[32,5120]{1,0:T(8,128)(2,1)S(1)}, bf16[32,5120]{1,0:T(8,128)(2,1)S(1)}, u32[]{:S(2)}, u32[]{:S(2)}) %collective-permute-start.10) | collective-permute-done | bytes 327712 | tf_op jit(solution)/shard_map/ppermute | solution.py:20
  69.6 8.0 %collective-permute-done.11 = bf16[32,5120]{1,0:T(8,128)(2,1)S(1)} collective-permute-done((bf16[32,5120]{1,0:T(8,128)(2,1)S(1)}, bf16[32,5120]{1,0:T(8,128)(2,1)S(1)}, u32[]{:S(2)}, u32[]{:S(2)}) %collective-permute-start.11) | collective-permute-done | bytes 327712 | tf_op jit(solution)/shard_map/ppermute | solution.py:20
  85.3 7.5 %all-to-all-start.1 = ((bf16[32,16,1024]{2,1,0:T(8,128)(2,1)}), bf16[32,16,1024]{2,1,0:T(8,128)(2,1)S(1)}, u32[]{:S(2)}, u32[]{:S(2)}) async-start(bf16[32,16,1024]{2,1,0:T(8,128)(2,1)} %bitcast.5), calls=%async_computation.1 | async-start | bytes 2097152 | tf_op jit(solution)/shard_map/all_to_all | solution.py:406
  93.3 2.1 slice.60
  105.3 7.0 %pick_rows.1.act_ref = bf16[512,5120]{1,0:T(8,128)(2,1)} custom-call(s32[512,1]{1,0:T(8,128)S(1)} %get-tuple-element.56.index_ref, bf16[256,5120]{1,0:T(8,128)(2,1)} %constant_dynamic-update-slice_fusion.4.own_ref, bf16[256,5120]{1,0:T(8,128)(2,1)} %collective-permute-done.12.other_ref), custom_call_target="tpu_custom_call" | custom-call | flops 2684354560 | bytes 10485760 | tf_op jit(solution)/shard_map/pick_rows/pallas_call | solution.py:173
  112.3 9.9 %collective-permute-done.13.refs_5_ = bf16[320,1024]{1,0:T(8,128)(2,1)S(1)} collective-permute-done((bf16[320,1024]{1,0:T(8,128)(2,1)}, bf16[320,1024]{1,0:T(8,128)(2,1)S(1)}, u32[]{:S(2)}, u32[]{:S(2)}) %collective-permute-start.13) | collective-permute-done | bytes 655392 | tf_op jit(solution)/shard_map/ppermute | solution.py:353
  124.1 13.5 %project_back.1 = (bf16[256,5120]{1,0:T(8,128)(2,1)}, bf16[256,5120]{1,0:T(8,128)(2,1)}, bf16[5120,1024]{1,0:T(8,128)(2,1)}) custom-call(s32[32]{0:T(128)S(1)} %stack.137.refs_0_, bf16[512,1024]{1,0:T(8,128)(2,1)S(1)} %unpick_rows.1.refs_1_, bf16[640,1024]{1,0:T(8,128)(2,1)S(1)} %get-tuple-element.21.refs_2_, bf16[640,1024]{1,0:T(8,128)(2,1)} %copy-done.12, ...), custom_call_target="tpu_custom_call" | custom-call | flops 5368709120 | bytes 31457280 | tf_op jit(solution)/shard_map/project_back/pallas_call | solution.py:247
  137.8 13.8 %project.1 = bf16[512,1024]{1,0:T(8,128)(2,1)} custom-call(bf16[512,5120]{1,0:T(8,128)(2,1)} %pick_rows.1.act_ref, f32[1,1024]{1,0:T(1,128)S(1)} %bitcast.72, bf16[5120,1024]{1,0:T(8,128)(2,1)} %get-tuple-element.33.weight_ref), custom_call_target="tpu_custom_call" | custom-call | flops 5368709120 | bytes 10485760 | tf_op jit(solution)/shard_map/project/pallas_call | solution.py:289
  151.6 5.0 %all-to-all-start.2 = ((bf16[32,16,1024]{2,1,0:T(8,128)(2,1)}), bf16[32,16,1024]{2,1,0:T(8,128)(2,1)S(1)}, u32[]{:S(2)}, u32[]{:S(2)}) async-start(bf16[32,16,1024]{2,1,0:T(8,128)(2,1)} %bitcast.52), calls=%async_computation.2 | async-start | bytes 2097152 | tf_op jit(solution)/shard_map/all_to_all | solution.py:420
  156.5 3.7 %add_bitcast_fusion.1 = (f32[64,5120]{1,0:T(8,128)}, f32[64,5120]{1,0:T(8,128)S(1)}, bf16[64,5120]{1,0:T(8,128)(2,1)S(1)}) fusion(bf16[4,64,5120]{2,1,0:T(8,128)(2,1)} %bitcast.55, s32[]{:T(128)S(6)} %select_n.882, bf16[4,64,5120]{2,1,0:T(8,128)(2,1)} %bitcast.73, s32[]{:T(128)S(6)} %select_n.886, s32[]{:T(128)S(6)} %select_n.884), kind=kLoop, calls=%fused_computation.17 | loop fusion | flops 3276800 | bytes 7208972 | tf_op jit(solution)/shard_map/add | solution.py:428
  162.8 10.5 %all-to-all-done.2 = bf16[32,16,1024]{2,1,0:T(8,128)(2,1)S(1)} async-done(((bf16[32,16,1024]{2,1,0:T(8,128)(2,1)}), bf16[32,16,1024]{2,1,0:T(8,128)(2,1)S(1)}, u32[]{:S(2)}, u32[]{:S(2)}) %all-to-all-start.2) | async-done | bytes 1048608 | tf_op jit(solution)/shard_map/all_to_all | solution.py:420
  175.8 5.3 %all-to-all-start.3 = ((bf16[4,128,2048]{2,1,0:T(8,128)(2,1)}), bf16[4,128,2048]{2,1,0:T(8,128)(2,1)S(1)}, u32[]{:S(2)}, u32[]{:S(2)}) async-start(bf16[4,128,2048]{2,1,0:T(8,128)(2,1)} %copy-done.1), calls=%async_computation.3 | async-start | bytes 4194304 | tf_op jit(solution)/shard_map/all_to_all | solution.py:451
  183.8 2.8 %collective-permute-start.21 = (bf16[64,2560]{1,0:T(8,128)(2,1)S(1)}, bf16[64,2560]{1,0:T(8,128)(2,1)S(1)}, u32[]{:S(2)}, u32[]{:S(2)}) collective-permute-start(bf16[64,2560]{1,0:T(8,128)(2,1)S(1)} %slice.87), channel_id=1, source_target_pairs={{0,1},{1,2},{2,3},{3,0},{4,5},{5,6},{6,7},{7,4},{8,9},{9,10},{10,1... | collective-permute-start | bytes 983048 | tf_op jit(solution)/shard_map/ppermute | solution.py:20
  188.8 30.3 %collective-permute-done.22 = bf16[64,2560]{1,0:T(8,128)(2,1)S(1)} collective-permute-done((bf16[64,2560]{1,0:T(8,128)(2,1)}, bf16[64,2560]{1,0:T(8,128)(2,1)S(1)}, u32[]{:S(2)}, u32[]{:S(2)}) %collective-permute-start.22) | collective-permute-done | bytes 327712 | tf_op jit(solution)/shard_map/ppermute | solution.py:20
  221.1 8.8 %collective-permute-done.23 = bf16[64,2560]{1,0:T(8,128)(2,1)S(1)} collective-permute-done((bf16[64,2560]{1,0:T(8,128)(2,1)S(1)}, bf16[64,2560]{1,0:T(8,128)(2,1)S(1)}, u32[]{:S(2)}, u32[]{:S(2)}) %collective-permute-start.23) | collective-permute-done | bytes 327712 | tf_op jit(solution)/shard_map/ppermute | solution.py:20
  229.9 2.9 %fusion.8 = bf16[64,5120]{1,0:T(8,128)(2,1)} fusion(bf16[64,5120]{1,0:T(8,128)(2,1)S(1)} %copy-done.8, f32[64,2560]{1,0:T(8,128)S(1)} %convert_add_fusion, f32[64,2560]{1,0:T(8,128)S(1)} %convert_add_fusion.1, bf16[4,64,5120]{2,1,0:T(8,128)(2,1)} %bitcast.55, s32[]{:T(128)S(6)} %select_n.880, bf16[4,64,5120]{2,1,0:T(8,128)(2,1)} %bitcast.74), kind=kLoop, calls=%fused_computation.13 | loop fusion | flops 5242880 | bytes 3932164 | tf_op jit(solution)/shard_map/convert_element_type | solution.py:448
  (146 shorter events, 61.1 us)
Async XLA Ops:
  0.6 14.6 %collective-permute-start = (bf16[160,2048]{1,0:T(8,128)(2,1)}, bf16[160,2048]{1,0:T(8,128)(2,1)}, u32[]{:S(2)}, u32[]{:S(2)}) collective-permute-start(bf16[160,2048]{1,0:T(8,128)(2,1)} %param.8), channel_id=1, source_target_pairs={{0,8},{4,36},{8,16},{12,44},{16,24},{20,52},{24,0},{28,60},{32,40}... | collective-permute-start | bytes 1966088 | tf_op jit(solution)/shard_map/ppermute | solution.py:353
  2.6 17.7 %collective-permute-start.1 = (bf16[160,2048]{1,0:T(8,128)(2,1)}, bf16[160,2048]{1,0:T(8,128)(2,1)}, u32[]{:S(2)}, u32[]{:S(2)}) collective-permute-start(bf16[160,2048]{1,0:T(8,128)(2,1)} %param.8), channel_id=1, source_target_pairs={{0,24},{4,100},{8,0},{12,108},{16,8},{20,116},{24,16},{28,124},{32... | collective-permute-start | bytes 1966088 | tf_op jit(solution)/shard_map/ppermute | solution.py:353
  4.8 17.2 %collective-permute-start.2 = (bf16[160,2048]{1,0:T(8,128)(2,1)}, bf16[160,2048]{1,0:T(8,128)(2,1)S(1)}, u32[]{:S(2)}, u32[]{:S(2)}) collective-permute-start(bf16[160,2048]{1,0:T(8,128)(2,1)} %param.8), channel_id=1, source_target_pairs={{0,16},{4,68},{8,24},{12,76},{16,0},{20,84},{24,8},{28,92},{32,48}... | collective-permute-start | bytes 1966088 | tf_op jit(solution)/shard_map/ppermute | solution.py:353
  9.9 27.7 %all-to-all-start = ((bf16[4,128,2048]{2,1,0:T(8,128)(2,1)}), bf16[4,128,2048]{2,1,0:T(8,128)(2,1)S(1)}, u32[]{:S(2)}, u32[]{:S(2)}) async-start(bf16[4,128,2048]{2,1,0:T(8,128)(2,1)} %copy-done), calls=%async_computation | async-start | bytes 4194304 | tf_op jit(solution)/shard_map/all_to_all | solution.py:324
  23.4 14.2 %collective-permute-start.3 = (bf16[640,1024]{1,0:T(8,128)(2,1)}, bf16[640,1024]{1,0:T(8,128)(2,1)}, u32[]{:S(2)}, u32[]{:S(2)}) collective-permute-start(bf16[640,1024]{1,0:T(8,128)(2,1)} %get-tuple-element.51), channel_id=1, source_target_pairs={{0,4},{4,0},{1,5},{5,1},{2,6},{6,2},{3,7},{7,3},{8,12},{12,8},{9,1... | collective-permute-start | bytes 3932168 | tf_op jit(solution)/shard_map/ppermute | solution.py:20
  41.1 19.9 %collective-permute-start.9 = (bf16[64,5120]{1,0:T(8,128)(2,1)}, bf16[64,5120]{1,0:T(8,128)(2,1)S(1)}, u32[]{:S(2)}, u32[]{:S(2)}) collective-permute-start(bf16[64,5120]{1,0:T(8,128)(2,1)} %fusion.3), channel_id=1, source_target_pairs={{0,3},{1,0},{2,1},{3,2},{4,7},{5,4},{6,5},{7,6},{8,11},{9,8},{10,9... | collective-permute-start | bytes 1966088 | tf_op jit(solution)/shard_map/ppermute | solution.py:20
  43.1 35.2 %collective-permute-start.4 = (bf16[640,1024]{1,0:T(8,128)(2,1)S(1)}, bf16[640,1024]{1,0:T(8,128)(2,1)S(1)}, u32[]{:S(2)}, u32[]{:S(2)}) collective-permute-start(bf16[640,1024]{1,0:T(8,128)(2,1)S(1)} %get-tuple-element.21.refs_2_), channel_id=1, source_target_pairs={{0,32},{4,12},{8,40},{12,20},{16,48},{20,28},{24,56},{28,4},{32,64... | collective-permute-start | bytes 3932168 | tf_op jit(solution)/shard_map/ppermute | solution.py:353
  44.1 34.3 %collective-permute-start.6 = (bf16[640,1024]{1,0:T(8,128)(2,1)S(1)}, bf16[640,1024]{1,0:T(8,128)(2,1)S(1)}, u32[]{:S(2)}, u32[]{:S(2)}) collective-permute-start(bf16[640,1024]{1,0:T(8,128)(2,1)S(1)} %get-tuple-element.21.refs_2_), channel_id=1, source_target_pairs={{0,96},{4,28},{8,104},{12,4},{16,112},{20,12},{24,120},{28,20},{32... | collective-permute-start | bytes 3932168 | tf_op jit(solution)/shard_map/ppermute | solution.py:353
  46.4 32.0 %collective-permute-start.5 = (bf16[640,1024]{1,0:T(8,128)(2,1)}, bf16[640,1024]{1,0:T(8,128)(2,1)S(1)}, u32[]{:S(2)}, u32[]{:S(2)}) collective-permute-start(bf16[640,1024]{1,0:T(8,128)(2,1)} %collective-permute-done.3.refs_7_), channel_id=1, source_target_pairs={{0,8},{4,36},{8,16},{12,44},{16,24},{20,52},{24,0},{28,60},{32,40}... | collective-permute-start | bytes 3932168 | tf_op jit(solution)/shard_map/ppermute | solution.py:353
  51.6 27.8 %collective-permute-start.7 = (bf16[640,1024]{1,0:T(8,128)(2,1)}, bf16[640,1024]{1,0:T(8,128)(2,1)S(1)}, u32[]{:S(2)}, u32[]{:S(2)}) collective-permute-start(bf16[640,1024]{1,0:T(8,128)(2,1)} %collective-permute-done.3.refs_7_), channel_id=1, source_target_pairs={{0,24},{4,100},{8,0},{12,108},{16,8},{20,116},{24,16},{28,124},{32... | collective-permute-start | bytes 3932168 | tf_op jit(solution)/shard_map/ppermute | solution.py:353
  81.7 23.7 %collective-permute-start.12 = (bf16[256,5120]{1,0:T(8,128)(2,1)}, bf16[256,5120]{1,0:T(8,128)(2,1)}, u32[]{:S(2)}, u32[]{:S(2)}) collective-permute-start(bf16[256,5120]{1,0:T(8,128)(2,1)} %constant_dynamic-update-slice_fusion.4.own_ref), channel_id=1, source_target_pairs={{0,4},{4,0},{1,5},{5,1},{2,6},{6,2},{3,7},{7,3},{8,12},{12,8},{9,1... | collective-permute-start | bytes 7864328 | tf_op jit(solution)/shard_map/ppermute | solution.py:20
  85.3 27.0 %all-to-all-start.1 = ((bf16[32,16,1024]{2,1,0:T(8,128)(2,1)}), bf16[32,16,1024]{2,1,0:T(8,128)(2,1)S(1)}, u32[]{:S(2)}, u32[]{:S(2)}) async-start(bf16[32,16,1024]{2,1,0:T(8,128)(2,1)} %bitcast.5), calls=%async_computation.1 | async-start | bytes 2097152 | tf_op jit(solution)/shard_map/all_to_all | solution.py:406
  95.4 26.8 %collective-permute-start.13 = (bf16[320,1024]{1,0:T(8,128)(2,1)}, bf16[320,1024]{1,0:T(8,128)(2,1)S(1)}, u32[]{:S(2)}, u32[]{:S(2)}) collective-permute-start(bf16[320,1024]{1,0:T(8,128)(2,1)} %slice.60), channel_id=1, source_target_pairs={{0,32},{4,12},{8,40},{12,20},{16,48},{20,28},{24,56},{28,4},{32,64... | collective-permute-start | bytes 1966088 | tf_op jit(solution)/shard_map/ppermute | solution.py:353
  98.0 25.0 %collective-permute-start.14 = (bf16[320,1024]{1,0:T(8,128)(2,1)}, bf16[320,1024]{1,0:T(8,128)(2,1)}, u32[]{:S(2)}, u32[]{:S(2)}) collective-permute-start(bf16[320,1024]{1,0:T(8,128)(2,1)} %slice.61), channel_id=1, source_target_pairs={{0,96},{4,28},{8,104},{12,4},{16,112},{20,12},{24,120},{28,20},{32... | collective-permute-start | bytes 1966088 | tf_op jit(solution)/shard_map/ppermute | solution.py:353
  100.4 22.7 %collective-permute-start.15 = (bf16[320,1024]{1,0:T(8,128)(2,1)}, bf16[320,1024]{1,0:T(8,128)(2,1)}, u32[]{:S(2)}, u32[]{:S(2)}) collective-permute-start(bf16[320,1024]{1,0:T(8,128)(2,1)} %slice.62), channel_id=1, source_target_pairs={{0,8},{4,36},{8,16},{12,44},{16,24},{20,52},{24,0},{28,60},{32,40}... | collective-permute-start | bytes 1966088 | tf_op jit(solution)/shard_map/ppermute | solution.py:353
  103.1 19.9 %collective-permute-start.16 = (bf16[320,1024]{1,0:T(8,128)(2,1)}, bf16[320,1024]{1,0:T(8,128)(2,1)}, u32[]{:S(2)}, u32[]{:S(2)}) collective-permute-start(bf16[320,1024]{1,0:T(8,128)(2,1)} %slice.63), channel_id=1, source_target_pairs={{0,24},{4,100},{8,0},{12,108},{16,8},{20,116},{24,16},{28,124},{32... | collective-permute-start | bytes 1966088 | tf_op jit(solution)/shard_map/ppermute | solution.py:353
  137.6 18.9 %collective-permute-start.17 = (bf16[256,5120]{1,0:T(8,128)(2,1)}, bf16[256,5120]{1,0:T(8,128)(2,1)}, u32[]{:S(2)}, u32[]{:S(2)}) collective-permute-start(bf16[256,5120]{1,0:T(8,128)(2,1)} %get-tuple-element.35), channel_id=1, source_target_pairs={{0,4},{4,0},{1,5},{5,1},{2,6},{6,2},{3,7},{7,3},{8,12},{12,8},{9,1... | collective-permute-start | bytes 7864328 | tf_op jit(solution)/shard_map/ppermute | solution.py:20
  151.6 21.8 %all-to-all-start.2 = ((bf16[32,16,1024]{2,1,0:T(8,128)(2,1)}), bf16[32,16,1024]{2,1,0:T(8,128)(2,1)S(1)}, u32[]{:S(2)}, u32[]{:S(2)}) async-start(bf16[32,16,1024]{2,1,0:T(8,128)(2,1)} %bitcast.52), calls=%async_computation.2 | async-start | bytes 2097152 | tf_op jit(solution)/shard_map/all_to_all | solution.py:420
  161.1 25.4 %collective-permute-start.18 = (bf16[64,2560]{1,0:T(8,128)(2,1)}, bf16[64,2560]{1,0:T(8,128)(2,1)}, u32[]{:S(2)}, u32[]{:S(2)}) collective-permute-start(bf16[64,2560]{1,0:T(8,128)(2,1)} %get-tuple-element.53), channel_id=1, source_target_pairs={{0,1},{1,2},{2,3},{3,0},{4,5},{5,6},{6,7},{7,4},{8,9},{9,10},{10,1... | collective-permute-start | bytes 983048 | tf_op jit(solution)/shard_map/ppermute | solution.py:20
  175.8 57.0 %all-to-all-start.3 = ((bf16[4,128,2048]{2,1,0:T(8,128)(2,1)}), bf16[4,128,2048]{2,1,0:T(8,128)(2,1)S(1)}, u32[]{:S(2)}, u32[]{:S(2)}) async-start(bf16[4,128,2048]{2,1,0:T(8,128)(2,1)} %copy-done.1), calls=%async_computation.3 | async-start | bytes 4194304 | tf_op jit(solution)/shard_map/all_to_all | solution.py:451
  181.2 39.8 %collective-permute-start.20 = (bf16[64,2560]{1,0:T(8,128)(2,1)S(1)}, bf16[64,2560]{1,0:T(8,128)(2,1)S(1)}, u32[]{:S(2)}, u32[]{:S(2)}) collective-permute-start(bf16[64,2560]{1,0:T(8,128)(2,1)S(1)} %slice.88), channel_id=1, source_target_pairs={{0,3},{1,0},{2,1},{3,2},{4,7},{5,4},{6,5},{7,6},{8,11},{9,8},{10,9... | collective-permute-start | bytes 983048 | tf_op jit(solution)/shard_map/ppermute | solution.py:20
  182.1 37.0 %collective-permute-start.22 = (bf16[64,2560]{1,0:T(8,128)(2,1)}, bf16[64,2560]{1,0:T(8,128)(2,1)S(1)}, u32[]{:S(2)}, u32[]{:S(2)}) collective-permute-start(bf16[64,2560]{1,0:T(8,128)(2,1)} %get-tuple-element.54), channel_id=1, source_target_pairs={{0,3},{1,0},{2,1},{3,2},{4,7},{5,4},{6,5},{7,6},{8,11},{9,8},{10,9... | collective-permute-start | bytes 983048 | tf_op jit(solution)/shard_map/ppermute | solution.py:20
  183.8 37.3 %collective-permute-start.21 = (bf16[64,2560]{1,0:T(8,128)(2,1)S(1)}, bf16[64,2560]{1,0:T(8,128)(2,1)S(1)}, u32[]{:S(2)}, u32[]{:S(2)}) collective-permute-start(bf16[64,2560]{1,0:T(8,128)(2,1)S(1)} %slice.87), channel_id=1, source_target_pairs={{0,1},{1,2},{2,3},{3,0},{4,5},{5,6},{6,7},{7,4},{8,9},{9,10},{10,1... | collective-permute-start | bytes 983048 | tf_op jit(solution)/shard_map/ppermute | solution.py:20
  187.6 33.4 %collective-permute-start.19 = (bf16[64,2560]{1,0:T(8,128)(2,1)S(1)}, bf16[64,2560]{1,0:T(8,128)(2,1)S(1)}, u32[]{:S(2)}, u32[]{:S(2)}) collective-permute-start(bf16[64,2560]{1,0:T(8,128)(2,1)S(1)} %fusion.11), channel_id=1, source_target_pairs={{0,1},{1,2},{2,3},{3,0},{4,5},{5,6},{6,7},{7,4},{8,9},{9,10},{10,1... | collective-permute-start | bytes 983048 | tf_op jit(solution)/shard_map/ppermute | solution.py:20
  (30 other events, 151.0 us)
